TPU v7x, 32 devices: a whole 2x2x4 slice. The times are simulated.
32 devices in a mesh: dp: 8 (over z, x), tensor: 4 (over y, core).
Axes of the slice: x: 2, y: 2, z: 4, core: 2. Of those that a mesh axis runs over, the one named last changes fastest.
Arguments:
- pre_act: bfloat16 [1024, 12288], P('dp', 'tensor'), may hold values from -6 to 6
- out_grad: bfloat16 [1024, 3072], P(('dp', 'tensor')), may hold values from -8 to 8
- w_up: bfloat16 [3072, 12288], P(None, 'tensor'), may hold values from -0.0546875 to 0.0546875
- w_down: bfloat16 [12288, 3072], P('tensor'), may hold values from -0.109375 to 0.109375
Outputs:
- in_grad: bfloat16 [1024, 3072], P(('dp', 'tensor'))
- down_grad_t: float32 [3072, 12288], P('dp', 'tensor')
All inputs are finite; a program needn't handle non-finite values.
Results may differ from a plain program's by a relative error of at most 0.0049.
Values may be sent and summed in bfloat16 or wider, within the bound.
No kernel may reach another device: no remote copies, remote signals or barrier semaphores. Data moves between devices by JAX's collectives and lax.ppermute only.
A program may use at most 128 MiB of HBM per device.

v0:
```python
import math

import jax
import jax.numpy as jnp
from jax import lax
from jax.sharding import PartitionSpec as P


def gelu_parts(pre_float):
    normal_cdf = 0.5 * (1.0 + jax.scipy.special.erf(pre_float / math.sqrt(2.0)))
    density = jnp.exp(-0.5 * pre_float * pre_float) / math.sqrt(2.0 * math.pi)
    return (pre_float * normal_cdf, normal_cdf + pre_float * density)


def gather_columns(gathered):
    return lax.all_to_all(gathered, "dp", split_axis=1, concat_axis=0, tiled=True)


def per_device(pre_act, out_grad, w_up, w_down):
    gelu_value, gelu_slope = gelu_parts(pre_act.astype(jnp.float32))
    act = gelu_value.astype(jnp.bfloat16)
    gathered = lax.all_gather(out_grad, "tensor", axis=0, tiled=True)
    hidden_grad = lax.dot_general(
        gathered, w_down, (((1,), (1,)), ((), ())), preferred_element_type=jnp.float32
    )
    pre_grad = (hidden_grad * gelu_slope).astype(jnp.bfloat16)
    data_count = lax.axis_size("dp")
    all_tokens = gathered.shape[0] * data_count
    my_columns = gather_columns(gathered)
    summed = lax.dot_general(
        my_columns,
        lax.all_gather(act, "dp", axis=0, tiled=True),
        (((0,), (0,)), ((), ())),
        preferred_element_type=jnp.float32,
    )
    down_grad_t = summed / math.sqrt(all_tokens)
    in_grad = lax.psum_scatter(
        lax.dot_general(
            pre_grad, w_up, (((1,), (1,)), ((), ())), preferred_element_type=jnp.float32
        ),
        "tensor",
        scatter_dimension=0,
        tiled=True,
    ).astype(jnp.bfloat16)
    return (in_grad, down_grad_t)


def solution(mesh):
    placed = (P("dp", "tensor"), P(("dp", "tensor"), None), P(None, "tensor"), P("tensor", None))
    return jax.shard_map(
        per_device,
        mesh=mesh,
        in_specs=placed,
        out_specs=(P(("dp", "tensor"), None), P("dp", "tensor")),
        check_vma=False,
    )
```

profile of v0, /device:TPU:0, one launch (start us, length us, event | category | flops | bytes accessed | tf_op | source)
XLA Modules:
  0.0 174.6 jit_solution(10731213487806221009)
XLA Ops:
  8.0 0.0 reduce-scatter.2.cloned.1.call-start
  8.0 10.3 %all_gather.6 = bf16[128,3072]{1,0:T(8,128)(2,1)S(1)} all-gather(bf16[32,3072]{1,0:T(8,128)(2,1)} %param.5), channel_id=1, replica_groups=mesh['dp'=8,'tensor'=4] {'tensor'}, dimensions={0}, use_global_device_ids=true | all-gather | bytes 983040 | tf_op jit(solution)/shard_map/all_gather | solution.py:22
  18.3 19.1 %fusion.8 = f32[128,3072]{1,0:T(8,128)} fusion(bf16[3072,3072]{1,0:T(8,128)(2,1)} %param.6, bf16[128,3072]{1,0:T(8,128)(2,1)S(1)} %all_gather.6, bf16[3072,3072]{1,0:T(8,128)(2,1)} %param.7, bf16[128,3072]{1,0:T(8,128)(2,1)} %param.4), kind=kOutput, calls=%fused_computation.15 | convolution fusion | flops 4836163584 | bytes 40894464 | tf_op jit(solution)/shard_map/dot_general | solution.py:38
  37.5 0.0 copy-start
  37.5 0.0 reduce-scatter.2.cloned.1.call-update
  37.5 0.0 all-gather.2.cloned.1.call-start
  37.6 1.1 copy-done
  38.6 1.2 fusion.7
  39.8 0.0 all-gather.2.cloned.1.call-update
  39.8 0.4 copy.11
  40.2 43.6 %all_to_all.19 = bf16[128,8,384]{0,2,1:T(8,128)(2,1)S(1)} all-to-all(bf16[128,8,384]{0,2,1:T(8,128)(2,1)S(1)} %bitcast.10), channel_id=1, replica_groups=mesh['dp'=8,'tensor'=4] {'dp'}, dimensions={1} | all-to-all | bytes 1572864 | tf_op jit(solution)/shard_map/all_to_all | solution.py:16
  83.8 0.4 copy.12
  84.2 0.0 reduce-scatter.2.cloned.1.call-done
  84.2 1.7 convert_element_type.14
  85.9 66.7 %all-gather.2.cloned.1.call-done = bf16[1024,3072]{1,0:T(8,128)(2,1)} async-done(((bf16[128,3072]{1,0:T(8,128)(2,1)}), bf16[1024,3072]{1,0:T(8,128)(2,1)}) %all-gather.2.cloned.1.call-update) | async-done | bytes 6291472 | tf_op jit(solution)/shard_map/all_gather | solution.py:32
  152.7 8.5 %multiply_bitcast_fusion = f32[384,3072]{0,1:T(8,128)} fusion(bf16[1024,3072]{1,0:T(8,128)(2,1)} %all-gather.2.cloned.1.call-done, bf16[1024,384]{1,0:T(8,128)(2,1)S(1)} %bitcast.12), kind=kOutput, calls=%fused_computation | convolution fusion | flops 2417098752 | bytes 11796480 | tf_op jit(solution)/shard_map/dot_general | solution.py:30
  161.2 6.0 %copy.13 = f32[384,3072]{1,0:T(8,128)} copy(f32[384,3072]{0,1:T(8,128)} %multiply_bitcast_fusion) | data formatting | bytes 9437184
Async XLA Ops:
  8.0 76.2 %reduce-scatter.2.cloned.1.call-start = ((), (), s32[]{:S(2)}) async-start(), calls=%async_computation.2 | async-start | bytes 1966080 | tf_op jit(solution)/shard_map/reduce_scatter | solution.py:37
  37.5 1.1 copy-start
  37.5 115.2 %all-gather.2.cloned.1.call-start = ((), (), s32[]{:S(2)}) async-start(), calls=%async_computation.3 | async-start | bytes 7077888 | tf_op jit(solution)/shard_map/all_gather | solution.py:32
Sparse Core Ops, SparseCore 0:
  37.6 29.0 reduce-scatter.1
Sparse Core Ops, SparseCore 1:
  40.4 112.2 all-gather.1
where the time goes:
time: 175 us
  waiting for transfers between devices  66.8 us (38%)
  blocking collectives  53.9 us (31%)
  matrix products  27.6 us (16%)
  between operations  15.5 us (9%)
  local copies, waits for them, and re-layouts  7.83 us (4%)
  other arithmetic  2.9 us (2%)
    all_gather x1, waiting for transfers between devices, per_device(): lax.all_gather(act, 'dp', axis=0, tiled=True)  66.7 us
    all_to_all x1, blocking collectives, gather_columns(): lax.all_to_all(gathered, 'dp', split_axis=1, concat_axis=0, tiled=True)  43.6 us
    dot_general x1, matrix products, per_device(): lax.dot_general(pre_grad, w_up, (((1,), (1,)), ((), ())), preferred_eleme...  19.1 us
    all_gather x1, blocking collectives, per_device(): gathered = lax.all_gather(out_grad, 'tensor', axis=0, tiled=True)  10.3 us
    dot_general x1, matrix products, per_device(): lax.dot_general(my_columns, lax.all_gather(act, 'dp', axis=0, tiled=True)...  8.49 us
    unnamed x3, local copies, waits for them, and re-layouts  7.1 us
  transfers between devices with their start and end apart: 2, of which 1 were waited for; matrix products, arithmetic and copies ran while one was open for 2% of the time, Pallas kernels for 0%

commit v1 on v0

v1 whole, which is shorter than its diff:
```python
import math

import jax
import jax.numpy as jnp
from jax import lax
from jax.sharding import PartitionSpec as P

BF16 = jnp.bfloat16
F32 = jnp.float32


def gelu_value_of(pre):
    pre_float = pre.astype(F32)
    normal_cdf = 0.5 * (1.0 + jax.scipy.special.erf(pre_float / math.sqrt(2.0)))
    return (pre_float * normal_cdf).astype(BF16)


def gelu_slope_of(pre):
    pre_float = pre.astype(F32)
    normal_cdf = 0.5 * (1.0 + jax.scipy.special.erf(pre_float / math.sqrt(2.0)))
    density = jnp.exp(-0.5 * pre_float * pre_float) / math.sqrt(2.0 * math.pi)
    return normal_cdf + pre_float * density


def xor_permute(value, axis, mask):
    count = lax.axis_size(axis)
    return lax.ppermute(value, axis, [(i, i ^ mask) for i in range(count)])


def either(bit, low, high):
    return jnp.where(bit == 0, low, high)


def gathered_plan(pre_act, out_grad, w_up, w_down):
    act = gelu_value_of(pre_act)
    gathered = lax.all_gather(out_grad, "tensor", axis=0, tiled=True)
    hidden_grad = lax.dot_general(gathered, w_down, (((1,), (1,)), ((), ())), preferred_element_type=F32)
    pre_grad = (hidden_grad * gelu_slope_of(pre_act)).astype(BF16)
    all_tokens = gathered.shape[0] * lax.axis_size("dp")
    my_columns = lax.all_to_all(gathered, "dp", split_axis=1, concat_axis=0, tiled=True)
    summed = lax.dot_general(
        my_columns,
        lax.all_gather(act, "dp", axis=0, tiled=True),
        (((0,), (0,)), ((), ())),
        preferred_element_type=F32,
    )
    in_grad = lax.psum_scatter(
        lax.dot_general(pre_grad, w_up, (((1,), (1,)), ((), ())), preferred_element_type=F32),
        "tensor",
        scatter_dimension=0,
        tiled=True,
    ).astype(BF16)
    return (in_grad, summed / math.sqrt(all_tokens))


def plane_plan(pre_act, out_grad, w_up, w_down):
    place, shard = lax.axis_index("dp"), lax.axis_index("tensor")
    z, x = place // 2, place % 2
    y, core = shard // 2, shard % 2
    rows, width = out_grad.shape
    tokens, units = pre_act.shape
    half = units // 2
    pair = width // 4
    block = pair // 2
    scale = 1.0 / math.sqrt(tokens * 8)
    chunks = ((0, half // 2), (half // 2, half // 3), (half // 2 + half // 3, half // 6))

    def columns(bit, offset, size):
        low = pre_act[:, offset : offset + size]
        high = pre_act[:, half + offset : half + offset + size]
        return gelu_value_of(either(bit, low, high))

    kept = [columns(x, o, w) for o, w in chunks]
    sent = [columns(1 - x, o, w) for o, w in chunks]

    def spread(own):
        far = xor_permute(own, "dp", 4)
        near = xor_permute(own, "dp", 2)
        return [own, near, far, xor_permute(far, "dp", 2)]

    got0 = xor_permute(sent[0], "dp", 1)
    first_own = spread(kept[0])
    first_got = spread(got0)
    acts = [jnp.concatenate([p for pair_ in zip(first_own, first_got) for p in pair_])]
    for own, out in zip(kept[1:], sent[1:]):
        acts.append(jnp.concatenate(spread(jnp.concatenate([own, xor_permute(out, "dp", 1)]))))

    def slab(k):
        return lax.dynamic_slice(out_grad, (0, (z ^ k) * pair), (rows, pair))

    grad = jnp.stack([slab(0)] + [xor_permute(slab(k), "dp", 2 * k) for k in (1, 2, 3)])
    grad = jnp.stack([grad, xor_permute(grad, "dp", 1)], axis=1)
    other = xor_permute(grad, "tensor", 2)
    grad = jnp.stack([either(y, grad, other), either(y, other, grad)], axis=2)
    other = xor_permute(grad, "tensor", 1)
    grad = jnp.stack([either(core, grad, other), either(core, other, grad)], axis=3)
    grad = grad.reshape(8 * tokens, 2, block)
    mine, theirs = either(x, grad[:, 0], grad[:, 1]), either(x, grad[:, 1], grad[:, 0])
    both = jnp.concatenate([mine, theirs], axis=1)

    gathered = lax.all_gather(out_grad, "tensor", axis=0, tiled=True)
    hidden_grad = lax.dot_general(gathered, w_down, (((1,), (1,)), ((), ())), preferred_element_type=F32)
    pre_grad = (hidden_grad * gelu_slope_of(pre_act)).astype(BF16)
    partial = lax.dot_general(pre_grad, w_up, (((1,), (1,)), ((), ())), preferred_element_type=F32)
    partial = partial.reshape(2, 2, rows, width)
    keep = either(core, partial[:, 0], partial[:, 1])
    give = either(core, partial[:, 1], partial[:, 0])
    keep = keep + xor_permute(give, "tensor", 1)
    in_grad = either(y, keep[0], keep[1]) + xor_permute(either(y, keep[1], keep[0]), "tensor", 2)

    ours, back = [], []
    for act in acts:
        product = scale * lax.dot_general(both, act, (((0,), (0,)), ((), ())), preferred_element_type=F32)
        ours.append(product[:block])
        back.append(xor_permute(product[block:].astype(BF16), "dp", 1))
    ours = jnp.concatenate(ours, axis=1)
    back = jnp.concatenate(back, axis=1).astype(F32)
    down_grad_t = jnp.concatenate([either(x, ours, back), either(x, back, ours)], axis=1)
    return (in_grad.astype(BF16), down_grad_t)


def solution(mesh):
    plan = plane_plan if (mesh.shape["dp"], mesh.shape["tensor"]) == (8, 4) else gathered_plan
    placed = (P("dp", "tensor"), P(("dp", "tensor"), None), P(None, "tensor"), P("tensor", None))
    return jax.shard_map(
        plan,
        mesh=mesh,
        in_specs=placed,
        out_specs=(P(("dp", "tensor"), None), P("dp", "tensor")),
        check_vma=False,
    )
```

time: 175 us -> 158 us (0.903)
  blocking collectives: 53.9 us -> 8.61 us
  starting transfers between devices: 0.08 us -> 26.1 us
  between operations: 15.5 us -> 1 us
  local copies, waits for them, and re-layouts: 7.83 us -> 21.2 us
  other arithmetic: 2.9 us -> 14.8 us
  matrix products: 27.6 us -> 21.1 us
    all_gather x1 -> x0, waiting for transfers between devices: 66.7 us -> none  [per_device(): lax.all_gather(act, 'dp', axis=0, tiled=True)]
    ppermute x0 -> x26, waiting for transfers between devices: none -> 65.2 us  [xor_permute(): return lax.ppermute(value, axis, [(i, i ^ mask) for i in range(count)])]
    all_to_all x1 -> x0, blocking collectives: 43.6 us -> none  [gather_columns(): lax.all_to_all(gathered, 'dp', split_axis=1, concat_axis=0, tiled=True)]
    ppermute x0 -> x26, starting transfers between devices: none -> 26.1 us  [xor_permute(): return lax.ppermute(value, axis, [(i, i ^ mask) for i in range(count)])]
    unnamed x3 -> x34, local copies, waits for them, and re-layouts: 7.1 us -> 14 us
    dot_general x2 -> x4, matrix products: 27.6 us -> 21.1 us  [the longest x1 17.9 us: plane_plan(): lax.dot_general(pre_grad, w_up, (((1,), (1,)), ((), ())), preferred_eleme...]
    select_n x0 -> x4, other arithmetic: none -> 4.33 us  [either(): return jnp.where(bit == 0, low, high)]
    unnamed x0 -> x3, other arithmetic: none -> 4.32 us
  transfers between devices with their start and end apart: 2 -> 26, of which waited for: 1 -> 10; matrix products, arithmetic and copies ran while one was open for 2% -> 27% of each run, Pallas kernels for 0% -> 0%
where the time goes in v1:
time: 158 us
  waiting for transfers between devices  65.2 us (41%)
  starting transfers between devices  26.1 us (17%)
  local copies, waits for them, and re-layouts  21.2 us (13%)
  matrix products  21.1 us (13%)
  other arithmetic  14.8 us (9%)
  blocking collectives  8.61 us (5%)
    ppermute x26, waiting for transfers between devices, xor_permute(): return lax.ppermute(value, axis, [(i, i ^ mask) for i in range(count)])  65.2 us
    ppermute x26, starting transfers between devices, xor_permute(): return lax.ppermute(value, axis, [(i, i ^ mask) for i in range(count)])  26.1 us
    dot_general x1, matrix products, plane_plan(): lax.dot_general(pre_grad, w_up, (((1,), (1,)), ((), ())), preferred_eleme...  17.9 us
    unnamed x34, local copies, waits for them, and re-layouts  14 us
    all_gather x1, blocking collectives, plane_plan(): gathered = lax.all_gather(out_grad, 'tensor', axis=0, tiled=True)  8.61 us
    select_n x4, other arithmetic, either(): return jnp.where(bit == 0, low, high)  4.33 us
    unnamed x3, other arithmetic  4.32 us
    reshape x1, local copies, waits for them, and re-layouts, plane_plan(): grad = grad.reshape(8 * tokens, 2, block)  3.39 us
  transfers between devices with their start and end apart: 26, of which 10 were waited for; matrix products, arithmetic and copies ran while one was open for 27% of the time, Pallas kernels for 0%

profile of v1, /device:TPU:0, one launch (start us, length us, event | category | flops | bytes accessed | tf_op | source)
XLA Modules:
  0.0 158.0 jit_solution(2597104528713561705)
XLA Ops:
  0.7 2.0 %constant_dynamic-update-slice_fusion.7 = (bf16[1024,768]{1,0:T(8,128)(2,1)}, bf16[128,768]{1,0:T(8,128)(2,1)}) fusion(bf16[128,3072]{1,0:T(8,128)(2,1)} %param.4, pred[]{:T(512)S(6)} %eq.13), kind=kLoop, calls=%fused_computation.90 | loop fusion | flops 688127 | bytes 786433
  2.6 3.0 %collective-permute-start.9 = (bf16[128,768]{1,0:T(8,128)(2,1)}, bf16[128,768]{1,0:T(8,128)(2,1)}, u32[]{:S(2)}, u32[]{:S(2)}) collective-permute-start(bf16[128,768]{1,0:T(8,128)(2,1)} %get-tuple-element.9), channel_id=1, source_target_pairs={{0,8},{4,12},{8,0},{12,4},{16,24},{20,28},{24,16},{28,20},{1,9},{5... | collective-permute-start | bytes 589832 | tf_op jit(solution)/shard_map/ppermute | solution.py:27
  5.7 2.6 %collective-permute-start.11 = (bf16[128,768]{1,0:T(8,128)(2,1)}, bf16[128,768]{1,0:T(8,128)(2,1)}, u32[]{:S(2)}, u32[]{:S(2)}) collective-permute-start(bf16[128,768]{1,0:T(8,128)(2,1)} %get-tuple-element.9), channel_id=1, source_target_pairs={{0,16},{4,20},{8,24},{12,28},{16,0},{20,4},{24,8},{28,12},{1,17},{... | collective-permute-start | bytes 589832 | tf_op jit(solution)/shard_map/ppermute | solution.py:27
  8.2 1.5 dynamic-slice_bitcast_fusion
  10.2 3.9 %collective-permute-start.4 = (bf16[32,768]{1,0:T(8,128)(2,1)}, bf16[32,768]{1,0:T(8,128)(2,1)}, u32[]{:S(2)}, u32[]{:S(2)}) collective-permute-start(bf16[32,768]{1,0:T(8,128)(2,1)} %get-tuple-element.26), channel_id=1, source_target_pairs={{0,24},{4,28},{8,16},{12,20},{16,8},{20,12},{24,0},{28,4},{1,25},{... | collective-permute-start | bytes 147464 | tf_op jit(solution)/shard_map/ppermute | solution.py:27
  14.2 1.7 %constant_dynamic-update-slice_fusion.12 = (bf16[1024,512]{1,0:T(8,128)(2,1)}, bf16[128,512]{1,0:T(8,128)(2,1)S(1)}) fusion(bf16[128,3072]{1,0:T(8,128)(2,1)} %param.4, pred[]{:T(512)S(6)} %eq.13), kind=kLoop, calls=%fused_computation.95 | loop fusion | flops 458751 | bytes 524289
  17.4 8.6 %all_gather.3 = bf16[128,3072]{1,0:T(8,128)(2,1)S(1)} all-gather(bf16[32,3072]{1,0:T(8,128)(2,1)S(1)} %copy-done.2), channel_id=1, replica_groups=mesh['dp'=8,'tensor'=4] {'tensor'}, dimensions={0}, use_global_device_ids=true | all-gather | bytes 983040 | tf_op jit(solution)/shard_map/all_gather | solution.py:101
  26.0 17.9 %fusion.7 = f32[128,3072]{1,0:T(8,128)S(1)} fusion(bf16[3072,3072]{1,0:T(8,128)(2,1)} %param.6, bf16[128,3072]{1,0:T(8,128)(2,1)S(1)} %all_gather.3, bf16[3072,3072]{1,0:T(8,128)(2,1)} %param.7, bf16[128,3072]{1,0:T(8,128)(2,1)S(1)} %copy-done), kind=kOutput, calls=%fused_computation.35 | convolution fusion | flops 4836163584 | bytes 40894464 | tf_op jit(solution)/shard_map/dot_general | solution.py:104
  46.7 1.5 collective-permute-start.19
  49.1 7.2 %collective-permute-done.19 = bf16[128,256]{1,0:T(8,128)(2,1)S(1)} collective-permute-done((bf16[128,256]{1,0:T(8,128)(2,1)}, bf16[128,256]{1,0:T(8,128)(2,1)S(1)}, u32[]{:S(2)}, u32[]{:S(2)}) %collective-permute-start.19) | collective-permute-done | bytes 65568 | tf_op jit(solution)/shard_map/ppermute | solution.py:27
  58.5 4.1 %collective-permute-done.20 = bf16[256,256]{1,0:T(8,128)(2,1)S(1)} collective-permute-done((bf16[256,256]{1,0:T(8,128)(2,1)S(1)}, bf16[256,256]{1,0:T(8,128)(2,1)S(1)}, u32[]{:S(2)}, u32[]{:S(2)}) %collective-permute-start.20) | collective-permute-done | bytes 131104 | tf_op jit(solution)/shard_map/ppermute | solution.py:27
  63.2 2.5 %collective-permute-done.21 = bf16[256,256]{1,0:T(8,128)(2,1)S(1)} collective-permute-done((bf16[256,256]{1,0:T(8,128)(2,1)S(1)}, bf16[256,256]{1,0:T(8,128)(2,1)S(1)}, u32[]{:S(2)}, u32[]{:S(2)}) %collective-permute-start.21) | collective-permute-done | bytes 131104 | tf_op jit(solution)/shard_map/ppermute | solution.py:27
  67.9 2.1 %collective-permute-start.22 = (bf16[256,256]{1,0:T(8,128)(2,1)S(1)}, bf16[256,256]{1,0:T(8,128)(2,1)S(1)}, u32[]{:S(2)}, u32[]{:S(2)}) collective-permute-start(bf16[256,256]{1,0:T(8,128)(2,1)S(1)} %collective-permute-done.21), channel_id=1, source_target_pairs={{0,8},{4,12},{8,0},{12,4},{16,24},{20,28},{24,16},{28,20},{1,9},{5... | collective-permute-start | bytes 393224 | tf_op jit(solution)/shard_map/ppermute | solution.py:27
  71.4 13.0 %collective-permute-done.22 = bf16[256,256]{1,0:T(8,128)(2,1)S(1)} collective-permute-done((bf16[256,256]{1,0:T(8,128)(2,1)S(1)}, bf16[256,256]{1,0:T(8,128)(2,1)S(1)}, u32[]{:S(2)}, u32[]{:S(2)}) %collective-permute-start.22) | collective-permute-done | bytes 131104 | tf_op jit(solution)/shard_map/ppermute | solution.py:27
  87.8 6.7 %collective-permute-done.10 = bf16[128,768]{1,0:T(8,128)(2,1)S(1)} collective-permute-done((bf16[128,768]{1,0:T(8,128)(2,1)S(1)}, bf16[128,768]{1,0:T(8,128)(2,1)S(1)}, u32[]{:S(2)}, u32[]{:S(2)}) %collective-permute-start.10) | collective-permute-done | bytes 196640 | tf_op jit(solution)/shard_map/ppermute | solution.py:27
  95.5 2.1 %collective-permute-start.14 = (bf16[128,768]{1,0:T(8,128)(2,1)S(1)}, bf16[128,768]{1,0:T(8,128)(2,1)S(1)}, u32[]{:S(2)}, u32[]{:S(2)}) collective-permute-start(bf16[128,768]{1,0:T(8,128)(2,1)S(1)} %collective-permute-done.12), channel_id=1, source_target_pairs={{0,8},{4,12},{8,0},{12,4},{16,24},{20,28},{24,16},{28,20},{1,9},{5... | collective-permute-start | bytes 589832 | tf_op jit(solution)/shard_map/ppermute | solution.py:27
  98.8 6.7 %collective-permute-done.14 = bf16[128,768]{1,0:T(8,128)(2,1)S(1)} collective-permute-done((bf16[128,768]{1,0:T(8,128)(2,1)S(1)}, bf16[128,768]{1,0:T(8,128)(2,1)S(1)}, u32[]{:S(2)}, u32[]{:S(2)}) %collective-permute-start.14) | collective-permute-done | bytes 196640 | tf_op jit(solution)/shard_map/ppermute | solution.py:27
  110.7 3.4 %reshape.23 = bf16[1024,2,384]{2,1,0:T(2,128)(2,1)S(1)} reshape(bf16[4,2,2,2,32,768]{5,4,3,2,1,0:T(8,128)(2,1)} %copy.18) | data formatting | bytes 3145728 | tf_op jit(solution)/shard_map/reshape | solution.py:97
  114.1 3.9 %broadcast_select_fusion.1 = (bf16[1024,1,384]{2,1,0:T(2,128)(2,1)S(1)}, bf16[1024,1,384]{2,1,0:T(2,128)(2,1)S(1)}) fusion(pred[]{:T(512)S(6)} %eq.13, bf16[1024,2,384]{2,1,0:T(2,128)(2,1)S(1)} %reshape.23), kind=kLoop, calls=%fused_computation.4 | loop fusion | flops 786432 | bytes 3145729 | tf_op jit(solution)/shard_map/jit(_where)/select_n | solution.py:31
  119.4 1.5 convolution_multiply_fusion.1
  122.8 1.6 collective-permute-start.24
  126.4 22.7 %collective-permute-done.25 = bf16[384,256]{0,1:T(8,128)(2,1)S(1)} collective-permute-done((bf16[384,256]{0,1:T(8,128)(2,1)S(1)}, bf16[384,256]{0,1:T(8,128)(2,1)S(1)}, u32[]{:S(2)}, u32[]{:S(2)}) %collective-permute-start.25) | collective-permute-done | bytes 196640 | tf_op jit(solution)/shard_map/ppermute | solution.py:27
  149.5 2.5 %pad_maximum_fusion = f32[384,3072]{0,1:T(8,128)} fusion(f32[384,1536]{0,1:T(8,128)S(1)} %get-tuple-element.15, f32[384,1536]{0,1:T(8,128)S(1)} %get-tuple-element.14), kind=kLoop, calls=%fused_computation | loop fusion | flops 1179648 | bytes 9437184 | tf_op jit(solution)/shard_map/concatenate | solution.py:118
  151.9 6.0 %copy.19 = f32[384,3072]{1,0:T(8,128)} copy(f32[384,3072]{0,1:T(8,128)} %pad_maximum_fusion) | data formatting | bytes 9437184
  (101 shorter events, 28.3 us)
Async XLA Ops:
  2.6 65.2 %collective-permute-start.9 = (bf16[128,768]{1,0:T(8,128)(2,1)}, bf16[128,768]{1,0:T(8,128)(2,1)}, u32[]{:S(2)}, u32[]{:S(2)}) collective-permute-start(bf16[128,768]{1,0:T(8,128)(2,1)} %get-tuple-element.9), channel_id=1, source_target_pairs={{0,8},{4,12},{8,0},{12,4},{16,24},{20,28},{24,16},{28,20},{1,9},{5... | collective-permute-start | bytes 589832 | tf_op jit(solution)/shard_map/ppermute | solution.py:27
  5.7 79.4 %collective-permute-start.11 = (bf16[128,768]{1,0:T(8,128)(2,1)}, bf16[128,768]{1,0:T(8,128)(2,1)}, u32[]{:S(2)}, u32[]{:S(2)}) collective-permute-start(bf16[128,768]{1,0:T(8,128)(2,1)} %get-tuple-element.9), channel_id=1, source_target_pairs={{0,16},{4,20},{8,24},{12,28},{16,0},{20,4},{24,8},{28,12},{1,17},{... | collective-permute-start | bytes 589832 | tf_op jit(solution)/shard_map/ppermute | solution.py:27
  9.8 34.9 %collective-permute-start.2 = (bf16[32,768]{1,0:T(8,128)(2,1)}, bf16[32,768]{1,0:T(8,128)(2,1)}, u32[]{:S(2)}, u32[]{:S(2)}) collective-permute-start(bf16[32,768]{1,0:T(8,128)(2,1)} %get-tuple-element.25), channel_id=1, source_target_pairs={{0,8},{4,12},{8,0},{12,4},{16,24},{20,28},{24,16},{28,20},{1,9},{5... | collective-permute-start | bytes 147464 | tf_op jit(solution)/shard_map/ppermute | solution.py:27
  10.2 35.9 %collective-permute-start.3 = (bf16[32,768]{1,0:T(8,128)(2,1)}, bf16[32,768]{1,0:T(8,128)(2,1)}, u32[]{:S(2)}, u32[]{:S(2)}) collective-permute-start(bf16[32,768]{1,0:T(8,128)(2,1)} %get-tuple-element.27), channel_id=1, source_target_pairs={{0,16},{4,20},{8,24},{12,28},{16,0},{20,4},{24,8},{28,12},{1,17},{... | collective-permute-start | bytes 147464 | tf_op jit(solution)/shard_map/ppermute | solution.py:27
  10.2 36.5 %collective-permute-start.4 = (bf16[32,768]{1,0:T(8,128)(2,1)}, bf16[32,768]{1,0:T(8,128)(2,1)}, u32[]{:S(2)}, u32[]{:S(2)}) collective-permute-start(bf16[32,768]{1,0:T(8,128)(2,1)} %get-tuple-element.26), channel_id=1, source_target_pairs={{0,24},{4,28},{8,16},{12,20},{16,8},{20,12},{24,0},{28,4},{1,25},{... | collective-permute-start | bytes 147464 | tf_op jit(solution)/shard_map/ppermute | solution.py:27
  44.7 23.1 %collective-permute-start.8 = (bf16[128,768]{1,0:T(8,128)(2,1)}, bf16[128,768]{1,0:T(8,128)(2,1)S(1)}, u32[]{:S(2)}, u32[]{:S(2)}) collective-permute-start(bf16[128,768]{1,0:T(8,128)(2,1)} %fusion.15), channel_id=1, source_target_pairs={{0,4},{4,0},{8,12},{12,8},{16,20},{20,16},{24,28},{28,24},{1,5},{5... | collective-permute-start | bytes 589832 | tf_op jit(solution)/shard_map/ppermute | solution.py:27
  46.2 10.8 %collective-permute-start.15 = (bf16[128,512]{1,0:T(8,128)(2,1)S(1)}, bf16[128,512]{1,0:T(8,128)(2,1)S(1)}, u32[]{:S(2)}, u32[]{:S(2)}) collective-permute-start(bf16[128,512]{1,0:T(8,128)(2,1)S(1)} %fusion.24), channel_id=1, source_target_pairs={{0,4},{4,0},{8,12},{12,8},{16,20},{20,16},{24,28},{28,24},{1,5},{5... | collective-permute-start | bytes 393224 | tf_op jit(solution)/shard_map/ppermute | solution.py:27
  46.7 9.5 %collective-permute-start.19 = (bf16[128,256]{1,0:T(8,128)(2,1)}, bf16[128,256]{1,0:T(8,128)(2,1)S(1)}, u32[]{:S(2)}, u32[]{:S(2)}) collective-permute-start(bf16[128,256]{1,0:T(8,128)(2,1)} %fusion.32), channel_id=1, source_target_pairs={{0,4},{4,0},{8,12},{12,8},{16,20},{20,16},{24,28},{28,24},{1,5},{5... | collective-permute-start | bytes 196616 | tf_op jit(solution)/shard_map/ppermute | solution.py:27
  56.3 6.3 %collective-permute-start.20 = (bf16[256,256]{1,0:T(8,128)(2,1)S(1)}, bf16[256,256]{1,0:T(8,128)(2,1)S(1)}, u32[]{:S(2)}, u32[]{:S(2)}) collective-permute-start(bf16[256,256]{1,0:T(8,128)(2,1)S(1)} %pad_maximum_fusion.12), channel_id=1, source_target_pairs={{0,8},{4,12},{8,0},{12,4},{16,24},{20,28},{24,16},{28,20},{1,9},{5... | collective-permute-start | bytes 393224 | tf_op jit(solution)/shard_map/ppermute | solution.py:27
  57.0 8.7 %collective-permute-start.21 = (bf16[256,256]{1,0:T(8,128)(2,1)S(1)}, bf16[256,256]{1,0:T(8,128)(2,1)S(1)}, u32[]{:S(2)}, u32[]{:S(2)}) collective-permute-start(bf16[256,256]{1,0:T(8,128)(2,1)S(1)} %pad_maximum_fusion.12), channel_id=1, source_target_pairs={{0,16},{4,20},{8,24},{12,28},{16,0},{20,4},{24,8},{28,12},{1,17},{... | collective-permute-start | bytes 393224 | tf_op jit(solution)/shard_map/ppermute | solution.py:27
  62.5 44.4 %collective-permute-start = (f32[2,32,3072]{2,1,0:T(8,128)S(1)}, f32[2,32,3072]{2,1,0:T(8,128)S(1)}, u32[]{:S(2)}, u32[]{:S(2)}) collective-permute-start(f32[2,32,3072]{2,1,0:T(8,128)S(1)} %select_bitcast_fusion.2), channel_id=1, source_target_pairs={{0,1},{1,0},{2,3},{3,2},{4,5},{5,4},{6,7},{7,6},{8,9},{9,8},{10,11... | collective-permute-start | bytes 2359304 | tf_op jit(solution)/shard_map/ppermute | solution.py:27
  67.8 18.2 %collective-permute-start.16 = (bf16[256,512]{1,0:T(8,128)(2,1)S(1)}, bf16[256,512]{1,0:T(8,128)(2,1)S(1)}, u32[]{:S(2)}, u32[]{:S(2)}) collective-permute-start(bf16[256,512]{1,0:T(8,128)(2,1)S(1)} %pad_maximum_fusion.10), channel_id=1, source_target_pairs={{0,8},{4,12},{8,0},{12,4},{16,24},{20,28},{24,16},{28,20},{1,9},{5... | collective-permute-start | bytes 786440 | tf_op jit(solution)/shard_map/ppermute | solution.py:27
  67.9 16.6 %collective-permute-start.22 = (bf16[256,256]{1,0:T(8,128)(2,1)S(1)}, bf16[256,256]{1,0:T(8,128)(2,1)S(1)}, u32[]{:S(2)}, u32[]{:S(2)}) collective-permute-start(bf16[256,256]{1,0:T(8,128)(2,1)S(1)} %collective-permute-done.21), channel_id=1, source_target_pairs={{0,8},{4,12},{8,0},{12,4},{16,24},{20,28},{24,16},{28,20},{1,9},{5... | collective-permute-start | bytes 393224 | tf_op jit(solution)/shard_map/ppermute | solution.py:27
  71.4 15.9 %collective-permute-start.17 = (bf16[256,512]{1,0:T(8,128)(2,1)S(1)}, bf16[256,512]{1,0:T(8,128)(2,1)S(1)}, u32[]{:S(2)}, u32[]{:S(2)}) collective-permute-start(bf16[256,512]{1,0:T(8,128)(2,1)S(1)} %pad_maximum_fusion.10), channel_id=1, source_target_pairs={{0,16},{4,20},{8,24},{12,28},{16,0},{20,4},{24,8},{28,12},{1,17},{... | collective-permute-start | bytes 786440 | tf_op jit(solution)/shard_map/ppermute | solution.py:27
  84.4 10.1 %collective-permute-start.10 = (bf16[128,768]{1,0:T(8,128)(2,1)S(1)}, bf16[128,768]{1,0:T(8,128)(2,1)S(1)}, u32[]{:S(2)}, u32[]{:S(2)}) collective-permute-start(bf16[128,768]{1,0:T(8,128)(2,1)S(1)} %collective-permute-done.8), channel_id=1, source_target_pairs={{0,8},{4,12},{8,0},{12,4},{16,24},{20,28},{24,16},{28,20},{1,9},{5... | collective-permute-start | bytes 589832 | tf_op jit(solution)/shard_map/ppermute | solution.py:27
  85.1 10.4 %collective-permute-start.12 = (bf16[128,768]{1,0:T(8,128)(2,1)S(1)}, bf16[128,768]{1,0:T(8,128)(2,1)S(1)}, u32[]{:S(2)}, u32[]{:S(2)}) collective-permute-start(bf16[128,768]{1,0:T(8,128)(2,1)S(1)} %collective-permute-done.8), channel_id=1, source_target_pairs={{0,16},{4,20},{8,24},{12,28},{16,0},{20,4},{24,8},{28,12},{1,17},{... | collective-permute-start | bytes 589832 | tf_op jit(solution)/shard_map/ppermute | solution.py:27
  86.0 12.7 %collective-permute-start.13 = (bf16[128,768]{1,0:T(8,128)(2,1)}, bf16[128,768]{1,0:T(8,128)(2,1)S(1)}, u32[]{:S(2)}, u32[]{:S(2)}) collective-permute-start(bf16[128,768]{1,0:T(8,128)(2,1)} %collective-permute-done.11), channel_id=1, source_target_pairs={{0,8},{4,12},{8,0},{12,4},{16,24},{20,28},{24,16},{28,20},{1,9},{5... | collective-permute-start | bytes 589832 | tf_op jit(solution)/shard_map/ppermute | solution.py:27
  87.2 19.5 %collective-permute-start.6 = (bf16[4,2,32,768]{3,2,0,1:T(8,128)(2,1)S(1)}, bf16[4,2,32,768]{3,2,0,1:T(8,128)(2,1)S(1)}, u32[]{:S(2)}, u32[]{:S(2)}) collective-permute-start(bf16[4,2,32,768]{3,2,0,1:T(8,128)(2,1)S(1)} %pad_maximum_fusion.9), channel_id=1, source_target_pairs={{0,2},{1,3},{2,0},{3,1},{4,6},{5,7},{6,4},{7,5},{8,10},{9,11},{10,... | collective-permute-start | bytes 1179656 | tf_op jit(solution)/shard_map/ppermute | solution.py:27
  94.5 12.4 %collective-permute-start.18 = (bf16[256,512]{1,0:T(8,128)(2,1)S(1)}, bf16[256,512]{1,0:T(8,128)(2,1)S(1)}, u32[]{:S(2)}, u32[]{:S(2)}) collective-permute-start(bf16[256,512]{1,0:T(8,128)(2,1)S(1)} %collective-permute-done.17), channel_id=1, source_target_pairs={{0,8},{4,12},{8,0},{12,4},{16,24},{20,28},{24,16},{28,20},{1,9},{5... | collective-permute-start | bytes 786440 | tf_op jit(solution)/shard_map/ppermute | solution.py:27
  95.5 10.0 %collective-permute-start.14 = (bf16[128,768]{1,0:T(8,128)(2,1)S(1)}, bf16[128,768]{1,0:T(8,128)(2,1)S(1)}, u32[]{:S(2)}, u32[]{:S(2)}) collective-permute-start(bf16[128,768]{1,0:T(8,128)(2,1)S(1)} %collective-permute-done.12), channel_id=1, source_target_pairs={{0,8},{4,12},{8,0},{12,4},{16,24},{20,28},{24,16},{28,20},{1,9},{5... | collective-permute-start | bytes 589832 | tf_op jit(solution)/shard_map/ppermute | solution.py:27
  108.0 17.6 %collective-permute-start.1 = (f32[32,3072]{1,0:T(8,128)S(1)}, f32[32,3072]{1,0:T(8,128)S(1)}, u32[]{:S(2)}, u32[]{:S(2)}) collective-permute-start(f32[32,3072]{1,0:T(8,128)S(1)} %select_bitcast_fusion.5), channel_id=1, source_target_pairs={{0,2},{1,3},{2,0},{3,1},{4,6},{5,7},{6,4},{7,5},{8,10},{9,11},{10,... | collective-permute-start | bytes 1179656 | tf_op jit(solution)/shard_map/ppermute | solution.py:27
  121.1 28.1 %collective-permute-start.23 = (bf16[384,768]{0,1:T(8,128)(2,1)S(1)}, bf16[384,768]{0,1:T(8,128)(2,1)S(1)}, u32[]{:S(2)}, u32[]{:S(2)}) collective-permute-start(bf16[384,768]{0,1:T(8,128)(2,1)S(1)} %slice.132), channel_id=1, source_target_pairs={{0,4},{4,0},{8,12},{12,8},{16,20},{20,16},{24,28},{28,24},{1,5},{5... | collective-permute-start | bytes 1769480 | tf_op jit(solution)/shard_map/ppermute | solution.py:27
  122.8 26.4 %collective-permute-start.24 = (bf16[384,512]{0,1:T(8,128)(2,1)S(1)}, bf16[384,512]{0,1:T(8,128)(2,1)S(1)}, u32[]{:S(2)}, u32[]{:S(2)}) collective-permute-start(bf16[384,512]{0,1:T(8,128)(2,1)S(1)} %slice.133), channel_id=1, source_target_pairs={{0,4},{4,0},{8,12},{12,8},{16,20},{20,16},{24,28},{28,24},{1,5},{5... | collective-permute-start | bytes 1179656 | tf_op jit(solution)/shard_map/ppermute | solution.py:27
  125.0 24.1 %collective-permute-start.25 = (bf16[384,256]{0,1:T(8,128)(2,1)S(1)}, bf16[384,256]{0,1:T(8,128)(2,1)S(1)}, u32[]{:S(2)}, u32[]{:S(2)}) collective-permute-start(bf16[384,256]{0,1:T(8,128)(2,1)S(1)} %slice.134), channel_id=1, source_target_pairs={{0,4},{4,0},{8,12},{12,8},{16,20},{20,16},{24,28},{28,24},{1,5},{5... | collective-permute-start | bytes 589832 | tf_op jit(solution)/shard_map/ppermute | solution.py:27
  (13 other events, 129.2 us)

commit v2 on v1

v2 whole, which is shorter than its diff:
```python
import math

import jax
import jax.numpy as jnp
from jax import lax
from jax.experimental import pallas as pl
from jax.experimental.pallas import tpu as pltpu
from jax.sharding import PartitionSpec as P

BF16 = jnp.bfloat16
F32 = jnp.float32


def gelu_value_of(pre):
    pre_float = pre.astype(F32)
    normal_cdf = 0.5 * (1.0 + jax.scipy.special.erf(pre_float / math.sqrt(2.0)))
    return (pre_float * normal_cdf).astype(BF16)


def gelu_slope_of(pre):
    pre_float = pre.astype(F32)
    normal_cdf = 0.5 * (1.0 + jax.scipy.special.erf(pre_float / math.sqrt(2.0)))
    density = jnp.exp(-0.5 * pre_float * pre_float) / math.sqrt(2.0 * math.pi)
    return normal_cdf + pre_float * density


def xor_permute(value, axis, mask):
    count = lax.axis_size(axis)
    return lax.ppermute(value, axis, [(i, i ^ mask) for i in range(count)])


def either(bit, low, high):
    return jnp.where(bit == 0, low, high)


def gathered_plan(pre_act, out_grad, w_up, w_down):
    act = gelu_value_of(pre_act)
    gathered = lax.all_gather(out_grad, "tensor", axis=0, tiled=True)
    hidden_grad = lax.dot_general(gathered, w_down, (((1,), (1,)), ((), ())), preferred_element_type=F32)
    pre_grad = (hidden_grad * gelu_slope_of(pre_act)).astype(BF16)
    all_tokens = gathered.shape[0] * lax.axis_size("dp")
    my_columns = lax.all_to_all(gathered, "dp", split_axis=1, concat_axis=0, tiled=True)
    summed = lax.dot_general(
        my_columns,
        lax.all_gather(act, "dp", axis=0, tiled=True),
        (((0,), (0,)), ((), ())),
        preferred_element_type=F32,
    )
    in_grad = lax.psum_scatter(
        lax.dot_general(pre_grad, w_up, (((1,), (1,)), ((), ())), preferred_element_type=F32),
        "tensor",
        scatter_dimension=0,
        tiled=True,
    ).astype(BF16)
    return (in_grad, summed / math.sqrt(all_tokens))


VMEM_LIMIT = 48 * 1024 * 1024
NT = (((1,), (1,)), ((), ()))


def params():
    return pltpu.CompilerParams(vmem_limit_bytes=VMEM_LIMIT)


def cost(flops, moved):
    return pl.CostEstimate(flops=flops, bytes_accessed=moved, transcendentals=0)


def whole():
    return pl.BlockSpec(memory_space=pltpu.VMEM)


def weights_pass(place, own, got, slope, w_up, w_down, before, first, last, size):
    pairs, rows, width = own.shape
    tokens = 2 * pairs * rows
    start = first // size

    def body(place_ref, own_ref, got_ref, slope_ref, up_ref, down_ref, *rest):
        before_ref = rest[0] if before is not None else None
        total_ref, grad_ref = rest[-2:]

        @pl.when(pl.program_id(0) == 0)
        def _():
            shard = place_ref[1]
            for i in range(pairs):
                for ref, bit in ((own_ref, 0), (got_ref, 1)):
                    at = pl.multiple_of(((2 * i + bit) ^ shard) * rows, rows)
                    grad_ref[pl.ds(at, rows), :] = ref[i]
            total_ref[...] = jnp.zeros_like(total_ref) if before_ref is None else before_ref[...]

        hidden = lax.dot_general(grad_ref[...], down_ref[...], NT, preferred_element_type=F32)
        pre_grad = (hidden * slope_ref[...]).astype(BF16)
        total_ref[...] += lax.dot_general(pre_grad, up_ref[...], NT, preferred_element_type=F32)

    const2, const3 = (lambda i: (0, 0)), (lambda i: (0, 0, 0))
    specs = [
        pl.BlockSpec(memory_space=pltpu.SMEM),
        pl.BlockSpec(own.shape, const3),
        pl.BlockSpec(got.shape, const3),
        pl.BlockSpec((tokens, size), lambda i: (0, i + start)),
        pl.BlockSpec((width, size), lambda i: (0, i + start)),
        pl.BlockSpec((size, width), lambda i: (i + start, 0)),
    ]
    operands = [place, own, got, slope, w_up, w_down]
    if before is not None:
        specs.append(pl.BlockSpec((tokens, width), const2))
        operands.append(before)
    units = last - first
    return pl.pallas_call(
        body,
        grid=(units // size,),
        in_specs=specs,
        out_specs=pl.BlockSpec((tokens, width), const2),
        out_shape=jax.ShapeDtypeStruct((tokens, width), F32),
        scratch_shapes=[pltpu.VMEM((tokens, width), BF16)],
        compiler_params=params(),
        cost_estimate=cost(4 * tokens * units * width, 4 * units * width),
    )(*operands)


def prepare(place, own, got):
    _, _, depth, rows, pair = own.shape
    block = pair // 2
    tokens = 2 * depth * 4 * rows

    def body(place_ref, own_ref, got_ref, mine_ref, theirs_ref, held_ref):
        x, shard = place_ref[0], place_ref[1]
        for k in range(depth):
            for j in range(2):
                for i in range(2):
                    for ref, bit in ((own_ref, 0), (got_ref, 1)):
                        at = (2 * k + j) * 4 * rows + ((2 * i + bit) ^ shard) * rows
                        held_ref[pl.ds(pl.multiple_of(at, rows), rows), :] = ref[i, j, k]
        for out, bit in ((mine_ref, x), (theirs_ref, 1 - x)):
            columns = pl.ds(pl.multiple_of(bit * block, 128), block)
            out[...] = held_ref[:, columns].T

    shape = jax.ShapeDtypeStruct((block, tokens), BF16)
    return pl.pallas_call(
        body,
        in_specs=[pl.BlockSpec(memory_space=pltpu.SMEM), whole(), whole()],
        out_specs=[whole(), whole()],
        out_shape=[shape, shape],
        scratch_shapes=[pltpu.VMEM((tokens, pair), BF16)],
        compiler_params=params(),
        cost_estimate=cost(0, 8 * tokens * pair),
    )(place, own, got)


def contract(grad_ref, refs, scale):
    total, at = None, 0
    for ref in refs:
        depth = ref.shape[0]
        part = jnp.dot(grad_ref[:, at : at + depth], ref[...], preferred_element_type=F32)
        total = part if total is None else total + part
        at += depth
    return total * scale


def their_product(theirs, pieces, scale):
    def body(grad_ref, *refs):
        refs[-1][...] = contract(grad_ref, refs[:-1], scale).astype(BF16)

    block, tokens = theirs.shape
    size = pieces[0].shape[1]
    return pl.pallas_call(
        body,
        in_specs=[whole()] * (1 + len(pieces)),
        out_specs=whole(),
        out_shape=jax.ShapeDtypeStruct((block, size), BF16),
        compiler_params=params(),
        cost_estimate=cost(2 * block * tokens * size, 4 * tokens * size),
    )(theirs, *pieces)


def my_product(place, mine, chunks, backs, width, scale):
    block, tokens = mine.shape
    counts = [len(pieces) for pieces in chunks]
    sizes = [pieces[0].shape[1] for pieces in chunks]
    half = sum(sizes)

    def body(place_ref, grad_ref, *refs):
        pieces, returned = refs[: sum(counts)], refs[sum(counts) : sum(counts) + len(backs)]
        out_ref, held_ref, sems = refs[sum(counts) + len(backs) :]
        copies = []

        def store(slot, offset, size, side, value):
            here = held_ref.at[:, pl.ds(side * half + offset, size)]
            here[...] = value
            bit = place_ref[0] if side == 0 else 1 - place_ref[0]
            to = pl.ds(pl.multiple_of(bit * half + offset, 128), size)
            copies.append(pltpu.make_async_copy(here, out_ref.at[:, to], sems.at[slot]))
            copies[-1].start()

        offset = 0
        for slot, (ref, size) in enumerate(zip(returned, sizes)):
            store(slot, offset, size, 1, ref[...].astype(F32))
            offset += size
        offset = at = 0
        for slot, (count, size) in enumerate(zip(counts, sizes)):
            store(len(backs) + slot, offset, size, 0, contract(grad_ref, pieces[at : at + count], scale))
            offset, at = offset + size, at + count
        for copy in copies:
            copy.wait()

    flat = [p for pieces in chunks for p in pieces]
    return pl.pallas_call(
        body,
        in_specs=[pl.BlockSpec(memory_space=pltpu.SMEM)] + [whole()] * (1 + len(flat) + len(backs)),
        out_specs=pl.BlockSpec(memory_space=pl.ANY),
        out_shape=jax.ShapeDtypeStruct((block, width), F32),
        scratch_shapes=[pltpu.VMEM((block, width), F32), pltpu.SemaphoreType.DMA((len(backs) + len(chunks),))],
        compiler_params=params(),
        cost_estimate=cost(2 * block * tokens * half, 4 * block * width),
    )(place, mine, *flat, *backs)


def place_back(place, result, back, offset):
    block, width = result.shape
    size = back.shape[1]

    def body(place_ref, back_ref, _, out_ref, held_ref, sem):
        held_ref[...] = back_ref[...].astype(F32)
        to = pl.ds(pl.multiple_of((1 - place_ref[0]) * (width // 2) + offset, 128), size)
        copy = pltpu.make_async_copy(held_ref, out_ref.at[:, to], sem)
        copy.start()
        copy.wait()

    return pl.pallas_call(
        body,
        in_specs=[pl.BlockSpec(memory_space=pltpu.SMEM), whole(), pl.BlockSpec(memory_space=pl.ANY)],
        out_specs=pl.BlockSpec(memory_space=pl.ANY),
        out_shape=jax.ShapeDtypeStruct(result.shape, F32),
        input_output_aliases={2: 0},
        scratch_shapes=[pltpu.VMEM((block, size), F32), pltpu.SemaphoreType.DMA],
        compiler_params=params(),
        cost_estimate=cost(0, 4 * block * size),
    )(place, back, result)


def after(value, *others):
    return lax.optimization_barrier((value, *others))[0]


def plane_plan(pre_act, out_grad, w_up, w_down):
    at, shard = lax.axis_index("dp"), lax.axis_index("tensor")
    z, x = at // 2, at % 2
    y, core = shard // 2, shard % 2
    place = jnp.stack([x, shard]).astype(jnp.int32)
    rows, width = out_grad.shape
    tokens, units = pre_act.shape
    half = units // 2
    pair = width // 4
    scale = 1.0 / math.sqrt(tokens * 8)
    chunks = ((0, half // 2), (half // 2, half // 3), (half // 2 + half // 3, half // 6))

    def columns(pre, bit, offset, size):
        low = pre[:, offset : offset + size]
        high = pre[:, half + offset : half + offset + size]
        return gelu_value_of(either(bit, low, high))

    def slab(k):
        return lax.dynamic_slice(out_grad, (0, (z ^ k) * pair), (rows, pair))

    grad = jnp.stack([slab(0)] + [xor_permute(slab(k), "dp", 2 * k) for k in (1, 2, 3)])

    kept0, sent0 = columns(pre_act, x, *chunks[0]), columns(pre_act, 1 - x, *chunks[0])

    got0 = xor_permute(sent0, "dp", 1)
    far_own = xor_permute(kept0, "dp", 4)
    later_act, later_kept0, later_grad, grad = lax.optimization_barrier((pre_act, kept0, out_grad, grad))
    near_own = xor_permute(later_kept0, "dp", 2)
    own_rows = xor_permute(later_grad, "tensor", 2)
    grad_x = xor_permute(grad, "dp", 1)
    slope = gelu_slope_of(later_act)
    kept = [columns(later_act, x, o, w) for o, w in chunks[1:]]
    sent = [columns(later_act, 1 - x, o, w) for o, w in chunks[1:]]

    group = jnp.stack([out_grad, own_rows])
    group_got = xor_permute(group, "tensor", 1)
    far_got = xor_permute(got0, "dp", 4)
    near_got = xor_permute(got0, "dp", 2)
    both_x = jnp.stack([grad, grad_x])
    grad_y = xor_permute(both_x, "tensor", 2)
    got1 = xor_permute(after(sent[0], grad_x), "dp", 1)
    last_own = xor_permute(far_own, "dp", 2)

    size = 256
    quarter = units // 4

    def weights(part, before, *waits):
        if before is None:
            first_group = after(group, *waits)
        else:
            first_group, before = group, after(before, *waits)
        return weights_pass(
            place, first_group, group_got, slope, w_up, w_down, before, part * quarter, (part + 1) * quarter, size
        )

    partial = weights(0, None, slope, far_own, near_own)
    got2 = xor_permute(after(sent[1], got1), "dp", 1)
    partial = weights(1, partial, grad_y, got1)
    both_y = jnp.stack([both_x, grad_y])
    grad_core = xor_permute(both_y, "tensor", 1)
    own1 = jnp.concatenate([kept[0], got1])
    far1 = xor_permute(after(own1, near_got), "dp", 4)
    last_got = xor_permute(far_got, "dp", 2)
    partial = weights(2, partial, far_got, near_got, got2)
    near1 = xor_permute(after(own1, last_own), "dp", 2)
    partial = weights(3, partial, last_own)
    mine, theirs = prepare(place, both_y, after(grad_core, partial))
    own2 = after(jnp.concatenate([kept[1], got2]), last_got)
    far2 = xor_permute(own2, "dp", 4)
    last1 = xor_permute(far1, "dp", 2)
    near2 = xor_permute(after(own2, near1), "dp", 2)
    last2 = xor_permute(far2, "dp", 2)
    acts = [
        [kept0, got0, near_own, near_got, far_own, far_got, last_own, last_got],
        [own1, near1, far1, last1],
        [own2, near2, far2, last2],
    ]

    partial = partial.reshape(2, 2, rows, width)
    keep = either(core, partial[:, 0], partial[:, 1])
    give = either(core, partial[:, 1], partial[:, 0])
    keep = keep + xor_permute(give, "tensor", 1)
    in_grad = either(y, keep[0], keep[1]) + xor_permute(either(y, keep[1], keep[0]), "tensor", 2)

    backs = [xor_permute(their_product(theirs, pieces, scale), "dp", 1) for pieces in acts]
    result = my_product(place, mine, acts, backs[:-1], units, scale)
    result = place_back(place, result, backs[-1], chunks[-1][0])
    return (in_grad.astype(BF16), result)


def solution(mesh):
    plan = plane_plan if (mesh.shape["dp"], mesh.shape["tensor"]) == (8, 4) else gathered_plan
    placed = (P("dp", "tensor"), P(("dp", "tensor"), None), P(None, "tensor"), P("tensor", None))
    return jax.shard_map(
        plan,
        mesh=mesh,
        in_specs=placed,
        out_specs=(P(("dp", "tensor"), None), P("dp", "tensor")),
        check_vma=False,
    )
```

time: 158 us -> 138 us (0.87)
  Pallas kernels: 0 us -> 39.9 us
  matrix products: 21.1 us -> 0 us
  local copies, waits for them, and re-layouts: 21.2 us -> 1 us
  blocking collectives: 8.61 us -> 0 us
  waiting for transfers between devices: 65.2 us -> 56.9 us
  other arithmetic: 14.8 us -> 7.24 us
  starting transfers between devices: 26.1 us -> 31.6 us
    pallas_call x0 -> x10, Pallas kernels: none -> 39.9 us  [the longest x4 31.4 us: weights_pass(): pl.pallas_call(body, grid=(units // size,), in_specs=specs, out_specs=pl....]
    dot_general x4 -> x0, matrix products: 21.1 us -> none  [the longest x1 17.9 us: plane_plan(): lax.dot_general(pre_grad, w_up, (((1,), (1,)), ((), ())), preferred_eleme...]
    unnamed x34 -> x12, local copies, waits for them, and re-layouts: 14 us -> 0.03 us
    all_gather x1 -> x0, blocking collectives: 8.61 us -> none  [plane_plan(): gathered = lax.all_gather(out_grad, 'tensor', axis=0, tiled=True)]
    ppermute x26 -> x28, waiting for transfers between devices: 65.2 us -> 56.9 us  [xor_permute(): return lax.ppermute(value, axis, [(i, i ^ mask) for i in range(count)])]
    ppermute x26 -> x28, starting transfers between devices: 26.1 us -> 31.6 us  [xor_permute(): return lax.ppermute(value, axis, [(i, i ^ mask) for i in range(count)])]
    unnamed x3 -> x0, other arithmetic: 4.32 us -> none
    reshape x1 -> x0, local copies, waits for them, and re-layouts: 3.39 us -> none  [plane_plan(): grad = grad.reshape(8 * tokens, 2, block)]
  transfers between devices with their start and end apart: 26 -> 28, of which waited for: 10 -> 8; matrix products, arithmetic and copies ran while one was open for 27% -> 5% of each run, Pallas kernels for 0% -> 22%
where the time goes in v2:
time: 138 us
  waiting for transfers between devices  56.9 us (41%)
  Pallas kernels  39.9 us (29%)
  starting transfers between devices  31.6 us (23%)
  other arithmetic  7.24 us (5%)
    ppermute x28, waiting for transfers between devices, xor_permute(): return lax.ppermute(value, axis, [(i, i ^ mask) for i in range(count)])  56.9 us
    ppermute x28, starting transfers between devices, xor_permute(): return lax.ppermute(value, axis, [(i, i ^ mask) for i in range(count)])  31.6 us
    pallas_call x4, Pallas kernels, weights_pass(): pl.pallas_call(body, grid=(units // size,), in_specs=specs, out_specs=pl....  31.4 us
    pallas_call x1, Pallas kernels, my_product(): pl.pallas_call(body, in_specs=[pl.BlockSpec(memory_space=pltpu.SMEM)] + [...  3.76 us
  transfers between devices with their start and end apart: 28, of which 8 were waited for; matrix products, arithmetic and copies ran while one was open for 5% of the time, Pallas kernels for 22%

profile of v2, /device:TPU:0, one launch (start us, length us, event | category | flops | bytes accessed | tf_op | source)
XLA Modules:
  0.0 137.7 jit_solution(344585211693113295)
XLA Ops:
  1.7 5.1 %collective-permute-start.2 = (bf16[32,768]{1,0:T(8,128)(2,1)S(1)}, bf16[32,768]{1,0:T(8,128)(2,1)S(1)}, u32[]{:S(2)}, u32[]{:S(2)}) collective-permute-start(bf16[32,768]{1,0:T(8,128)(2,1)S(1)} %get-tuple-element.47), channel_id=1, source_target_pairs={{0,24},{4,28},{8,16},{12,20},{16,8},{20,12},{24,0},{28,4},{1,25},{... | collective-permute-start | bytes 147464 | tf_op jit(solution)/shard_map/ppermute | solution.py:29
  8.6 2.4 %collective-permute-start.5 = (bf16[128,768]{1,0:T(8,128)(2,1)S(1)}, bf16[128,768]{1,0:T(8,128)(2,1)S(1)}, u32[]{:S(2)}, u32[]{:S(2)}) collective-permute-start(bf16[128,768]{1,0:T(8,128)(2,1)S(1)} %get-tuple-element.21.refs_0_), channel_id=1, source_target_pairs={{0,16},{4,20},{8,24},{12,28},{16,0},{20,4},{24,8},{28,12},{1,17},{... | collective-permute-start | bytes 589832 | tf_op jit(solution)/shard_map/ppermute | solution.py:29
  11.0 1.5 %collective-permute-start.10 = (bf16[128,768]{1,0:T(8,128)(2,1)S(1)}, bf16[128,768]{1,0:T(8,128)(2,1)S(1)}, u32[]{:S(2)}, u32[]{:S(2)}) collective-permute-start(bf16[128,768]{1,0:T(8,128)(2,1)S(1)} %get-tuple-element.40), channel_id=1, source_target_pairs={{0,4},{4,0},{8,12},{12,8},{16,20},{20,16},{24,28},{28,24},{1,5},{5... | collective-permute-start | bytes 589832 | tf_op jit(solution)/shard_map/ppermute | solution.py:29
  12.6 1.6 %collective-permute-start.3 = (bf16[32,3072]{1,0:T(8,128)(2,1)S(1)}, bf16[32,3072]{1,0:T(8,128)(2,1)S(1)}, u32[]{:S(2)}, u32[]{:S(2)}) collective-permute-start(bf16[32,3072]{1,0:T(8,128)(2,1)S(1)} %copy-done.1), channel_id=1, source_target_pairs={{0,2},{1,3},{2,0},{3,1},{4,6},{5,7},{6,4},{7,5},{8,10},{9,11},{10,... | collective-permute-start | bytes 589832 | tf_op jit(solution)/shard_map/ppermute | solution.py:29
  15.9 2.5 %collective-permute-done.3 = bf16[32,3072]{1,0:T(8,128)(2,1)S(1)} collective-permute-done((bf16[32,3072]{1,0:T(8,128)(2,1)S(1)}, bf16[32,3072]{1,0:T(8,128)(2,1)S(1)}, u32[]{:S(2)}, u32[]{:S(2)}) %collective-permute-start.3) | collective-permute-done | bytes 196640 | tf_op jit(solution)/shard_map/ppermute | solution.py:29
  18.5 2.5 %collective-permute-done.7 = bf16[4,32,768]{2,1,0:T(8,128)(2,1)S(1)} collective-permute-done((bf16[4,32,768]{2,1,0:T(8,128)(2,1)S(1)}, bf16[4,32,768]{2,1,0:T(8,128)(2,1)S(1)}, u32[]{:S(2)}, u32[]{:S(2)}) %collective-permute-start.7) | collective-permute-done | bytes 196640 | tf_op jit(solution)/shard_map/ppermute | solution.py:29
  21.1 1.6 %collective-permute-start.8 = (bf16[2,4,32,768]{3,2,1,0:T(8,128)(2,1)S(1)}, bf16[2,4,32,768]{3,2,1,0:T(8,128)(2,1)S(1)}, u32[]{:S(2)}, u32[]{:S(2)}) collective-permute-start(bf16[2,4,32,768]{3,2,1,0:T(8,128)(2,1)S(1)} %get-tuple-element.43), channel_id=1, source_target_pairs={{0,2},{1,3},{2,0},{3,1},{4,6},{5,7},{6,4},{7,5},{8,10},{9,11},{10,... | collective-permute-start | bytes 1179656 | tf_op jit(solution)/shard_map/ppermute | solution.py:29
  22.8 2.0 %collective-permute-start.6 = (bf16[128,768]{1,0:T(8,128)(2,1)S(1)}, bf16[128,768]{1,0:T(8,128)(2,1)S(1)}, u32[]{:S(2)}, u32[]{:S(2)}) collective-permute-start(bf16[128,768]{1,0:T(8,128)(2,1)S(1)} %get-tuple-element.21.refs_0_), channel_id=1, source_target_pairs={{0,8},{4,12},{8,0},{12,4},{16,24},{20,28},{24,16},{28,20},{1,9},{5... | collective-permute-start | bytes 589832 | tf_op jit(solution)/shard_map/ppermute | solution.py:29
  26.6 5.4 %collective-permute-done.6.refs_2_ = bf16[128,768]{1,0:T(8,128)(2,1)S(1)} collective-permute-done((bf16[128,768]{1,0:T(8,128)(2,1)S(1)}, bf16[128,768]{1,0:T(8,128)(2,1)S(1)}, u32[]{:S(2)}, u32[]{:S(2)}) %collective-permute-start.6) | collective-permute-done | bytes 196640 | tf_op jit(solution)/shard_map/ppermute | solution.py:29
  32.6 1.4 %collective-permute-start.14 = (bf16[128,768]{1,0:T(8,128)(2,1)S(1)}, bf16[128,768]{1,0:T(8,128)(2,1)S(1)}, u32[]{:S(2)}, u32[]{:S(2)}) collective-permute-start(bf16[128,768]{1,0:T(8,128)(2,1)S(1)} %collective-permute-done.5.refs_4_), channel_id=1, source_target_pairs={{0,8},{4,12},{8,0},{12,4},{16,24},{20,28},{24,16},{28,20},{1,9},{5... | collective-permute-start | bytes 589832 | tf_op jit(solution)/shard_map/ppermute | solution.py:29
  34.0 2.4 %collective-permute-start.13 = (bf16[128,256]{1,0:T(8,128)(2,1)S(1)}, bf16[128,256]{1,0:T(8,128)(2,1)S(1)}, u32[]{:S(2)}, u32[]{:S(2)}) collective-permute-start(bf16[128,256]{1,0:T(8,128)(2,1)S(1)} %get-tuple-element.26), channel_id=1, source_target_pairs={{0,4},{4,0},{8,12},{12,8},{16,20},{20,16},{24,28},{28,24},{1,5},{5... | collective-permute-start | bytes 196616 | tf_op jit(solution)/shard_map/ppermute | solution.py:29
  36.5 7.8 %shard_map.59.rest_0_ = f32[128,3072]{1,0:T(8,128)S(1)} custom-call(s32[2]{0:T(128)S(1)} %pad_add_fusion.place_ref, bf16[2,32,3072]{2,1,0:T(8,128)(2,1)S(1)} %pad_maximum_fusion.1.own_ref, bf16[2,32,3072]{2,1,0:T(8,128)(2,1)S(1)} %collective-permute-done.4.got_ref, f32[128,3072]{1,0:T(8,128)S(1)} %fusion.3.slope_ref, bf16[3072,3072]{1,0:T(8,128)(2,1)} %up_ref.7, ...), custom_call_target="tpu_custom_call" | custom-call | flops 1207959552 | bytes 9437184 | tf_op jit(solution)/shard_map/pallas_call | solution.py:110
  44.3 7.9 %shard_map.60.rest_0_ = f32[128,3072]{1,0:T(8,128)S(1)} custom-call(s32[2]{0:T(128)S(1)} %pad_add_fusion.place_ref, bf16[2,32,3072]{2,1,0:T(8,128)(2,1)S(1)} %pad_maximum_fusion.1.own_ref, bf16[2,32,3072]{2,1,0:T(8,128)(2,1)S(1)} %collective-permute-done.4.got_ref, f32[128,3072]{1,0:T(8,128)S(1)} %fusion.3.slope_ref, bf16[3072,3072]{1,0:T(8,128)(2,1)} %up_ref.7, ...), custom_call_target="tpu_custom_call" | custom-call | flops 1207959552 | bytes 9437184 | tf_op jit(solution)/shard_map/pallas_call | solution.py:110
  52.3 7.8 %shard_map.61.rest_0_ = f32[128,3072]{1,0:T(8,128)S(1)} custom-call(s32[2]{0:T(128)S(1)} %pad_add_fusion.place_ref, bf16[2,32,3072]{2,1,0:T(8,128)(2,1)S(1)} %pad_maximum_fusion.1.own_ref, bf16[2,32,3072]{2,1,0:T(8,128)(2,1)S(1)} %collective-permute-done.4.got_ref, f32[128,3072]{1,0:T(8,128)S(1)} %fusion.3.slope_ref, bf16[3072,3072]{1,0:T(8,128)(2,1)} %up_ref.7, ...), custom_call_target="tpu_custom_call" | custom-call | flops 1207959552 | bytes 9437184 | tf_op jit(solution)/shard_map/pallas_call | solution.py:110
  60.1 7.8 %shard_map.62 = f32[128,3072]{1,0:T(8,128)S(1)} custom-call(s32[2]{0:T(128)S(1)} %pad_add_fusion.place_ref, bf16[2,32,3072]{2,1,0:T(8,128)(2,1)S(1)} %pad_maximum_fusion.1.own_ref, bf16[2,32,3072]{2,1,0:T(8,128)(2,1)S(1)} %collective-permute-done.4.got_ref, f32[128,3072]{1,0:T(8,128)S(1)} %fusion.3.slope_ref, bf16[3072,3072]{1,0:T(8,128)(2,1)} %up_ref.7, ...), custom_call_target="tpu_custom_call" | custom-call | flops 1207959552 | bytes 9437184 | tf_op jit(solution)/shard_map/pallas_call | solution.py:110
  70.0 2.3 %collective-permute-start.24 = (bf16[256,512]{1,0:T(8,128)(2,1)S(1)}, bf16[256,512]{1,0:T(8,128)(2,1)S(1)}, u32[]{:S(2)}, u32[]{:S(2)}) collective-permute-start(bf16[256,512]{1,0:T(8,128)(2,1)S(1)} %pad_maximum_fusion.3.refs_0_.refs_8_), channel_id=1, source_target_pairs={{0,16},{4,20},{8,24},{12,28},{16,0},{20,4},{24,8},{28,12},{1,17},{... | collective-permute-start | bytes 786440 | tf_op jit(solution)/shard_map/ppermute | solution.py:29
  76.0 12.5 %collective-permute-done.18.refs_7_ = bf16[128,768]{1,0:T(8,128)(2,1)S(1)} collective-permute-done((bf16[128,768]{1,0:T(8,128)(2,1)S(1)}, bf16[128,768]{1,0:T(8,128)(2,1)S(1)}, u32[]{:S(2)}, u32[]{:S(2)}) %collective-permute-start.18) | collective-permute-done | bytes 196640 | tf_op jit(solution)/shard_map/ppermute | solution.py:29
  89.2 1.7 %collective-permute-start.25 = (bf16[256,512]{1,0:T(8,128)(2,1)S(1)}, bf16[256,512]{1,0:T(8,128)(2,1)S(1)}, u32[]{:S(2)}, u32[]{:S(2)}) collective-permute-start(bf16[256,512]{1,0:T(8,128)(2,1)S(1)} %collective-permute-done.24.refs_2_.refs_10_), channel_id=1, source_target_pairs={{0,8},{4,12},{8,0},{12,4},{16,24},{20,28},{24,16},{28,20},{1,9},{5... | collective-permute-start | bytes 786440 | tf_op jit(solution)/shard_map/ppermute | solution.py:29
  91.2 6.1 %collective-permute-done.21.refs_2_.refs_14_ = bf16[256,256]{1,0:T(8,128)(2,1)S(1)} collective-permute-done((bf16[256,256]{1,0:T(8,128)(2,1)S(1)}, bf16[256,256]{1,0:T(8,128)(2,1)S(1)}, u32[]{:S(2)}, u32[]{:S(2)}) %collective-permute-start.21) | collective-permute-done | bytes 131104 | tf_op jit(solution)/shard_map/ppermute | solution.py:29
  98.5 5.5 %collective-permute-done.20.refs_1_.refs_13_ = bf16[256,256]{1,0:T(8,128)(2,1)S(1)} collective-permute-done((bf16[256,256]{1,0:T(8,128)(2,1)S(1)}, bf16[256,256]{1,0:T(8,128)(2,1)S(1)}, u32[]{:S(2)}, u32[]{:S(2)}) %collective-permute-start.20) | collective-permute-done | bytes 131104 | tf_op jit(solution)/shard_map/ppermute | solution.py:29
  103.9 1.5 %collective-permute-done.22.refs_3_.refs_15_ = bf16[256,256]{1,0:T(8,128)(2,1)S(1)} collective-permute-done((bf16[256,256]{1,0:T(8,128)(2,1)S(1)}, bf16[256,256]{1,0:T(8,128)(2,1)S(1)}, u32[]{:S(2)}, u32[]{:S(2)}) %collective-permute-start.22) | collective-permute-done | bytes 131104 | tf_op jit(solution)/shard_map/ppermute | solution.py:29
  106.8 1.4 shard_map.65
  111.6 20.8 %collective-permute-done.27.refs_17_ = bf16[384,512]{1,0:T(8,128)(2,1)S(1)} collective-permute-done((bf16[384,512]{1,0:T(8,128)(2,1)S(1)}, bf16[384,512]{1,0:T(8,128)(2,1)S(1)}, u32[]{:S(2)}, u32[]{:S(2)}) %collective-permute-start.27) | collective-permute-done | bytes 393248 | tf_op jit(solution)/shard_map/ppermute | solution.py:29
  132.5 3.8 %shard_map.67._ = f32[384,3072]{1,0:T(8,128)} custom-call(s32[2]{0:T(128)S(1)} %pad_add_fusion.place_ref, bf16[384,1024]{1,0:T(8,128)(2,1)S(1)} %get-tuple-element.34.grad_ref, bf16[128,768]{1,0:T(8,128)(2,1)S(1)} %get-tuple-element.21.refs_0_, bf16[128,768]{1,0:T(8,128)(2,1)S(1)} %collective-permute-done.10.refs_1_, ...), custom_call_target="tpu_custom_call" | custom-call | flops 1207959552 | bytes 4718592 | tf_op jit(solution)/shard_map/pallas_call | solution.py:208
  (70 shorter events, 21.3 us)
Async XLA Ops:
  1.7 10.9 %collective-permute-start.2 = (bf16[32,768]{1,0:T(8,128)(2,1)S(1)}, bf16[32,768]{1,0:T(8,128)(2,1)S(1)}, u32[]{:S(2)}, u32[]{:S(2)}) collective-permute-start(bf16[32,768]{1,0:T(8,128)(2,1)S(1)} %get-tuple-element.47), channel_id=1, source_target_pairs={{0,24},{4,28},{8,16},{12,20},{16,8},{20,12},{24,0},{28,4},{1,25},{... | collective-permute-start | bytes 147464 | tf_op jit(solution)/shard_map/ppermute | solution.py:29
  8.6 16.1 %collective-permute-start.5 = (bf16[128,768]{1,0:T(8,128)(2,1)S(1)}, bf16[128,768]{1,0:T(8,128)(2,1)S(1)}, u32[]{:S(2)}, u32[]{:S(2)}) collective-permute-start(bf16[128,768]{1,0:T(8,128)(2,1)S(1)} %get-tuple-element.21.refs_0_), channel_id=1, source_target_pairs={{0,16},{4,20},{8,24},{12,28},{16,0},{20,4},{24,8},{28,12},{1,17},{... | collective-permute-start | bytes 589832 | tf_op jit(solution)/shard_map/ppermute | solution.py:29
  11.0 15.2 %collective-permute-start.10 = (bf16[128,768]{1,0:T(8,128)(2,1)S(1)}, bf16[128,768]{1,0:T(8,128)(2,1)S(1)}, u32[]{:S(2)}, u32[]{:S(2)}) collective-permute-start(bf16[128,768]{1,0:T(8,128)(2,1)S(1)} %get-tuple-element.40), channel_id=1, source_target_pairs={{0,4},{4,0},{8,12},{12,8},{16,20},{20,16},{24,28},{28,24},{1,5},{5... | collective-permute-start | bytes 589832 | tf_op jit(solution)/shard_map/ppermute | solution.py:29
  14.8 6.2 %collective-permute-start.7 = (bf16[4,32,768]{2,1,0:T(8,128)(2,1)S(1)}, bf16[4,32,768]{2,1,0:T(8,128)(2,1)S(1)}, u32[]{:S(2)}, u32[]{:S(2)}) collective-permute-start(bf16[4,32,768]{2,1,0:T(8,128)(2,1)S(1)} %pad_maximum_fusion.4), channel_id=1, source_target_pairs={{0,4},{4,0},{8,12},{12,8},{16,20},{20,16},{24,28},{28,24},{1,5},{5... | collective-permute-start | bytes 589832 | tf_op jit(solution)/shard_map/ppermute | solution.py:29
  18.4 15.6 %collective-permute-start.4 = (bf16[2,32,3072]{2,1,0:T(8,128)(2,1)S(1)}, bf16[2,32,3072]{2,1,0:T(8,128)(2,1)S(1)}, u32[]{:S(2)}, u32[]{:S(2)}) collective-permute-start(bf16[2,32,3072]{2,1,0:T(8,128)(2,1)S(1)} %pad_maximum_fusion.1.own_ref), channel_id=1, source_target_pairs={{0,1},{1,0},{2,3},{3,2},{4,5},{5,4},{6,7},{7,6},{8,9},{9,8},{10,11... | collective-permute-start | bytes 1179656 | tf_op jit(solution)/shard_map/ppermute | solution.py:29
  21.1 23.2 %collective-permute-start.8 = (bf16[2,4,32,768]{3,2,1,0:T(8,128)(2,1)S(1)}, bf16[2,4,32,768]{3,2,1,0:T(8,128)(2,1)S(1)}, u32[]{:S(2)}, u32[]{:S(2)}) collective-permute-start(bf16[2,4,32,768]{3,2,1,0:T(8,128)(2,1)S(1)} %get-tuple-element.43), channel_id=1, source_target_pairs={{0,2},{1,3},{2,0},{3,1},{4,6},{5,7},{6,4},{7,5},{8,10},{9,11},{10,... | collective-permute-start | bytes 1179656 | tf_op jit(solution)/shard_map/ppermute | solution.py:29
  22.8 9.2 %collective-permute-start.6 = (bf16[128,768]{1,0:T(8,128)(2,1)S(1)}, bf16[128,768]{1,0:T(8,128)(2,1)S(1)}, u32[]{:S(2)}, u32[]{:S(2)}) collective-permute-start(bf16[128,768]{1,0:T(8,128)(2,1)S(1)} %get-tuple-element.21.refs_0_), channel_id=1, source_target_pairs={{0,8},{4,12},{8,0},{12,4},{16,24},{20,28},{24,16},{28,20},{1,9},{5... | collective-permute-start | bytes 589832 | tf_op jit(solution)/shard_map/ppermute | solution.py:29
  24.7 7.8 %collective-permute-start.9 = (bf16[128,512]{1,0:T(8,128)(2,1)S(1)}, bf16[128,512]{1,0:T(8,128)(2,1)S(1)}, u32[]{:S(2)}, u32[]{:S(2)}) collective-permute-start(bf16[128,512]{1,0:T(8,128)(2,1)S(1)} %get-tuple-element.24), channel_id=1, source_target_pairs={{0,4},{4,0},{8,12},{12,8},{16,20},{20,16},{24,28},{28,24},{1,5},{5... | collective-permute-start | bytes 393224 | tf_op jit(solution)/shard_map/ppermute | solution.py:29
  26.2 26.1 %collective-permute-start.11 = (bf16[128,768]{1,0:T(8,128)(2,1)S(1)}, bf16[128,768]{1,0:T(8,128)(2,1)S(1)}, u32[]{:S(2)}, u32[]{:S(2)}) collective-permute-start(bf16[128,768]{1,0:T(8,128)(2,1)S(1)} %collective-permute-done.10.refs_1_), channel_id=1, source_target_pairs={{0,16},{4,20},{8,24},{12,28},{16,0},{20,4},{24,8},{28,12},{1,17},{... | collective-permute-start | bytes 589832 | tf_op jit(solution)/shard_map/ppermute | solution.py:29
  32.0 20.3 %collective-permute-start.12 = (bf16[128,768]{1,0:T(8,128)(2,1)S(1)}, bf16[128,768]{1,0:T(8,128)(2,1)S(1)}, u32[]{:S(2)}, u32[]{:S(2)}) collective-permute-start(bf16[128,768]{1,0:T(8,128)(2,1)S(1)} %collective-permute-done.10.refs_1_), channel_id=1, source_target_pairs={{0,8},{4,12},{8,0},{12,4},{16,24},{20,28},{24,16},{28,20},{1,9},{5... | collective-permute-start | bytes 589832 | tf_op jit(solution)/shard_map/ppermute | solution.py:29
  32.6 27.5 %collective-permute-start.14 = (bf16[128,768]{1,0:T(8,128)(2,1)S(1)}, bf16[128,768]{1,0:T(8,128)(2,1)S(1)}, u32[]{:S(2)}, u32[]{:S(2)}) collective-permute-start(bf16[128,768]{1,0:T(8,128)(2,1)S(1)} %collective-permute-done.5.refs_4_), channel_id=1, source_target_pairs={{0,8},{4,12},{8,0},{12,4},{16,24},{20,28},{24,16},{28,20},{1,9},{5... | collective-permute-start | bytes 589832 | tf_op jit(solution)/shard_map/ppermute | solution.py:29
  34.0 18.2 %collective-permute-start.13 = (bf16[128,256]{1,0:T(8,128)(2,1)S(1)}, bf16[128,256]{1,0:T(8,128)(2,1)S(1)}, u32[]{:S(2)}, u32[]{:S(2)}) collective-permute-start(bf16[128,256]{1,0:T(8,128)(2,1)S(1)} %get-tuple-element.26), channel_id=1, source_target_pairs={{0,4},{4,0},{8,12},{12,8},{16,20},{20,16},{24,28},{28,24},{1,5},{5... | collective-permute-start | bytes 196616 | tf_op jit(solution)/shard_map/ppermute | solution.py:29
  69.9 21.0 %collective-permute-start.19 = (bf16[256,512]{1,0:T(8,128)(2,1)S(1)}, bf16[256,512]{1,0:T(8,128)(2,1)S(1)}, u32[]{:S(2)}, u32[]{:S(2)}) collective-permute-start(bf16[256,512]{1,0:T(8,128)(2,1)S(1)} %pad_maximum_fusion.3.refs_0_.refs_8_), channel_id=1, source_target_pairs={{0,8},{4,12},{8,0},{12,4},{16,24},{20,28},{24,16},{28,20},{1,9},{5... | collective-permute-start | bytes 786440 | tf_op jit(solution)/shard_map/ppermute | solution.py:29
  70.0 19.2 %collective-permute-start.24 = (bf16[256,512]{1,0:T(8,128)(2,1)S(1)}, bf16[256,512]{1,0:T(8,128)(2,1)S(1)}, u32[]{:S(2)}, u32[]{:S(2)}) collective-permute-start(bf16[256,512]{1,0:T(8,128)(2,1)S(1)} %pad_maximum_fusion.3.refs_0_.refs_8_), channel_id=1, source_target_pairs={{0,16},{4,20},{8,24},{12,28},{16,0},{20,4},{24,8},{28,12},{1,17},{... | collective-permute-start | bytes 786440 | tf_op jit(solution)/shard_map/ppermute | solution.py:29
  72.3 16.2 %collective-permute-start.18 = (bf16[128,768]{1,0:T(8,128)(2,1)S(1)}, bf16[128,768]{1,0:T(8,128)(2,1)S(1)}, u32[]{:S(2)}, u32[]{:S(2)}) collective-permute-start(bf16[128,768]{1,0:T(8,128)(2,1)S(1)} %collective-permute-done.11.refs_5_), channel_id=1, source_target_pairs={{0,8},{4,12},{8,0},{12,4},{16,24},{20,28},{24,16},{28,20},{1,9},{5... | collective-permute-start | bytes 589832 | tf_op jit(solution)/shard_map/ppermute | solution.py:29
  73.5 23.9 %collective-permute-start.17 = (bf16[2,2,4,32,768]{4,3,2,1,0:T(8,128)(2,1)S(1)}, bf16[2,2,4,32,768]{4,3,2,1,0:T(8,128)(2,1)S(1)}, u32[]{:S(2)}, u32[]{:S(2)}) collective-permute-start(bf16[2,2,4,32,768]{4,3,2,1,0:T(8,128)(2,1)S(1)} %pad_maximum_fusion.own_ref), channel_id=1, source_target_pairs={{0,1},{1,0},{2,3},{3,2},{4,5},{5,4},{6,7},{7,6},{8,9},{9,8},{10,11... | collective-permute-start | bytes 2359304 | tf_op jit(solution)/shard_map/ppermute | solution.py:29
  74.9 36.0 %collective-permute-start.16 = (f32[32,3072]{1,0:T(8,128)S(1)}, f32[32,3072]{1,0:T(8,128)S(1)}, u32[]{:S(2)}, u32[]{:S(2)}) collective-permute-start(f32[32,3072]{1,0:T(8,128)S(1)} %select_bitcast_fusion.1), channel_id=1, source_target_pairs={{0,2},{1,3},{2,0},{3,1},{4,6},{5,7},{6,4},{7,5},{8,10},{9,11},{10,... | collective-permute-start | bytes 1179656 | tf_op jit(solution)/shard_map/ppermute | solution.py:29
  88.5 8.8 %collective-permute-start.21 = (bf16[256,256]{1,0:T(8,128)(2,1)S(1)}, bf16[256,256]{1,0:T(8,128)(2,1)S(1)}, u32[]{:S(2)}, u32[]{:S(2)}) collective-permute-start(bf16[256,256]{1,0:T(8,128)(2,1)S(1)} %pad_maximum_fusion.5.refs_0_.refs_12_), channel_id=1, source_target_pairs={{0,16},{4,20},{8,24},{12,28},{16,0},{20,4},{24,8},{28,12},{1,17},{... | collective-permute-start | bytes 393224 | tf_op jit(solution)/shard_map/ppermute | solution.py:29
  89.2 20.1 %collective-permute-start.25 = (bf16[256,512]{1,0:T(8,128)(2,1)S(1)}, bf16[256,512]{1,0:T(8,128)(2,1)S(1)}, u32[]{:S(2)}, u32[]{:S(2)}) collective-permute-start(bf16[256,512]{1,0:T(8,128)(2,1)S(1)} %collective-permute-done.24.refs_2_.refs_10_), channel_id=1, source_target_pairs={{0,8},{4,12},{8,0},{12,4},{16,24},{20,28},{24,16},{28,20},{1,9},{5... | collective-permute-start | bytes 786440 | tf_op jit(solution)/shard_map/ppermute | solution.py:29
  90.9 13.1 %collective-permute-start.20 = (bf16[256,256]{1,0:T(8,128)(2,1)S(1)}, bf16[256,256]{1,0:T(8,128)(2,1)S(1)}, u32[]{:S(2)}, u32[]{:S(2)}) collective-permute-start(bf16[256,256]{1,0:T(8,128)(2,1)S(1)} %pad_maximum_fusion.5.refs_0_.refs_12_), channel_id=1, source_target_pairs={{0,8},{4,12},{8,0},{12,4},{16,24},{20,28},{24,16},{28,20},{1,9},{5... | collective-permute-start | bytes 393224 | tf_op jit(solution)/shard_map/ppermute | solution.py:29
  97.3 8.1 %collective-permute-start.22 = (bf16[256,256]{1,0:T(8,128)(2,1)S(1)}, bf16[256,256]{1,0:T(8,128)(2,1)S(1)}, u32[]{:S(2)}, u32[]{:S(2)}) collective-permute-start(bf16[256,256]{1,0:T(8,128)(2,1)S(1)} %collective-permute-done.21.refs_2_.refs_14_), channel_id=1, source_target_pairs={{0,8},{4,12},{8,0},{12,4},{16,24},{20,28},{24,16},{28,20},{1,9},{5... | collective-permute-start | bytes 393224 | tf_op jit(solution)/shard_map/ppermute | solution.py:29
  105.8 30.5 %collective-permute-start.23 = (bf16[384,256]{1,0:T(8,128)(2,1)S(1)}, bf16[384,256]{1,0:T(8,128)(2,1)S(1)}, u32[]{:S(2)}, u32[]{:S(2)}) collective-permute-start(bf16[384,256]{1,0:T(8,128)(2,1)S(1)} %shard_map.64), channel_id=1, source_target_pairs={{0,4},{4,0},{8,12},{12,8},{16,20},{20,16},{24,28},{28,24},{1,5},{5... | collective-permute-start | bytes 589832 | tf_op jit(solution)/shard_map/ppermute | solution.py:29
  108.1 24.3 %collective-permute-start.26 = (bf16[384,768]{1,0:T(8,128)(2,1)S(1)}, bf16[384,768]{1,0:T(8,128)(2,1)S(1)}, u32[]{:S(2)}, u32[]{:S(2)}) collective-permute-start(bf16[384,768]{1,0:T(8,128)(2,1)S(1)} %shard_map.65), channel_id=1, source_target_pairs={{0,4},{4,0},{8,12},{12,8},{16,20},{20,16},{24,28},{28,24},{1,5},{5... | collective-permute-start | bytes 1769480 | tf_op jit(solution)/shard_map/ppermute | solution.py:29
  109.9 22.6 %collective-permute-start.27 = (bf16[384,512]{1,0:T(8,128)(2,1)S(1)}, bf16[384,512]{1,0:T(8,128)(2,1)S(1)}, u32[]{:S(2)}, u32[]{:S(2)}) collective-permute-start(bf16[384,512]{1,0:T(8,128)(2,1)S(1)} %shard_map.66), channel_id=1, source_target_pairs={{0,4},{4,0},{8,12},{12,8},{16,20},{20,16},{24,28},{28,24},{1,5},{5... | collective-permute-start | bytes 1179656 | tf_op jit(solution)/shard_map/ppermute | solution.py:29
  (10 other events, 77.4 us)

commit v3 on v2

v3 whole, which is shorter than its diff:
```python
import math

import jax
import jax.numpy as jnp
from jax import lax
from jax.experimental import pallas as pl
from jax.experimental.pallas import tpu as pltpu
from jax.sharding import PartitionSpec as P

BF16 = jnp.bfloat16
F32 = jnp.float32


def gelu_value_of(pre):
    pre_float = pre.astype(F32)
    normal_cdf = 0.5 * (1.0 + jax.scipy.special.erf(pre_float / math.sqrt(2.0)))
    return (pre_float * normal_cdf).astype(BF16)


def gelu_slope_of(pre):
    pre_float = pre.astype(F32)
    normal_cdf = 0.5 * (1.0 + jax.scipy.special.erf(pre_float / math.sqrt(2.0)))
    density = jnp.exp(-0.5 * pre_float * pre_float) / math.sqrt(2.0 * math.pi)
    return normal_cdf + pre_float * density


def xor_permute(value, axis, mask):
    count = lax.axis_size(axis)
    return lax.ppermute(value, axis, [(i, i ^ mask) for i in range(count)])


def either(bit, low, high):
    return jnp.where(bit == 0, low, high)


def gathered_plan(pre_act, out_grad, w_up, w_down):
    act = gelu_value_of(pre_act)
    gathered = lax.all_gather(out_grad, "tensor", axis=0, tiled=True)
    hidden_grad = lax.dot_general(gathered, w_down, (((1,), (1,)), ((), ())), preferred_element_type=F32)
    pre_grad = (hidden_grad * gelu_slope_of(pre_act)).astype(BF16)
    all_tokens = gathered.shape[0] * lax.axis_size("dp")
    my_columns = lax.all_to_all(gathered, "dp", split_axis=1, concat_axis=0, tiled=True)
    summed = lax.dot_general(
        my_columns,
        lax.all_gather(act, "dp", axis=0, tiled=True),
        (((0,), (0,)), ((), ())),
        preferred_element_type=F32,
    )
    in_grad = lax.psum_scatter(
        lax.dot_general(pre_grad, w_up, (((1,), (1,)), ((), ())), preferred_element_type=F32),
        "tensor",
        scatter_dimension=0,
        tiled=True,
    ).astype(BF16)
    return (in_grad, summed / math.sqrt(all_tokens))


VMEM_LIMIT = 16 * 1024 * 1024


def params():
    return pltpu.CompilerParams(vmem_limit_bytes=VMEM_LIMIT)


def cost(flops, moved):
    return pl.CostEstimate(flops=flops, bytes_accessed=moved, transcendentals=0)


def whole():
    return pl.BlockSpec(memory_space=pltpu.VMEM)


def prepare(place, own, got):
    _, _, depth, rows, pair = own.shape
    block = pair // 2
    tokens = 2 * depth * 4 * rows

    def body(place_ref, own_ref, got_ref, mine_ref, theirs_ref, held_ref):
        x, shard = place_ref[0], place_ref[1]
        for k in range(depth):
            for j in range(2):
                for i in range(2):
                    for ref, bit in ((own_ref, 0), (got_ref, 1)):
                        at = (2 * k + j) * 4 * rows + ((2 * i + bit) ^ shard) * rows
                        held_ref[pl.ds(pl.multiple_of(at, rows), rows), :] = ref[i, j, k]
        for out, bit in ((mine_ref, x), (theirs_ref, 1 - x)):
            columns = pl.ds(pl.multiple_of(bit * block, 128), block)
            out[...] = held_ref[:, columns].T

    shape = jax.ShapeDtypeStruct((block, tokens), BF16)
    return pl.pallas_call(
        body,
        in_specs=[pl.BlockSpec(memory_space=pltpu.SMEM), whole(), whole()],
        out_specs=[whole(), whole()],
        out_shape=[shape, shape],
        scratch_shapes=[pltpu.VMEM((tokens, pair), BF16)],
        compiler_params=params(),
        cost_estimate=cost(0, 8 * tokens * pair),
    )(place, own, got)


def contract(grad_ref, refs, scale):
    total, at = None, 0
    for ref in refs:
        depth = ref.shape[0]
        part = jnp.dot(grad_ref[:, at : at + depth], ref[...], preferred_element_type=F32)
        total = part if total is None else total + part
        at += depth
    return total * scale


def their_product(theirs, shared, last, chunk, scale):
    def body(grad_ref, *refs):
        refs[-1][...] = contract(grad_ref, refs[:-1], scale).astype(BF16)

    block, tokens = theirs.shape
    offset, size = chunk
    specs = [pl.BlockSpec(p.shape[:1] + (size,), lambda i: (0, offset // size)) for p in shared]
    return pl.pallas_call(
        body,
        grid=(1,),
        in_specs=[pl.BlockSpec(theirs.shape, lambda i: (0, 0))]
        + specs
        + [pl.BlockSpec(last.shape, lambda i: (0, 0))],
        out_specs=pl.BlockSpec((block, size), lambda i: (0, 0)),
        out_shape=jax.ShapeDtypeStruct((block, size), BF16),
        compiler_params=params(),
        cost_estimate=cost(2 * block * tokens * size, 4 * tokens * size),
    )(theirs, *shared, last)


def my_product(place, mine, shared, lasts, chunks, backs, width, scale):
    block, tokens = mine.shape
    half = width // 2
    count = len(chunks)

    def body(place_ref, grad_ref, *refs):
        shared_refs, refs = refs[: len(shared)], refs[len(shared) :]
        last_refs, returned = refs[:count], refs[count : count + len(backs)]
        out_ref, held_ref, sems = refs[count + len(backs) :]
        copies = []

        def store(slot, offset, size, side, value):
            here = held_ref.at[:, pl.ds(side * half + offset, size)]
            here[...] = value
            bit = place_ref[0] if side == 0 else 1 - place_ref[0]
            to = pl.ds(pl.multiple_of(bit * half + offset, 128), size)
            copies.append(pltpu.make_async_copy(here, out_ref.at[:, to], sems.at[slot]))
            copies[-1].start()

        for slot, (ref, (offset, size)) in enumerate(zip(returned, chunks)):
            store(slot, offset, size, 1, ref[...].astype(F32))
        for slot, (ref, (offset, size)) in enumerate(zip(last_refs, chunks)):
            pieces = [r.at[:, pl.ds(offset, size)] for r in shared_refs] + [ref]
            store(len(backs) + slot, offset, size, 0, contract(grad_ref, pieces, scale))
        for copy in copies:
            copy.wait()

    return pl.pallas_call(
        body,
        in_specs=[pl.BlockSpec(memory_space=pltpu.SMEM)] + [whole()] * (1 + len(shared) + count + len(backs)),
        out_specs=pl.BlockSpec(memory_space=pl.ANY),
        out_shape=jax.ShapeDtypeStruct((block, width), F32),
        scratch_shapes=[pltpu.VMEM((block, width), F32), pltpu.SemaphoreType.DMA((len(backs) + count,))],
        compiler_params=params(),
        cost_estimate=cost(2 * block * tokens * half, 4 * block * width),
    )(place, mine, *shared, *lasts, *backs)


def place_back(place, result, back, offset):
    block, width = result.shape
    size = back.shape[1]

    def body(place_ref, back_ref, _, out_ref, held_ref, sem):
        held_ref[...] = back_ref[...].astype(F32)
        to = pl.ds(pl.multiple_of((1 - place_ref[0]) * (width // 2) + offset, 128), size)
        copy = pltpu.make_async_copy(held_ref, out_ref.at[:, to], sem)
        copy.start()
        copy.wait()

    return pl.pallas_call(
        body,
        in_specs=[pl.BlockSpec(memory_space=pltpu.SMEM), whole(), pl.BlockSpec(memory_space=pl.ANY)],
        out_specs=pl.BlockSpec(memory_space=pl.ANY),
        out_shape=jax.ShapeDtypeStruct(result.shape, F32),
        input_output_aliases={2: 0},
        scratch_shapes=[pltpu.VMEM((block, size), F32), pltpu.SemaphoreType.DMA],
        compiler_params=params(),
        cost_estimate=cost(0, 4 * block * size),
    )(place, back, result)


def after(value, *others):
    return lax.optimization_barrier((value, *others))[0]


def plane_plan(pre_act, out_grad, w_up, w_down):
    at, shard = lax.axis_index("dp"), lax.axis_index("tensor")
    z, x = at // 2, at % 2
    y, core = shard // 2, shard % 2
    place = jnp.stack([x, shard]).astype(jnp.int32)
    rows, width = out_grad.shape
    tokens, units = pre_act.shape
    half = units // 2
    pair = width // 4
    scale = 1.0 / math.sqrt(tokens * 8)
    chunks = tuple((i * half // 3, half // 3) for i in range(3))

    def columns(pre, bit):
        return gelu_value_of(either(bit, pre[:, :half], pre[:, half:]))

    def slab(k):
        return lax.dynamic_slice(out_grad, (0, (z ^ k) * pair), (rows, pair))

    grad = jnp.stack([slab(0)] + [xor_permute(slab(k), "dp", 2 * k) for k in (1, 2, 3)])

    kept, sent = columns(pre_act, x), columns(pre_act, 1 - x)
    grad = after(grad, kept, sent)
    far_own = xor_permute(kept, "dp", 4)
    near_own = xor_permute(kept, "dp", 2)
    grad_x = xor_permute(grad, "dp", 1)
    got = xor_permute(after(sent, grad), "dp", 1)
    far_got = xor_permute(got, "dp", 4)
    near_got = xor_permute(got, "dp", 2)

    both_x = jnp.stack([grad, grad_x])
    grad_y = xor_permute(both_x, "tensor", 2)

    other = xor_permute(out_grad, "tensor", 2)
    rows_y = jnp.stack([either(y, out_grad, other), either(y, other, out_grad)])
    other = xor_permute(rows_y, "tensor", 1)
    group = jnp.stack([either(core, rows_y, other), either(core, other, rows_y)], axis=1).reshape(tokens, width)
    group = after(group, got, grad_x)
    hidden_grad = lax.dot_general(group, w_down, (((1,), (1,)), ((), ())), preferred_element_type=F32)
    pre_grad = (hidden_grad * gelu_slope_of(pre_act)).astype(BF16)
    partial = lax.dot_general(pre_grad, w_up, (((1,), (1,)), ((), ())), preferred_element_type=F32)

    far_own, far_got, near_own, near_got, grad_y = lax.optimization_barrier(
        (far_own, far_got, near_own, near_got, grad_y, partial)
    )[:5]
    both_y = jnp.stack([both_x, grad_y])
    grad_core = xor_permute(both_y, "tensor", 1)
    lasts = []
    for offset, size in chunks:
        far = jnp.concatenate([far_own[:, offset : offset + size], far_got[:, offset : offset + size]])
        lasts.append(xor_permute(far, "dp", 2))
    mine, theirs = prepare(place, both_y, grad_core)
    shared = [kept, got, near_own, near_got, far_own, far_got]
    backs = [xor_permute(their_product(theirs, shared, f, c, scale), "dp", 1) for f, c in zip(lasts, chunks)]

    partial = after(partial, grad_core).reshape(2, 2, rows, width)
    keep = either(core, partial[:, 0], partial[:, 1])
    give = either(core, partial[:, 1], partial[:, 0])
    keep = keep + xor_permute(give, "tensor", 1)
    in_grad = either(y, keep[0], keep[1]) + xor_permute(either(y, keep[1], keep[0]), "tensor", 2)

    result = my_product(place, mine, shared, lasts, chunks, backs[:-1], units, scale)
    result = place_back(place, result, backs[-1], chunks[-1][0])
    return (in_grad.astype(BF16), result)


def solution(mesh):
    plan = plane_plan if (mesh.shape["dp"], mesh.shape["tensor"]) == (8, 4) else gathered_plan
    placed = (P("dp", "tensor"), P(("dp", "tensor"), None), P(None, "tensor"), P("tensor", None))
    return jax.shard_map(
        plan,
        mesh=mesh,
        in_specs=placed,
        out_specs=(P(("dp", "tensor"), None), P("dp", "tensor")),
        check_vma=False,
    )
```

time: 138 us -> 101 us (0.73)
  Pallas kernels: 39.9 us -> 9 us
  matrix products: 0 us -> 19.2 us
  waiting for transfers between devices: 56.9 us -> 41.5 us
  starting transfers between devices: 31.6 us -> 23.4 us
  other arithmetic: 7.24 us -> 5.75 us
    pallas_call x7 -> x3, Pallas kernels: 33.7 us -> 2.57 us  [their_product(): pl.pallas_call(body, grid=(1,), in_specs=[pl.BlockSpec(theirs.shape, lamb...]
    dot_general x0 -> x1, matrix products: none -> 19.2 us  [plane_plan(): lax.dot_general(pre_grad, w_up, (((1,), (1,)), ((), ())), preferred_eleme...]
    ppermute x28 -> x21, waiting for transfers between devices: 56.9 us -> 41.5 us  [xor_permute(): return lax.ppermute(value, axis, [(i, i ^ mask) for i in range(count)])]
    ppermute x28 -> x21, starting transfers between devices: 31.6 us -> 23.4 us  [xor_permute(): return lax.ppermute(value, axis, [(i, i ^ mask) for i in range(count)])]
  transfers between devices with their start and end apart: 28 -> 21, of which waited for: 8 -> 11; matrix products, arithmetic and copies ran while one was open for 5% -> 24% of each run, Pallas kernels for 22% -> 9%
where the time goes in v3:
time: 101 us
  waiting for transfers between devices  41.5 us (41%)
  starting transfers between devices  23.4 us (23%)
  matrix products  19.2 us (19%)
  Pallas kernels  9 us (9%)
  other arithmetic  5.75 us (6%)
    ppermute x21, waiting for transfers between devices, xor_permute(): return lax.ppermute(value, axis, [(i, i ^ mask) for i in range(count)])  41.5 us
    ppermute x21, starting transfers between devices, xor_permute(): return lax.ppermute(value, axis, [(i, i ^ mask) for i in range(count)])  23.4 us
    dot_general x1, matrix products, plane_plan(): lax.dot_general(pre_grad, w_up, (((1,), (1,)), ((), ())), preferred_eleme...  19.2 us
    pallas_call x1, Pallas kernels, my_product(): pl.pallas_call(body, in_specs=[pl.BlockSpec(memory_space=pltpu.SMEM)] + [...  3.82 us
    pallas_call x3, Pallas kernels, their_product(): pl.pallas_call(body, grid=(1,), in_specs=[pl.BlockSpec(theirs.shape, lamb...  2.57 us
  transfers between devices with their start and end apart: 21, of which 11 were waited for; matrix products, arithmetic and copies ran while one was open for 24% of the time, Pallas kernels for 9%

profile of v3, /device:TPU:0, one launch (start us, length us, event | category | flops | bytes accessed | tf_op | source)
XLA Modules:
  0.0 100.6 jit_solution(7403744679515610377)
XLA Ops:
  0.6 3.0 %collective-permute-start = (bf16[32,3072]{1,0:T(8,128)(2,1)}, bf16[32,3072]{1,0:T(8,128)(2,1)S(1)}, u32[]{:S(2)}, u32[]{:S(2)}) collective-permute-start(bf16[32,3072]{1,0:T(8,128)(2,1)} %param.5), channel_id=1, source_target_pairs={{0,2},{1,3},{2,0},{3,1},{4,6},{5,7},{6,4},{7,5},{8,10},{9,11},{10,... | collective-permute-start | bytes 589832 | tf_op jit(solution)/shard_map/ppermute | solution.py:29
  4.6 3.7 %collective-permute-start.4 = (bf16[32,768]{1,0:T(8,128)(2,1)S(1)}, bf16[32,768]{1,0:T(8,128)(2,1)S(1)}, u32[]{:S(2)}, u32[]{:S(2)}) collective-permute-start(bf16[32,768]{1,0:T(8,128)(2,1)S(1)} %get-tuple-element.40), channel_id=1, source_target_pairs={{0,24},{4,28},{8,16},{12,20},{16,8},{20,12},{24,0},{28,4},{1,25},{... | collective-permute-start | bytes 147464 | tf_op jit(solution)/shard_map/ppermute | solution.py:29
  9.0 1.5 %fusion.14 = (bf16[128,1536]{1,0:T(8,128)(2,1)S(1)}, bf16[128,1536]{1,0:T(8,128)(2,1)S(1)}) fusion(pred[]{:T(512)S(6)} %eq.24, bf16[128,3072]{1,0:T(8,128)(2,1)} %param.4, pred[]{:T(512)S(6)} %eq.23), kind=kLoop, calls=%fused_computation.23 | loop fusion | flops 2752512 | bytes 1572866 | tf_op jit(solution)/shard_map/convert_element_type | solution.py:17
  11.0 2.2 %collective-permute-done.3 = bf16[32,768]{1,0:T(8,128)(2,1)S(1)} collective-permute-done((bf16[32,768]{1,0:T(8,128)(2,1)S(1)}, bf16[32,768]{1,0:T(8,128)(2,1)S(1)}, u32[]{:S(2)}, u32[]{:S(2)}) %collective-permute-start.3) | collective-permute-done | bytes 49184 | tf_op jit(solution)/shard_map/ppermute | solution.py:29
  13.3 1.6 %collective-permute-start.5 = (bf16[128,1536]{1,0:T(8,128)(2,1)S(1)}, bf16[128,1536]{1,0:T(8,128)(2,1)S(1)}, u32[]{:S(2)}, u32[]{:S(2)}) collective-permute-start(bf16[128,1536]{1,0:T(8,128)(2,1)S(1)} %get-tuple-element.14), channel_id=1, source_target_pairs={{0,4},{4,0},{8,12},{12,8},{16,20},{20,16},{24,28},{28,24},{1,5},{5... | collective-permute-start | bytes 1179656 | tf_op jit(solution)/shard_map/ppermute | solution.py:29
  15.6 2.0 %collective-permute-start.7 = (bf16[128,1536]{1,0:T(8,128)(2,1)S(1)}, bf16[128,1536]{1,0:T(8,128)(2,1)S(1)}, u32[]{:S(2)}, u32[]{:S(2)}) collective-permute-start(bf16[128,1536]{1,0:T(8,128)(2,1)S(1)} %get-tuple-element.24.refs_0_), channel_id=1, source_target_pairs={{0,16},{4,20},{8,24},{12,28},{16,0},{20,4},{24,8},{28,12},{1,17},{... | collective-permute-start | bytes 1179656 | tf_op jit(solution)/shard_map/ppermute | solution.py:29
  18.0 8.8 %collective-permute-done.6 = bf16[4,32,768]{2,1,0:T(8,128)(2,1)S(1)} collective-permute-done((bf16[4,32,768]{2,1,0:T(8,128)(2,1)S(1)}, bf16[4,32,768]{2,1,0:T(8,128)(2,1)S(1)}, u32[]{:S(2)}, u32[]{:S(2)}) %collective-permute-start.6) | collective-permute-done | bytes 196640 | tf_op jit(solution)/shard_map/ppermute | solution.py:29
  28.0 1.8 %collective-permute-start.8 = (bf16[128,1536]{1,0:T(8,128)(2,1)S(1)}, bf16[128,1536]{1,0:T(8,128)(2,1)S(1)}, u32[]{:S(2)}, u32[]{:S(2)}) collective-permute-start(bf16[128,1536]{1,0:T(8,128)(2,1)S(1)} %collective-permute-done.5.refs_1_), channel_id=1, source_target_pairs={{0,16},{4,20},{8,24},{12,28},{16,0},{20,4},{24,8},{28,12},{1,17},{... | collective-permute-start | bytes 1179656 | tf_op jit(solution)/shard_map/ppermute | solution.py:29
  31.8 19.2 %fusion.15 = f32[128,3072]{1,0:T(8,128)} fusion(bf16[3072,3072]{1,0:T(8,128)(2,1)} %param.6, bf16[128,3072]{1,0:T(8,128)(2,1)S(1)} %bitcast.51, bf16[3072,3072]{1,0:T(8,128)(2,1)} %param.7, bf16[128,3072]{1,0:T(8,128)(2,1)} %param.4), kind=kOutput, calls=%fused_computation.30 | convolution fusion | flops 4836163584 | bytes 40894464 | tf_op jit(solution)/shard_map/dot_general | solution.py:236
  51.0 1.9 %collective-permute-done.8.refs_5_ = bf16[128,1536]{1,0:T(8,128)(2,1)S(1)} collective-permute-done((bf16[128,1536]{1,0:T(8,128)(2,1)S(1)}, bf16[128,1536]{1,0:T(8,128)(2,1)S(1)}, u32[]{:S(2)}, u32[]{:S(2)}) %collective-permute-start.8) | collective-permute-done | bytes 393248 | tf_op jit(solution)/shard_map/ppermute | solution.py:29
  53.7 1.1 %pad_maximum_fusion.1.own_ref = bf16[2,2,4,32,768]{4,3,2,1,0:T(8,128)(2,1)S(1)} fusion(bf16[1,2,4,32,768]{4,3,2,1,0:T(8,128)(2,1)} %bitcast.13, bf16[1,2,4,32,768]{4,3,2,1,0:T(8,128)(2,1)S(1)} %get-tuple-element.34), kind=kLoop, calls=%fused_computation.27 | loop fusion | flops 393216 | bytes 1572864 | tf_op jit(solution)/shard_map/stack | solution.py:241
  54.9 2.3 %collective-permute-done.12.got_ref = bf16[2,2,4,32,768]{4,3,2,1,0:T(8,128)(2,1)S(1)} collective-permute-done((bf16[2,2,4,32,768]{4,3,2,1,0:T(8,128)(2,1)S(1)}, bf16[2,2,4,32,768]{4,3,2,1,0:T(8,128)(2,1)S(1)}, u32[]{:S(2)}, u32[]{:S(2)}) %collective-permute-start.12) | collective-permute-done | bytes 786464 | tf_op jit(solution)/shard_map/ppermute | solution.py:29
  58.1 1.6 %collective-permute-start.17 = (bf16[256,512]{1,0:T(8,128)(2,1)S(1)}, bf16[256,512]{1,0:T(8,128)(2,1)S(1)}, u32[]{:S(2)}, u32[]{:S(2)}) collective-permute-start(bf16[256,512]{1,0:T(8,128)(2,1)S(1)} %pad_maximum_fusion.5), channel_id=1, source_target_pairs={{0,8},{4,12},{8,0},{12,4},{16,24},{20,28},{24,16},{28,20},{1,9},{5... | collective-permute-start | bytes 786440 | tf_op jit(solution)/shard_map/ppermute | solution.py:29
  60.3 1.1 %shard_map.59 = (bf16[384,1024]{1,0:T(8,128)(2,1)S(1)}, bf16[384,1024]{1,0:T(8,128)(2,1)S(1)}) custom-call(s32[2]{0:T(128)S(1)} %pad_add_fusion.place_ref, bf16[2,2,4,32,768]{4,3,2,1,0:T(8,128)(2,1)S(1)} %pad_maximum_fusion.1.own_ref, bf16[2,2,4,32,768]{4,3,2,1,0:T(8,128)(2,1)S(1)} %collective-permute-done.12.got_ref), custom_call_target="tpu_custom_call" | custom-call | bytes 6291456 | tf_op jit(solution)/shard_map/pallas_call | solution.py:91
  61.5 5.3 %collective-permute-done.15.refs_6_.refs_8_ = bf16[256,512]{1,0:T(8,128)(2,1)S(1)} collective-permute-done((bf16[256,512]{1,0:T(8,128)(2,1)S(1)}, bf16[256,512]{1,0:T(8,128)(2,1)S(1)}, u32[]{:S(2)}, u32[]{:S(2)}) %collective-permute-start.15) | collective-permute-done | bytes 262176 | tf_op jit(solution)/shard_map/ppermute | solution.py:29
  67.6 1.6 %collective-permute-start.16 = (bf16[384,512]{1,0:T(8,128)(2,1)S(1)}, bf16[384,512]{1,0:T(8,128)(2,1)S(1)}, u32[]{:S(2)}, u32[]{:S(2)}) collective-permute-start(bf16[384,512]{1,0:T(8,128)(2,1)S(1)} %shard_map.60), channel_id=1, source_target_pairs={{0,4},{4,0},{8,12},{12,8},{16,20},{20,16},{24,28},{28,24},{1,5},{5... | collective-permute-start | bytes 1179656 | tf_op jit(solution)/shard_map/ppermute | solution.py:29
  69.1 3.2 %collective-permute-done.17.refs_6_ = bf16[256,512]{1,0:T(8,128)(2,1)S(1)} collective-permute-done((bf16[256,512]{1,0:T(8,128)(2,1)S(1)}, bf16[256,512]{1,0:T(8,128)(2,1)S(1)}, u32[]{:S(2)}, u32[]{:S(2)}) %collective-permute-start.17) | collective-permute-done | bytes 262176 | tf_op jit(solution)/shard_map/ppermute | solution.py:29
  73.2 1.6 %collective-permute-start.19 = (bf16[384,512]{1,0:T(8,128)(2,1)S(1)}, bf16[384,512]{1,0:T(8,128)(2,1)S(1)}, u32[]{:S(2)}, u32[]{:S(2)}) collective-permute-start(bf16[384,512]{1,0:T(8,128)(2,1)S(1)} %shard_map.61), channel_id=1, source_target_pairs={{0,4},{4,0},{8,12},{12,8},{16,20},{20,16},{24,28},{28,24},{1,5},{5... | collective-permute-start | bytes 1179656 | tf_op jit(solution)/shard_map/ppermute | solution.py:29
  74.8 2.6 %collective-permute-done.18.refs_6_.refs_7_ = bf16[256,512]{1,0:T(8,128)(2,1)S(1)} collective-permute-done((bf16[256,512]{1,0:T(8,128)(2,1)S(1)}, bf16[256,512]{1,0:T(8,128)(2,1)S(1)}, u32[]{:S(2)}, u32[]{:S(2)}) %collective-permute-start.18) | collective-permute-done | bytes 262176 | tf_op jit(solution)/shard_map/ppermute | solution.py:29
  78.3 1.6 %collective-permute-start.20 = (bf16[384,512]{1,0:T(8,128)(2,1)S(1)}, bf16[384,512]{1,0:T(8,128)(2,1)S(1)}, u32[]{:S(2)}, u32[]{:S(2)}) collective-permute-start(bf16[384,512]{1,0:T(8,128)(2,1)S(1)} %shard_map.62), channel_id=1, source_target_pairs={{0,4},{4,0},{8,12},{12,8},{16,20},{20,16},{24,28},{28,24},{1,5},{5... | collective-permute-start | bytes 1179656 | tf_op jit(solution)/shard_map/ppermute | solution.py:29
  80.6 7.5 %collective-permute-done.19.refs_9_ = bf16[384,512]{1,0:T(8,128)(2,1)S(1)} collective-permute-done((bf16[384,512]{1,0:T(8,128)(2,1)S(1)}, bf16[384,512]{1,0:T(8,128)(2,1)S(1)}, u32[]{:S(2)}, u32[]{:S(2)}) %collective-permute-start.19) | collective-permute-done | bytes 393248 | tf_op jit(solution)/shard_map/ppermute | solution.py:29
  88.1 6.4 %collective-permute-done.20.refs_10_ = bf16[384,512]{1,0:T(8,128)(2,1)S(1)} collective-permute-done((bf16[384,512]{1,0:T(8,128)(2,1)S(1)}, bf16[384,512]{1,0:T(8,128)(2,1)S(1)}, u32[]{:S(2)}, u32[]{:S(2)}) %collective-permute-start.20) | collective-permute-done | bytes 393248 | tf_op jit(solution)/shard_map/ppermute | solution.py:29
  94.5 3.8 %shard_map.63._ = f32[384,3072]{1,0:T(8,128)} custom-call(s32[2]{0:T(128)S(1)} %pad_add_fusion.place_ref, bf16[384,1024]{1,0:T(8,128)(2,1)S(1)} %get-tuple-element.23.grad_ref, bf16[128,1536]{1,0:T(8,128)(2,1)S(1)} %get-tuple-element.24.refs_0_, bf16[128,1536]{1,0:T(8,128)(2,1)S(1)} %collective-permute-done.5.refs_1_, ...), custom_call_target="tpu_custom_call" | custom-call | flops 1207959552 | bytes 4718592 | tf_op jit(solution)/shard_map/pallas_call | solution.py:159
  98.4 1.5 %shard_map.64 = f32[384,3072]{1,0:T(8,128)} custom-call(s32[2]{0:T(128)S(1)} %pad_add_fusion.place_ref, bf16[384,512]{1,0:T(8,128)(2,1)S(1)} %collective-permute-done.16.back_ref, f32[384,3072]{1,0:T(8,128)} %shard_map.63._), custom_call_target="tpu_custom_call", output_to_operand_aliasing={{}: (2, {})} | custom-call | bytes 786432 | tf_op jit(solution)/shard_map/pallas_call | solution.py:181
  (47 shorter events, 13.1 us)
Async XLA Ops:
  0.6 14.2 %copy-start.1 = (bf16[32,3072]{1,0:T(8,128)(2,1)S(1)}, bf16[32,3072]{1,0:T(8,128)(2,1)}, u32[]{:S(2)}) copy-start(bf16[32,3072]{1,0:T(8,128)(2,1)} %param.5) | copy-start | bytes 589828
  0.6 14.2 %collective-permute-start = (bf16[32,3072]{1,0:T(8,128)(2,1)}, bf16[32,3072]{1,0:T(8,128)(2,1)S(1)}, u32[]{:S(2)}, u32[]{:S(2)}) collective-permute-start(bf16[32,3072]{1,0:T(8,128)(2,1)} %param.5), channel_id=1, source_target_pairs={{0,2},{1,3},{2,0},{3,1},{4,6},{5,7},{6,4},{7,5},{8,10},{9,11},{10,... | collective-permute-start | bytes 589832 | tf_op jit(solution)/shard_map/ppermute | solution.py:29
  4.6 6.5 %collective-permute-start.4 = (bf16[32,768]{1,0:T(8,128)(2,1)S(1)}, bf16[32,768]{1,0:T(8,128)(2,1)S(1)}, u32[]{:S(2)}, u32[]{:S(2)}) collective-permute-start(bf16[32,768]{1,0:T(8,128)(2,1)S(1)} %get-tuple-element.40), channel_id=1, source_target_pairs={{0,24},{4,28},{8,16},{12,20},{16,8},{20,12},{24,0},{28,4},{1,25},{... | collective-permute-start | bytes 147464 | tf_op jit(solution)/shard_map/ppermute | solution.py:29
  8.2 5.0 %collective-permute-start.3 = (bf16[32,768]{1,0:T(8,128)(2,1)S(1)}, bf16[32,768]{1,0:T(8,128)(2,1)S(1)}, u32[]{:S(2)}, u32[]{:S(2)}) collective-permute-start(bf16[32,768]{1,0:T(8,128)(2,1)S(1)} %get-tuple-element.41), channel_id=1, source_target_pairs={{0,16},{4,20},{8,24},{12,28},{16,0},{20,4},{24,8},{28,12},{1,17},{... | collective-permute-start | bytes 147464 | tf_op jit(solution)/shard_map/ppermute | solution.py:29
  8.2 5.0 %collective-permute-start.2 = (bf16[32,768]{1,0:T(8,128)(2,1)S(1)}, bf16[32,768]{1,0:T(8,128)(2,1)S(1)}, u32[]{:S(2)}, u32[]{:S(2)}) collective-permute-start(bf16[32,768]{1,0:T(8,128)(2,1)S(1)} %get-tuple-element.39), channel_id=1, source_target_pairs={{0,8},{4,12},{8,0},{12,4},{16,24},{20,28},{24,16},{28,20},{1,9},{5... | collective-permute-start | bytes 147464 | tf_op jit(solution)/shard_map/ppermute | solution.py:29
  13.3 14.7 %collective-permute-start.5 = (bf16[128,1536]{1,0:T(8,128)(2,1)S(1)}, bf16[128,1536]{1,0:T(8,128)(2,1)S(1)}, u32[]{:S(2)}, u32[]{:S(2)}) collective-permute-start(bf16[128,1536]{1,0:T(8,128)(2,1)S(1)} %get-tuple-element.14), channel_id=1, source_target_pairs={{0,4},{4,0},{8,12},{12,8},{16,20},{20,16},{24,28},{28,24},{1,5},{5... | collective-permute-start | bytes 1179656 | tf_op jit(solution)/shard_map/ppermute | solution.py:29
  14.9 14.9 %collective-permute-start.1 = (bf16[2,32,3072]{2,1,0:T(8,128)(2,1)S(1)}, bf16[2,32,3072]{2,1,0:T(8,128)(2,1)}, u32[]{:S(2)}, u32[]{:S(2)}) collective-permute-start(bf16[2,32,3072]{2,1,0:T(8,128)(2,1)S(1)} %pad_maximum_fusion.2), channel_id=1, source_target_pairs={{0,1},{1,0},{2,3},{3,2},{4,5},{5,4},{6,7},{7,6},{8,9},{9,8},{10,11... | collective-permute-start | bytes 1179656 | tf_op jit(solution)/shard_map/ppermute | solution.py:29
  15.0 11.8 %collective-permute-start.6 = (bf16[4,32,768]{2,1,0:T(8,128)(2,1)S(1)}, bf16[4,32,768]{2,1,0:T(8,128)(2,1)S(1)}, u32[]{:S(2)}, u32[]{:S(2)}) collective-permute-start(bf16[4,32,768]{2,1,0:T(8,128)(2,1)S(1)} %pad_maximum_fusion.7), channel_id=1, source_target_pairs={{0,4},{4,0},{8,12},{12,8},{16,20},{20,16},{24,28},{28,24},{1,5},{5... | collective-permute-start | bytes 589832 | tf_op jit(solution)/shard_map/ppermute | solution.py:29
  15.6 35.4 %collective-permute-start.7 = (bf16[128,1536]{1,0:T(8,128)(2,1)S(1)}, bf16[128,1536]{1,0:T(8,128)(2,1)S(1)}, u32[]{:S(2)}, u32[]{:S(2)}) collective-permute-start(bf16[128,1536]{1,0:T(8,128)(2,1)S(1)} %get-tuple-element.24.refs_0_), channel_id=1, source_target_pairs={{0,16},{4,20},{8,24},{12,28},{16,0},{20,4},{24,8},{28,12},{1,17},{... | collective-permute-start | bytes 1179656 | tf_op jit(solution)/shard_map/ppermute | solution.py:29
  17.6 33.4 %collective-permute-start.9 = (bf16[128,1536]{1,0:T(8,128)(2,1)S(1)}, bf16[128,1536]{1,0:T(8,128)(2,1)S(1)}, u32[]{:S(2)}, u32[]{:S(2)}) collective-permute-start(bf16[128,1536]{1,0:T(8,128)(2,1)S(1)} %get-tuple-element.24.refs_0_), channel_id=1, source_target_pairs={{0,8},{4,12},{8,0},{12,4},{16,24},{20,28},{24,16},{28,20},{1,9},{5... | collective-permute-start | bytes 1179656 | tf_op jit(solution)/shard_map/ppermute | solution.py:29
  27.6 23.4 %collective-permute-start.11 = (bf16[2,4,32,768]{3,2,1,0:T(8,128)(2,1)}, bf16[2,4,32,768]{3,2,1,0:T(8,128)(2,1)}, u32[]{:S(2)}, u32[]{:S(2)}) collective-permute-start(bf16[2,4,32,768]{3,2,1,0:T(8,128)(2,1)} %get-tuple-element.35), channel_id=1, source_target_pairs={{0,2},{1,3},{2,0},{3,1},{4,6},{5,7},{6,4},{7,5},{8,10},{9,11},{10,... | collective-permute-start | bytes 1179656 | tf_op jit(solution)/shard_map/ppermute | solution.py:29
  28.0 24.9 %collective-permute-start.8 = (bf16[128,1536]{1,0:T(8,128)(2,1)S(1)}, bf16[128,1536]{1,0:T(8,128)(2,1)S(1)}, u32[]{:S(2)}, u32[]{:S(2)}) collective-permute-start(bf16[128,1536]{1,0:T(8,128)(2,1)S(1)} %collective-permute-done.5.refs_1_), channel_id=1, source_target_pairs={{0,16},{4,20},{8,24},{12,28},{16,0},{20,4},{24,8},{28,12},{1,17},{... | collective-permute-start | bytes 1179656 | tf_op jit(solution)/shard_map/ppermute | solution.py:29
  29.8 23.9 %collective-permute-start.10 = (bf16[128,1536]{1,0:T(8,128)(2,1)S(1)}, bf16[128,1536]{1,0:T(8,128)(2,1)S(1)}, u32[]{:S(2)}, u32[]{:S(2)}) collective-permute-start(bf16[128,1536]{1,0:T(8,128)(2,1)S(1)} %collective-permute-done.5.refs_1_), channel_id=1, source_target_pairs={{0,8},{4,12},{8,0},{12,4},{16,24},{20,28},{24,16},{28,20},{1,9},{5... | collective-permute-start | bytes 1179656 | tf_op jit(solution)/shard_map/ppermute | solution.py:29
  51.0 6.2 %copy-start = (f32[128,3072]{1,0:T(8,128)S(1)}, f32[128,3072]{1,0:T(8,128)}, u32[]{:S(2)}) copy-start(f32[128,3072]{1,0:T(8,128)} %fusion.15) | copy-start | bytes 4718596
  54.8 2.4 %collective-permute-start.12 = (bf16[2,2,4,32,768]{4,3,2,1,0:T(8,128)(2,1)S(1)}, bf16[2,2,4,32,768]{4,3,2,1,0:T(8,128)(2,1)S(1)}, u32[]{:S(2)}, u32[]{:S(2)}) collective-permute-start(bf16[2,2,4,32,768]{4,3,2,1,0:T(8,128)(2,1)S(1)} %pad_maximum_fusion.1.own_ref), channel_id=1, source_target_pairs={{0,1},{1,0},{2,3},{3,2},{4,5},{5,4},{6,7},{7,6},{8,9},{9,8},{10,11... | collective-permute-start | bytes 2359304 | tf_op jit(solution)/shard_map/ppermute | solution.py:29
  57.2 22.6 %collective-permute-start.13 = (f32[2,32,3072]{2,1,0:T(8,128)S(1)}, f32[2,32,3072]{2,1,0:T(8,128)S(1)}, u32[]{:S(2)}, u32[]{:S(2)}) collective-permute-start(f32[2,32,3072]{2,1,0:T(8,128)S(1)} %select_bitcast_fusion), channel_id=1, source_target_pairs={{0,1},{1,0},{2,3},{3,2},{4,5},{5,4},{6,7},{7,6},{8,9},{9,8},{10,11... | collective-permute-start | bytes 2359304 | tf_op jit(solution)/shard_map/ppermute | solution.py:29
  57.5 9.2 %collective-permute-start.15 = (bf16[256,512]{1,0:T(8,128)(2,1)S(1)}, bf16[256,512]{1,0:T(8,128)(2,1)S(1)}, u32[]{:S(2)}, u32[]{:S(2)}) collective-permute-start(bf16[256,512]{1,0:T(8,128)(2,1)S(1)} %pad_maximum_fusion.4), channel_id=1, source_target_pairs={{0,8},{4,12},{8,0},{12,4},{16,24},{20,28},{24,16},{28,20},{1,9},{5... | collective-permute-start | bytes 786440 | tf_op jit(solution)/shard_map/ppermute | solution.py:29
  58.1 14.3 %collective-permute-start.17 = (bf16[256,512]{1,0:T(8,128)(2,1)S(1)}, bf16[256,512]{1,0:T(8,128)(2,1)S(1)}, u32[]{:S(2)}, u32[]{:S(2)}) collective-permute-start(bf16[256,512]{1,0:T(8,128)(2,1)S(1)} %pad_maximum_fusion.5), channel_id=1, source_target_pairs={{0,8},{4,12},{8,0},{12,4},{16,24},{20,28},{24,16},{28,20},{1,9},{5... | collective-permute-start | bytes 786440 | tf_op jit(solution)/shard_map/ppermute | solution.py:29
  59.7 17.7 %collective-permute-start.18 = (bf16[256,512]{1,0:T(8,128)(2,1)S(1)}, bf16[256,512]{1,0:T(8,128)(2,1)S(1)}, u32[]{:S(2)}, u32[]{:S(2)}) collective-permute-start(bf16[256,512]{1,0:T(8,128)(2,1)S(1)} %pad_maximum_fusion.6), channel_id=1, source_target_pairs={{0,8},{4,12},{8,0},{12,4},{16,24},{20,28},{24,16},{28,20},{1,9},{5... | collective-permute-start | bytes 786440 | tf_op jit(solution)/shard_map/ppermute | solution.py:29
  67.6 30.8 %collective-permute-start.16 = (bf16[384,512]{1,0:T(8,128)(2,1)S(1)}, bf16[384,512]{1,0:T(8,128)(2,1)S(1)}, u32[]{:S(2)}, u32[]{:S(2)}) collective-permute-start(bf16[384,512]{1,0:T(8,128)(2,1)S(1)} %shard_map.60), channel_id=1, source_target_pairs={{0,4},{4,0},{8,12},{12,8},{16,20},{20,16},{24,28},{28,24},{1,5},{5... | collective-permute-start | bytes 1179656 | tf_op jit(solution)/shard_map/ppermute | solution.py:29
  73.2 14.9 %collective-permute-start.19 = (bf16[384,512]{1,0:T(8,128)(2,1)S(1)}, bf16[384,512]{1,0:T(8,128)(2,1)S(1)}, u32[]{:S(2)}, u32[]{:S(2)}) collective-permute-start(bf16[384,512]{1,0:T(8,128)(2,1)S(1)} %shard_map.61), channel_id=1, source_target_pairs={{0,4},{4,0},{8,12},{12,8},{16,20},{20,16},{24,28},{28,24},{1,5},{5... | collective-permute-start | bytes 1179656 | tf_op jit(solution)/shard_map/ppermute | solution.py:29
  78.3 16.3 %collective-permute-start.20 = (bf16[384,512]{1,0:T(8,128)(2,1)S(1)}, bf16[384,512]{1,0:T(8,128)(2,1)S(1)}, u32[]{:S(2)}, u32[]{:S(2)}) collective-permute-start(bf16[384,512]{1,0:T(8,128)(2,1)S(1)} %shard_map.62), channel_id=1, source_target_pairs={{0,4},{4,0},{8,12},{12,8},{16,20},{20,16},{24,28},{28,24},{1,5},{5... | collective-permute-start | bytes 1179656 | tf_op jit(solution)/shard_map/ppermute | solution.py:29
  80.0 19.8 %collective-permute-start.14 = (f32[32,3072]{1,0:T(8,128)S(1)}, f32[32,3072]{1,0:T(8,128)S(1)}, u32[]{:S(2)}, u32[]{:S(2)}) collective-permute-start(f32[32,3072]{1,0:T(8,128)S(1)} %select_bitcast_fusion.1), channel_id=1, source_target_pairs={{0,2},{1,3},{2,0},{3,1},{4,6},{5,7},{6,4},{7,5},{8,10},{9,11},{10,... | collective-permute-start | bytes 1179656 | tf_op jit(solution)/shard_map/ppermute | solution.py:29

commit v4 on v1

v4 whole, which is shorter than its diff:
```python
import math

import jax
import jax.numpy as jnp
from jax import lax
from jax.experimental import pallas as pl
from jax.experimental.pallas import tpu as pltpu
from jax.sharding import PartitionSpec as P

BF16 = jnp.bfloat16
F32 = jnp.float32


def gelu_value_of(pre):
    pre_float = pre.astype(F32)
    normal_cdf = 0.5 * (1.0 + jax.scipy.special.erf(pre_float / math.sqrt(2.0)))
    return (pre_float * normal_cdf).astype(BF16)


def gelu_slope_of(pre):
    pre_float = pre.astype(F32)
    normal_cdf = 0.5 * (1.0 + jax.scipy.special.erf(pre_float / math.sqrt(2.0)))
    density = jnp.exp(-0.5 * pre_float * pre_float) / math.sqrt(2.0 * math.pi)
    return normal_cdf + pre_float * density


def xor_permute(value, axis, mask):
    count = lax.axis_size(axis)
    return lax.ppermute(value, axis, [(i, i ^ mask) for i in range(count)])


def either(bit, low, high):
    return jnp.where(bit == 0, low, high)


def gathered_plan(pre_act, out_grad, w_up, w_down):
    act = gelu_value_of(pre_act)
    gathered = lax.all_gather(out_grad, "tensor", axis=0, tiled=True)
    hidden_grad = lax.dot_general(gathered, w_down, (((1,), (1,)), ((), ())), preferred_element_type=F32)
    pre_grad = (hidden_grad * gelu_slope_of(pre_act)).astype(BF16)
    all_tokens = gathered.shape[0] * lax.axis_size("dp")
    my_columns = lax.all_to_all(gathered, "dp", split_axis=1, concat_axis=0, tiled=True)
    summed = lax.dot_general(
        my_columns,
        lax.all_gather(act, "dp", axis=0, tiled=True),
        (((0,), (0,)), ((), ())),
        preferred_element_type=F32,
    )
    in_grad = lax.psum_scatter(
        lax.dot_general(pre_grad, w_up, (((1,), (1,)), ((), ())), preferred_element_type=F32),
        "tensor",
        scatter_dimension=0,
        tiled=True,
    ).astype(BF16)
    return (in_grad, summed / math.sqrt(all_tokens))


VMEM_LIMIT = 16 * 1024 * 1024


def params():
    return pltpu.CompilerParams(vmem_limit_bytes=VMEM_LIMIT)


def cost(flops, moved):
    return pl.CostEstimate(flops=flops, bytes_accessed=moved, transcendentals=0)


def whole():
    return pl.BlockSpec(memory_space=pltpu.VMEM)


def prepare(place, blocks):
    _, depth, rows, pair = blocks[0].shape
    block = pair // 2
    tokens = 2 * depth * len(blocks) * rows

    def body(place_ref, *refs):
        mine_ref, theirs_ref, held_ref = refs[len(blocks) :]
        x, shard = place_ref[0], place_ref[1]
        for i, ref in enumerate(refs[: len(blocks)]):
            for k in range(depth):
                for j in range(2):
                    at = ((2 * (k % 2 * 2 + k // 2) + j) * len(blocks) + (i ^ shard)) * rows
                    held_ref[pl.ds(pl.multiple_of(at, rows), rows), :] = ref[j, k]
        for out, bit in ((mine_ref, x), (theirs_ref, 1 - x)):
            columns = pl.ds(pl.multiple_of(bit * block, 128), block)
            out[...] = held_ref[:, columns].T

    shape = jax.ShapeDtypeStruct((block, tokens), BF16)
    return pl.pallas_call(
        body,
        in_specs=[pl.BlockSpec(memory_space=pltpu.SMEM)] + [whole()] * len(blocks),
        out_specs=[whole(), whole()],
        out_shape=[shape, shape],
        scratch_shapes=[pltpu.VMEM((tokens, pair), BF16)],
        compiler_params=params(),
        cost_estimate=cost(0, 8 * tokens * pair),
    )(place, *blocks)


def contract(grad_ref, refs, pieces, scale):
    total, row = None, 0
    for ref, (piece, offset, size) in zip(refs, pieces):
        depth = piece.shape[0]
        value = ref[:, offset : offset + size]
        part = jnp.dot(grad_ref[:, row : row + depth], value, preferred_element_type=F32)
        total = part if total is None else total + part
        row += depth
    return total * scale


def their_product(theirs, pieces, scale):
    def body(grad_ref, *refs):
        refs[-1][...] = contract(grad_ref, refs[:-1], pieces, scale).astype(BF16)

    block, tokens = theirs.shape
    size = pieces[0][2]
    return pl.pallas_call(
        body,
        in_specs=[whole()] * (1 + len(pieces)),
        out_specs=whole(),
        out_shape=jax.ShapeDtypeStruct((block, size), BF16),
        compiler_params=params(),
        cost_estimate=cost(2 * block * tokens * size, 4 * tokens * size),
    )(theirs, *[piece for piece, _, _ in pieces])


def write_columns(place, result, mine, products, backs, width, scale):
    block, tokens = mine.shape
    half = width // 2
    flat = [piece for pieces, _ in products for piece, _, _ in pieces]
    sizes = [pieces[0][2] for pieces, _ in products] + [back.shape[1] for back, _ in backs]
    first = 0 if result is None else 1

    def body(place_ref, grad_ref, *refs):
        refs = refs[first:]
        piece_refs, back_refs = refs[: len(flat)], refs[len(flat) : len(flat) + len(backs)]
        out_ref, held_ref, sems = refs[len(flat) + len(backs) :]
        copies = []

        def store(bit, column, size, value):
            slot = len(copies)
            here = held_ref.at[:, pl.ds(sum(sizes[:slot]), size)]
            here[...] = value
            to = pl.ds(pl.multiple_of(bit * half + column, 128), size)
            copies.append(pltpu.make_async_copy(here, out_ref.at[:, to], sems.at[slot]))
            copies[-1].start()

        at = 0
        for pieces, column in products:
            value = contract(grad_ref, piece_refs[at : at + len(pieces)], pieces, scale)
            store(place_ref[0], column, pieces[0][2], value)
            at += len(pieces)
        for ref, (back, column) in zip(back_refs, backs):
            store(1 - place_ref[0], column, back.shape[1], ref[...].astype(F32))
        for copy in copies:
            copy.wait()

    held = [] if result is None else [result]
    return pl.pallas_call(
        body,
        in_specs=[pl.BlockSpec(memory_space=pltpu.SMEM), whole() if products else pl.BlockSpec(memory_space=pl.ANY)]
        + [pl.BlockSpec(memory_space=pl.ANY)] * first
        + [whole()] * (len(flat) + len(backs)),
        out_specs=pl.BlockSpec(memory_space=pl.ANY),
        out_shape=jax.ShapeDtypeStruct((block, width), F32),
        input_output_aliases={2: 0} if first else {},
        scratch_shapes=[pltpu.VMEM((block, sum(sizes)), F32), pltpu.SemaphoreType.DMA((len(sizes),))],
        compiler_params=params(),
        cost_estimate=cost(2 * block * tokens * sum(sizes) if products else 0, 4 * block * sum(sizes)),
    )(place, mine, *held, *flat, *[back for back, _ in backs])


def after(value, *others):
    return lax.optimization_barrier((value, *others))[0]


def plane_plan(pre_act, out_grad, w_up, w_down):
    at, shard = lax.axis_index("dp"), lax.axis_index("tensor")
    z, x = at // 2, at % 2
    y, core = shard // 2, shard % 2
    place = jnp.stack([x, shard]).astype(jnp.int32)
    rows, width = out_grad.shape
    tokens, units = pre_act.shape
    half = units // 2
    pair = width // 4
    scale = 1.0 / math.sqrt(tokens * 8)
    head = half // 3
    tail = half // 4
    middle = half - head - tail

    def columns(pre, bit, offset, size):
        low = pre[:, offset : offset + size]
        high = pre[:, half + offset : half + offset + size]
        return gelu_value_of(either(bit, low, high))

    kept0, sent0 = columns(pre_act, x, 0, head), columns(pre_act, 1 - x, 0, head)
    got0 = xor_permute(sent0, "dp", 1)
    later_act = after(pre_act, sent0)
    kept, sent = columns(later_act, x, head, half - head), columns(later_act, 1 - x, head, half - head)
    got = xor_permute(sent, "dp", 1)
    own0 = jnp.concatenate([kept0, got0])
    far0 = xor_permute(own0, "dp", 4)
    near0 = xor_permute(own0, "dp", 2)

    other = xor_permute(out_grad, "tensor", 2)
    rows_y = jnp.stack([either(y, out_grad, other), either(y, other, out_grad)])
    other = xor_permute(rows_y, "tensor", 1)
    group = jnp.stack([either(core, rows_y, other), either(core, other, rows_y)], axis=1).reshape(tokens, width)

    later_grad = after(out_grad, own0)

    def slab(k):
        return lax.dynamic_slice(later_grad, (0, (z ^ k) * pair), (rows, pair))

    grad = jnp.stack([slab(0)] + [xor_permute(slab(k), "dp", 2 * k) for k in (1, 2, 3)])
    grad_x = xor_permute(grad, "dp", 1)
    both_x = jnp.stack([grad, grad_x])
    grads = [xor_permute(both_x, "tensor", i) for i in (1, 2, 3)]

    own = jnp.concatenate([kept, got])
    joint = xor_permute(after(jnp.concatenate([far0, own[:, :middle]], axis=1), near0), "dp", 2)
    far = xor_permute(after(own, far0, near0), "dp", 4)

    group = after(group, own, grad_x, far0, near0)
    hidden_grad = lax.dot_general(group, w_down, (((1,), (1,)), ((), ())), preferred_element_type=F32)
    pre_grad = (hidden_grad * gelu_slope_of(pre_act)).astype(BF16)
    partial = lax.dot_general(pre_grad, w_up, (((1,), (1,)), ((), ())), preferred_element_type=F32)

    joint, *grads = lax.optimization_barrier((joint, *grads, partial))[:-1]
    mine, theirs = prepare(place, [both_x, *grads])
    pieces0 = [(p, 0, head) for p in (own0, far0, near0, joint)]
    their0 = their_product(theirs, pieces0, scale)
    back0 = xor_permute(their0, "dp", 1)
    far = after(far, their0)
    last = xor_permute(far[:, :middle], "dp", 2)
    pieces1 = [(own, 0, middle), (far, 0, middle), (joint, head, middle), (last, 0, middle)]
    their1 = their_product(theirs, pieces1, scale)
    back1 = xor_permute(their1, "dp", 1)
    ends = xor_permute(jnp.concatenate([own[:, middle:], far[:, middle:]]), "dp", 2)
    pieces2 = [(own, middle, tail), (far, middle, tail), (ends, 0, tail)]
    their2 = their_product(theirs, pieces2, scale)
    back2 = xor_permute(their2, "dp", 1)
    products = [(pieces0, 0), (pieces1, head), (pieces2, head + middle)]
    backs = [(back0, 0), (back1, head), (back2, head + middle)]

    partial = after(partial, their0).reshape(2, 2, rows, width)
    keep = either(core, partial[:, 0], partial[:, 1])
    give = either(core, partial[:, 1], partial[:, 0])
    keep = keep + xor_permute(give, "tensor", 1)
    in_grad = either(y, keep[0], keep[1]) + xor_permute(either(y, keep[1], keep[0]), "tensor", 2)

    result = write_columns(place, None, after(mine, their2), products, backs[:1], units, scale)
    result = write_columns(place, result, mine, [], backs[1:2], units, scale)
    result = write_columns(place, result, mine, [], backs[2:], units, scale)
    return (in_grad.astype(BF16), result)


def solution(mesh):
    plan = plane_plan if (mesh.shape["dp"], mesh.shape["tensor"]) == (8, 4) else gathered_plan
    placed = (P("dp", "tensor"), P(("dp", "tensor"), None), P(None, "tensor"), P("tensor", None))
    return jax.shard_map(
        plan,
        mesh=mesh,
        in_specs=placed,
        out_specs=(P(("dp", "tensor"), None), P("dp", "tensor")),
        check_vma=False,
    )
```

time: 158 us -> 93.7 us (0.59)
  waiting for transfers between devices: 65.2 us -> 29.3 us
  local copies, waits for them, and re-layouts: 21.2 us -> 0.91 us
  Pallas kernels: 0 us -> 10.2 us
  other arithmetic: 14.8 us -> 5.65 us
  blocking collectives: 8.61 us -> 0 us
  matrix products: 21.1 us -> 19.4 us
    ppermute x26 -> x22, waiting for transfers between devices: 65.2 us -> 29.3 us  [xor_permute(): return lax.ppermute(value, axis, [(i, i ^ mask) for i in range(count)])]
    unnamed x34 -> x8, local copies, waits for them, and re-layouts: 14 us -> 0.82 us
    pallas_call x0 -> x7, Pallas kernels: none -> 10.2 us  [the longest x3 6.59 us: write_columns(): pl.pallas_call(body, in_specs=[pl.BlockSpec(memory_space=pltpu.SMEM), who...]
    all_gather x1 -> x0, blocking collectives: 8.61 us -> none  [plane_plan(): gathered = lax.all_gather(out_grad, 'tensor', axis=0, tiled=True)]
    unnamed x3 -> x0, other arithmetic: 4.32 us -> none
    select_n x4 -> x2, other arithmetic: 4.33 us -> 0.13 us  [either(): return jnp.where(bit == 0, low, high)]
    reshape x1 -> x0, local copies, waits for them, and re-layouts: 3.39 us -> none  [plane_plan(): grad = grad.reshape(8 * tokens, 2, block)]
    dot_general x3 -> x0, matrix products: 3.21 us -> none  [plane_plan(): lax.dot_general(both, act, (((0,), (0,)), ((), ())), preferred_element_ty...]
  transfers between devices with their start and end apart: 26 -> 22, of which waited for: 10 -> 10; matrix products, arithmetic and copies ran while one was open for 27% -> 26% of each run, Pallas kernels for 0% -> 11%
where the time goes in v4:
time: 93.7 us; the launch traced here: 93.5 us
  waiting for transfers between devices  29.3 us (31%)
  starting transfers between devices  27.2 us (29%)
  matrix products  19.4 us (21%)
  Pallas kernels  10.2 us (11%)
  other arithmetic  5.65 us (6%)
    ppermute x22, waiting for transfers between devices, xor_permute(): return lax.ppermute(value, axis, [(i, i ^ mask) for i in range(count)])  29.3 us
    ppermute x22, starting transfers between devices, xor_permute(): return lax.ppermute(value, axis, [(i, i ^ mask) for i in range(count)])  27.2 us
    dot_general x1, matrix products, plane_plan(): lax.dot_general(pre_grad, w_up, (((1,), (1,)), ((), ())), preferred_eleme...  19.4 us
    pallas_call x3, Pallas kernels, write_columns(): pl.pallas_call(body, in_specs=[pl.BlockSpec(memory_space=pltpu.SMEM), who...  6.59 us
    convert_element_type x2, other arithmetic, gelu_value_of(): return (pre_float * normal_cdf).astype(BF16)  2.39 us
    pallas_call x3, Pallas kernels, their_product(): pl.pallas_call(body, in_specs=[whole()] * (1 + len(pieces)), out_specs=wh...  1.93 us
  transfers between devices with their start and end apart: 22, of which 10 were waited for; matrix products, arithmetic and copies ran while one was open for 26% of the time, Pallas kernels for 11%

profile of v4, /device:TPU:0, one launch (start us, length us, event | category | flops | bytes accessed | tf_op | source)
XLA Modules:
  0.0 93.5 jit_solution(15289660666525835295)
XLA Ops:
  0.6 3.0 %collective-permute-start = (bf16[32,3072]{1,0:T(8,128)(2,1)}, bf16[32,3072]{1,0:T(8,128)(2,1)S(1)}, u32[]{:S(2)}, u32[]{:S(2)}) collective-permute-start(bf16[32,3072]{1,0:T(8,128)(2,1)} %param.5), channel_id=1, source_target_pairs={{0,2},{1,3},{2,0},{3,1},{4,6},{5,7},{6,4},{7,5},{8,10},{9,11},{10,... | collective-permute-start | bytes 589832 | tf_op jit(solution)/shard_map/ppermute | solution.py:29
  4.8 1.6 %collective-permute-start.3 = (bf16[128,512]{1,0:T(8,128)(2,1)S(1)}, bf16[128,512]{1,0:T(8,128)(2,1)S(1)}, u32[]{:S(2)}, u32[]{:S(2)}) collective-permute-start(bf16[128,512]{1,0:T(8,128)(2,1)S(1)} %get-tuple-element.31), channel_id=1, source_target_pairs={{0,4},{4,0},{8,12},{12,8},{16,20},{20,16},{24,28},{28,24},{1,5},{5... | collective-permute-start | bytes 393224 | tf_op jit(solution)/shard_map/ppermute | solution.py:29
  8.2 1.8 %collective-permute-done.3 = bf16[128,512]{1,0:T(8,128)(2,1)S(1)} collective-permute-done((bf16[128,512]{1,0:T(8,128)(2,1)S(1)}, bf16[128,512]{1,0:T(8,128)(2,1)S(1)}, u32[]{:S(2)}, u32[]{:S(2)}) %collective-permute-start.3) | collective-permute-done | bytes 131104 | tf_op jit(solution)/shard_map/ppermute | solution.py:29
  10.1 3.7 %collective-permute-start.6 = (bf16[32,768]{1,0:T(8,128)(2,1)S(1)}, bf16[32,768]{1,0:T(8,128)(2,1)S(1)}, u32[]{:S(2)}, u32[]{:S(2)}) collective-permute-start(bf16[32,768]{1,0:T(8,128)(2,1)S(1)} %get-tuple-element.41), channel_id=1, source_target_pairs={{0,24},{4,28},{8,16},{12,20},{16,8},{20,12},{24,0},{28,4},{1,25},{... | collective-permute-start | bytes 147464 | tf_op jit(solution)/shard_map/ppermute | solution.py:29
  14.6 1.5 %collective-permute-done.6 = bf16[32,768]{1,0:T(8,128)(2,1)S(1)} collective-permute-done((bf16[32,768]{1,0:T(8,128)(2,1)S(1)}, bf16[32,768]{1,0:T(8,128)(2,1)S(1)}, u32[]{:S(2)}, u32[]{:S(2)}) %collective-permute-start.6) | collective-permute-done | bytes 49184 | tf_op jit(solution)/shard_map/ppermute | solution.py:29
  16.2 2.7 %collective-permute-done.5 = bf16[32,768]{1,0:T(8,128)(2,1)S(1)} collective-permute-done((bf16[32,768]{1,0:T(8,128)(2,1)S(1)}, bf16[32,768]{1,0:T(8,128)(2,1)S(1)}, u32[]{:S(2)}, u32[]{:S(2)}) %collective-permute-start.5) | collective-permute-done | bytes 49184 | tf_op jit(solution)/shard_map/ppermute | solution.py:29
  18.9 1.9 %collective-permute-start.8 = (bf16[256,512]{1,0:T(8,128)(2,1)S(1)}, bf16[256,512]{1,0:T(8,128)(2,1)S(1)}, u32[]{:S(2)}, u32[]{:S(2)}) collective-permute-start(bf16[256,512]{1,0:T(8,128)(2,1)S(1)} %pad_maximum_fusion.6.refs_0_), channel_id=1, source_target_pairs={{0,16},{4,20},{8,24},{12,28},{16,0},{20,4},{24,8},{28,12},{1,17},{... | collective-permute-start | bytes 786440 | tf_op jit(solution)/shard_map/ppermute | solution.py:29
  20.9 2.7 %collective-permute-start.7 = (bf16[4,32,768]{2,1,0:T(8,128)(2,1)S(1)}, bf16[4,32,768]{2,1,0:T(8,128)(2,1)S(1)}, u32[]{:S(2)}, u32[]{:S(2)}) collective-permute-start(bf16[4,32,768]{2,1,0:T(8,128)(2,1)S(1)} %get-tuple-element.39), channel_id=1, source_target_pairs={{0,4},{4,0},{8,12},{12,8},{16,20},{20,16},{24,28},{28,24},{1,5},{5... | collective-permute-start | bytes 589832 | tf_op jit(solution)/shard_map/ppermute | solution.py:29
  23.8 3.4 %collective-permute-done.7 = bf16[4,32,768]{2,1,0:T(8,128)(2,1)S(1)} collective-permute-done((bf16[4,32,768]{2,1,0:T(8,128)(2,1)S(1)}, bf16[4,32,768]{2,1,0:T(8,128)(2,1)S(1)}, u32[]{:S(2)}, u32[]{:S(2)}) %collective-permute-start.7) | collective-permute-done | bytes 196640 | tf_op jit(solution)/shard_map/ppermute | solution.py:29
  29.2 2.0 %collective-permute-done.8.refs_1_ = bf16[256,512]{1,0:T(8,128)(2,1)S(1)} collective-permute-done((bf16[256,512]{1,0:T(8,128)(2,1)S(1)}, bf16[256,512]{1,0:T(8,128)(2,1)S(1)}, u32[]{:S(2)}, u32[]{:S(2)}) %collective-permute-start.8) | collective-permute-done | bytes 262176 | tf_op jit(solution)/shard_map/ppermute | solution.py:29
  32.1 1.6 %collective-permute-start.10 = (bf16[256,1152]{1,0:T(8,128)(2,1)}, bf16[256,1152]{1,0:T(8,128)(2,1)S(1)}, u32[]{:S(2)}, u32[]{:S(2)}) collective-permute-start(bf16[256,1152]{1,0:T(8,128)(2,1)} %pad_maximum_fusion.2), channel_id=1, source_target_pairs={{0,8},{4,12},{8,0},{12,4},{16,24},{20,28},{24,16},{28,20},{1,9},{5... | collective-permute-start | bytes 1769480 | tf_op jit(solution)/shard_map/ppermute | solution.py:29
  34.7 19.4 %fusion.7 = f32[128,3072]{1,0:T(8,128)} fusion(bf16[3072,3072]{1,0:T(8,128)(2,1)} %param.6, bf16[128,3072]{1,0:T(8,128)(2,1)} %bitcast.49, bf16[3072,3072]{1,0:T(8,128)(2,1)} %param.7, bf16[128,3072]{1,0:T(8,128)(2,1)} %param.4), kind=kOutput, calls=%fused_computation.26 | convolution fusion | flops 4836163584 | bytes 40894464 | tf_op jit(solution)/shard_map/dot_general | solution.py:229
  54.1 3.4 %collective-permute-done.10.refs_3_.refs_6_.refs_2_ = bf16[256,1152]{1,0:T(8,128)(2,1)S(1)} collective-permute-done((bf16[256,1152]{1,0:T(8,128)(2,1)}, bf16[256,1152]{1,0:T(8,128)(2,1)S(1)}, u32[]{:S(2)}, u32[]{:S(2)}) %collective-permute-start.10) | collective-permute-done | bytes 589856 | tf_op jit(solution)/shard_map/ppermute | solution.py:29
  57.5 1.7 %shard_map.59 = (bf16[384,1024]{1,0:T(8,128)(2,1)S(1)}, bf16[384,1024]{1,0:T(8,128)(2,1)S(1)}) custom-call(s32[2]{0:T(128)S(1)} %pad_add_fusion.place_ref, bf16[2,4,32,768]{3,2,1,0:T(8,128)(2,1)S(1)} %pad_maximum_fusion.4.refs_0_, bf16[2,4,32,768]{3,2,1,0:T(8,128)(2,1)} %collective-permute-done.11.refs_1_, ...), custom_call_target="tpu_custom_call" | custom-call | bytes 6291456 | tf_op jit(solution)/shard_map/pallas_call | solution.py:91
  61.1 2.1 %collective-permute-start.19 = (bf16[384,512]{1,0:T(8,128)(2,1)S(1)}, bf16[384,512]{1,0:T(8,128)(2,1)S(1)}, u32[]{:S(2)}, u32[]{:S(2)}) collective-permute-start(bf16[384,512]{1,0:T(8,128)(2,1)S(1)} %shard_map.60), channel_id=1, source_target_pairs={{0,4},{4,0},{8,12},{12,8},{16,20},{20,16},{24,28},{28,24},{1,5},{5... | collective-permute-start | bytes 1179656 | tf_op jit(solution)/shard_map/ppermute | solution.py:29
  63.2 2.0 %collective-permute-start.17 = (bf16[512,384]{1,0:T(8,128)(2,1)S(1)}, bf16[512,384]{1,0:T(8,128)(2,1)S(1)}, u32[]{:S(2)}, u32[]{:S(2)}) collective-permute-start(bf16[512,384]{1,0:T(8,128)(2,1)S(1)} %pad_maximum_fusion.5), channel_id=1, source_target_pairs={{0,8},{4,12},{8,0},{12,4},{16,24},{20,28},{24,16},{28,20},{1,9},{5... | collective-permute-start | bytes 1179656 | tf_op jit(solution)/shard_map/ppermute | solution.py:29
  65.2 6.2 %collective-permute-done.18.refs_7_.refs_3_ = bf16[256,640]{1,0:T(8,128)(2,1)S(1)} collective-permute-done((bf16[256,640]{1,0:T(8,128)(2,1)S(1)}, bf16[256,640]{1,0:T(8,128)(2,1)S(1)}, u32[]{:S(2)}, u32[]{:S(2)}) %collective-permute-start.18) | collective-permute-done | bytes 327712 | tf_op jit(solution)/shard_map/ppermute | solution.py:29
  72.2 2.1 %collective-permute-start.20 = (bf16[384,640]{1,0:T(8,128)(2,1)S(1)}, bf16[384,640]{1,0:T(8,128)(2,1)S(1)}, u32[]{:S(2)}, u32[]{:S(2)}) collective-permute-start(bf16[384,640]{1,0:T(8,128)(2,1)S(1)} %shard_map.63), channel_id=1, source_target_pairs={{0,4},{4,0},{8,12},{12,8},{16,20},{20,16},{24,28},{28,24},{1,5},{5... | collective-permute-start | bytes 1474568 | tf_op jit(solution)/shard_map/ppermute | solution.py:29
  75.3 4.2 %collective-permute-done.17.refs_2_.refs_10_ = bf16[512,384]{1,0:T(8,128)(2,1)S(1)} collective-permute-done((bf16[512,384]{1,0:T(8,128)(2,1)S(1)}, bf16[512,384]{1,0:T(8,128)(2,1)S(1)}, u32[]{:S(2)}, u32[]{:S(2)}) %collective-permute-start.17) | collective-permute-done | bytes 393248 | tf_op jit(solution)/shard_map/ppermute | solution.py:29
  80.0 2.1 %collective-permute-start.21 = (bf16[384,384]{1,0:T(8,128)(2,1)S(1)}, bf16[384,384]{1,0:T(8,128)(2,1)S(1)}, u32[]{:S(2)}, u32[]{:S(2)}) collective-permute-start(bf16[384,384]{1,0:T(8,128)(2,1)S(1)} %shard_map.61), channel_id=1, source_target_pairs={{0,4},{4,0},{8,12},{12,8},{16,20},{20,16},{24,28},{28,24},{1,5},{5... | collective-permute-start | bytes 884744 | tf_op jit(solution)/shard_map/ppermute | solution.py:29
  82.1 3.6 %shard_map.62.refs_0_ = f32[384,3072]{1,0:T(8,128)} custom-call(s32[2]{0:T(128)S(1)} %pad_add_fusion.place_ref, bf16[384,1024]{1,0:T(8,128)(2,1)S(1)} %get-tuple-element.29.grad_ref, bf16[256,512]{1,0:T(8,128)(2,1)S(1)} %pad_maximum_fusion.6.refs_0_, bf16[256,512]{1,0:T(8,128)(2,1)S(1)} %collective-permute-done.8.refs_1_, ...), custom_call_target="tpu_custom_call" | custom-call | flops 1610612736 | bytes 3145728 | tf_op jit(solution)/shard_map/pallas_call | solution.py:161
  86.5 1.6 %shard_map.64.refs_0_ = f32[384,3072]{1,0:T(8,128)} custom-call(s32[2]{0:T(128)S(1)} %pad_add_fusion.place_ref, bf16[384,1024]{1,0:T(8,128)(2,1)S(1)} %get-tuple-element.29.grad_ref, f32[384,3072]{1,0:T(8,128)} %shard_map.62.refs_0_, bf16[384,640]{1,0:T(8,128)(2,1)S(1)} %collective-permute-done.20.refs_1_), custom_call_target="tpu_custom_call", output_to_operand_aliasing={{}: (2, {})} | custom-call | bytes 983040 | tf_op jit(solution)/shard_map/pallas_call | solution.py:161
  88.0 3.3 %collective-permute-done.21.refs_1_ = bf16[384,384]{1,0:T(8,128)(2,1)S(1)} collective-permute-done((bf16[384,384]{1,0:T(8,128)(2,1)S(1)}, bf16[384,384]{1,0:T(8,128)(2,1)S(1)}, u32[]{:S(2)}, u32[]{:S(2)}) %collective-permute-start.21) | collective-permute-done | bytes 294944 | tf_op jit(solution)/shard_map/ppermute | solution.py:29
  91.3 1.4 %shard_map.65 = f32[384,3072]{1,0:T(8,128)} custom-call(s32[2]{0:T(128)S(1)} %pad_add_fusion.place_ref, bf16[384,1024]{1,0:T(8,128)(2,1)S(1)} %get-tuple-element.29.grad_ref, f32[384,3072]{1,0:T(8,128)} %shard_map.64.refs_0_, bf16[384,384]{1,0:T(8,128)(2,1)S(1)} %collective-permute-done.21.refs_1_), custom_call_target="tpu_custom_call", output_to_operand_aliasing={{}: (2, {})} | custom-call | bytes 589824 | tf_op jit(solution)/shard_map/pallas_call | solution.py:161
  (58 shorter events, 13.6 us)
Async XLA Ops:
  0.6 9.4 %copy-start.3 = (bf16[32,3072]{1,0:T(8,128)(2,1)S(1)}, bf16[32,3072]{1,0:T(8,128)(2,1)}, u32[]{:S(2)}) copy-start(bf16[32,3072]{1,0:T(8,128)(2,1)} %param.5) | copy-start | bytes 589828
  0.6 22.9 %collective-permute-start = (bf16[32,3072]{1,0:T(8,128)(2,1)}, bf16[32,3072]{1,0:T(8,128)(2,1)S(1)}, u32[]{:S(2)}, u32[]{:S(2)}) collective-permute-start(bf16[32,3072]{1,0:T(8,128)(2,1)} %param.5), channel_id=1, source_target_pairs={{0,2},{1,3},{2,0},{3,1},{4,6},{5,7},{6,4},{7,5},{8,10},{9,11},{10,... | collective-permute-start | bytes 589832 | tf_op jit(solution)/shard_map/ppermute | solution.py:29
  4.8 5.3 %collective-permute-start.3 = (bf16[128,512]{1,0:T(8,128)(2,1)S(1)}, bf16[128,512]{1,0:T(8,128)(2,1)S(1)}, u32[]{:S(2)}, u32[]{:S(2)}) collective-permute-start(bf16[128,512]{1,0:T(8,128)(2,1)S(1)} %get-tuple-element.31), channel_id=1, source_target_pairs={{0,4},{4,0},{8,12},{12,8},{16,20},{20,16},{24,28},{28,24},{1,5},{5... | collective-permute-start | bytes 393224 | tf_op jit(solution)/shard_map/ppermute | solution.py:29
  7.6 16.1 %collective-permute-start.2 = (bf16[128,1024]{1,0:T(8,128)(2,1)S(1)}, bf16[128,1024]{1,0:T(8,128)(2,1)S(1)}, u32[]{:S(2)}, u32[]{:S(2)}) collective-permute-start(bf16[128,1024]{1,0:T(8,128)(2,1)S(1)} %get-tuple-element.33), channel_id=1, source_target_pairs={{0,4},{4,0},{8,12},{12,8},{16,20},{20,16},{24,28},{28,24},{1,5},{5... | collective-permute-start | bytes 786440 | tf_op jit(solution)/shard_map/ppermute | solution.py:29
  10.1 6.1 %collective-permute-start.6 = (bf16[32,768]{1,0:T(8,128)(2,1)S(1)}, bf16[32,768]{1,0:T(8,128)(2,1)S(1)}, u32[]{:S(2)}, u32[]{:S(2)}) collective-permute-start(bf16[32,768]{1,0:T(8,128)(2,1)S(1)} %get-tuple-element.41), channel_id=1, source_target_pairs={{0,24},{4,28},{8,16},{12,20},{16,8},{20,12},{24,0},{28,4},{1,25},{... | collective-permute-start | bytes 147464 | tf_op jit(solution)/shard_map/ppermute | solution.py:29
  13.8 5.1 %collective-permute-start.5 = (bf16[32,768]{1,0:T(8,128)(2,1)S(1)}, bf16[32,768]{1,0:T(8,128)(2,1)S(1)}, u32[]{:S(2)}, u32[]{:S(2)}) collective-permute-start(bf16[32,768]{1,0:T(8,128)(2,1)S(1)} %get-tuple-element.42), channel_id=1, source_target_pairs={{0,16},{4,20},{8,24},{12,28},{16,0},{20,4},{24,8},{28,12},{1,17},{... | collective-permute-start | bytes 147464 | tf_op jit(solution)/shard_map/ppermute | solution.py:29
  13.8 7.0 %collective-permute-start.4 = (bf16[32,768]{1,0:T(8,128)(2,1)S(1)}, bf16[32,768]{1,0:T(8,128)(2,1)S(1)}, u32[]{:S(2)}, u32[]{:S(2)}) collective-permute-start(bf16[32,768]{1,0:T(8,128)(2,1)S(1)} %get-tuple-element.43), channel_id=1, source_target_pairs={{0,8},{4,12},{8,0},{12,4},{16,24},{20,28},{24,16},{28,20},{1,9},{5... | collective-permute-start | bytes 147464 | tf_op jit(solution)/shard_map/ppermute | solution.py:29
  16.2 11.7 %collective-permute-start.9 = (bf16[256,512]{1,0:T(8,128)(2,1)S(1)}, bf16[256,512]{1,0:T(8,128)(2,1)S(1)}, u32[]{:S(2)}, u32[]{:S(2)}) collective-permute-start(bf16[256,512]{1,0:T(8,128)(2,1)S(1)} %pad_maximum_fusion.6.refs_0_), channel_id=1, source_target_pairs={{0,8},{4,12},{8,0},{12,4},{16,24},{20,28},{24,16},{28,20},{1,9},{5... | collective-permute-start | bytes 786440 | tf_op jit(solution)/shard_map/ppermute | solution.py:29
  18.9 12.3 %collective-permute-start.8 = (bf16[256,512]{1,0:T(8,128)(2,1)S(1)}, bf16[256,512]{1,0:T(8,128)(2,1)S(1)}, u32[]{:S(2)}, u32[]{:S(2)}) collective-permute-start(bf16[256,512]{1,0:T(8,128)(2,1)S(1)} %pad_maximum_fusion.6.refs_0_), channel_id=1, source_target_pairs={{0,16},{4,20},{8,24},{12,28},{16,0},{20,4},{24,8},{28,12},{1,17},{... | collective-permute-start | bytes 786440 | tf_op jit(solution)/shard_map/ppermute | solution.py:29
  20.9 6.4 %collective-permute-start.7 = (bf16[4,32,768]{2,1,0:T(8,128)(2,1)S(1)}, bf16[4,32,768]{2,1,0:T(8,128)(2,1)S(1)}, u32[]{:S(2)}, u32[]{:S(2)}) collective-permute-start(bf16[4,32,768]{2,1,0:T(8,128)(2,1)S(1)} %get-tuple-element.39), channel_id=1, source_target_pairs={{0,4},{4,0},{8,12},{12,8},{16,20},{20,16},{24,28},{28,24},{1,5},{5... | collective-permute-start | bytes 589832 | tf_op jit(solution)/shard_map/ppermute | solution.py:29
  23.7 8.4 %collective-permute-start.1 = (bf16[2,32,3072]{2,1,0:T(8,128)(2,1)S(1)}, bf16[2,32,3072]{2,1,0:T(8,128)(2,1)S(1)}, u32[]{:S(2)}, u32[]{:S(2)}) collective-permute-start(bf16[2,32,3072]{2,1,0:T(8,128)(2,1)S(1)} %pad_maximum_fusion.3), channel_id=1, source_target_pairs={{0,1},{1,0},{2,3},{3,2},{4,5},{5,4},{6,7},{7,6},{8,9},{9,8},{10,11... | collective-permute-start | bytes 1179656 | tf_op jit(solution)/shard_map/ppermute | solution.py:29
  23.7 7.5 %copy-start.1 = (bf16[128,1024]{1,0:T(8,128)(2,1)}, bf16[128,1024]{1,0:T(8,128)(2,1)S(1)}, u32[]{:S(2)}) copy-start(bf16[128,1024]{1,0:T(8,128)(2,1)S(1)} %collective-permute-done.2) | copy-start | bytes 786436
  27.3 26.8 %collective-permute-start.13 = (bf16[2,4,32,768]{3,2,1,0:T(8,128)(2,1)S(1)}, bf16[2,4,32,768]{3,2,1,0:T(8,128)(2,1)S(1)}, u32[]{:S(2)}, u32[]{:S(2)}) collective-permute-start(bf16[2,4,32,768]{3,2,1,0:T(8,128)(2,1)S(1)} %pad_maximum_fusion.4.refs_0_), channel_id=1, source_target_pairs={{0,3},{1,2},{2,1},{3,0},{4,7},{5,6},{6,5},{7,4},{8,11},{9,10},{10,... | collective-permute-start | bytes 1179656 | tf_op jit(solution)/shard_map/ppermute | solution.py:29
  27.3 26.7 %collective-permute-start.12 = (bf16[2,4,32,768]{3,2,1,0:T(8,128)(2,1)S(1)}, bf16[2,4,32,768]{3,2,1,0:T(8,128)(2,1)}, u32[]{:S(2)}, u32[]{:S(2)}) collective-permute-start(bf16[2,4,32,768]{3,2,1,0:T(8,128)(2,1)S(1)} %pad_maximum_fusion.4.refs_0_), channel_id=1, source_target_pairs={{0,2},{1,3},{2,0},{3,1},{4,6},{5,7},{6,4},{7,5},{8,10},{9,11},{10,... | collective-permute-start | bytes 1179656 | tf_op jit(solution)/shard_map/ppermute | solution.py:29
  27.9 26.2 %collective-permute-start.11 = (bf16[2,4,32,768]{3,2,1,0:T(8,128)(2,1)S(1)}, bf16[2,4,32,768]{3,2,1,0:T(8,128)(2,1)}, u32[]{:S(2)}, u32[]{:S(2)}) collective-permute-start(bf16[2,4,32,768]{3,2,1,0:T(8,128)(2,1)S(1)} %pad_maximum_fusion.4.refs_0_), channel_id=1, source_target_pairs={{0,1},{1,0},{2,3},{3,2},{4,5},{5,4},{6,7},{7,6},{8,9},{9,8},{10,11... | collective-permute-start | bytes 1179656 | tf_op jit(solution)/shard_map/ppermute | solution.py:29
  32.1 28.7 %collective-permute-start.16 = (bf16[256,1024]{1,0:T(8,128)(2,1)S(1)}, bf16[256,1024]{1,0:T(8,128)(2,1)S(1)}, u32[]{:S(2)}, u32[]{:S(2)}) collective-permute-start(bf16[256,1024]{1,0:T(8,128)(2,1)S(1)} %pad_maximum_fusion.1.refs_0_.refs_4_.refs_8_), channel_id=1, source_target_pairs={{0,16},{4,20},{8,24},{12,28},{16,0},{20,4},{24,8},{28,12},{1,17},{... | collective-permute-start | bytes 1572872 | tf_op jit(solution)/shard_map/ppermute | solution.py:29
  32.1 25.4 %collective-permute-start.10 = (bf16[256,1152]{1,0:T(8,128)(2,1)}, bf16[256,1152]{1,0:T(8,128)(2,1)S(1)}, u32[]{:S(2)}, u32[]{:S(2)}) collective-permute-start(bf16[256,1152]{1,0:T(8,128)(2,1)} %pad_maximum_fusion.2), channel_id=1, source_target_pairs={{0,8},{4,12},{8,0},{12,4},{16,24},{20,28},{24,16},{28,20},{1,9},{5... | collective-permute-start | bytes 1769480 | tf_op jit(solution)/shard_map/ppermute | solution.py:29
  60.7 13.6 %collective-permute-start.14 = (f32[2,32,3072]{2,1,0:T(8,128)S(1)}, f32[2,32,3072]{2,1,0:T(8,128)S(1)}, u32[]{:S(2)}, u32[]{:S(2)}) collective-permute-start(f32[2,32,3072]{2,1,0:T(8,128)S(1)} %select_bitcast_fusion), channel_id=1, source_target_pairs={{0,1},{1,0},{2,3},{3,2},{4,5},{5,4},{6,7},{7,6},{8,9},{9,8},{10,11... | collective-permute-start | bytes 2359304 | tf_op jit(solution)/shard_map/ppermute | solution.py:29
  60.9 10.6 %collective-permute-start.18 = (bf16[256,640]{1,0:T(8,128)(2,1)S(1)}, bf16[256,640]{1,0:T(8,128)(2,1)S(1)}, u32[]{:S(2)}, u32[]{:S(2)}) collective-permute-start(bf16[256,640]{1,0:T(8,128)(2,1)S(1)} %slice.55), channel_id=1, source_target_pairs={{0,8},{4,12},{8,0},{12,4},{16,24},{20,28},{24,16},{28,20},{1,9},{5... | collective-permute-start | bytes 983048 | tf_op jit(solution)/shard_map/ppermute | solution.py:29
  61.1 21.0 %collective-permute-start.19 = (bf16[384,512]{1,0:T(8,128)(2,1)S(1)}, bf16[384,512]{1,0:T(8,128)(2,1)S(1)}, u32[]{:S(2)}, u32[]{:S(2)}) collective-permute-start(bf16[384,512]{1,0:T(8,128)(2,1)S(1)} %shard_map.60), channel_id=1, source_target_pairs={{0,4},{4,0},{8,12},{12,8},{16,20},{20,16},{24,28},{28,24},{1,5},{5... | collective-permute-start | bytes 1179656 | tf_op jit(solution)/shard_map/ppermute | solution.py:29
  63.2 16.2 %collective-permute-start.17 = (bf16[512,384]{1,0:T(8,128)(2,1)S(1)}, bf16[512,384]{1,0:T(8,128)(2,1)S(1)}, u32[]{:S(2)}, u32[]{:S(2)}) collective-permute-start(bf16[512,384]{1,0:T(8,128)(2,1)S(1)} %pad_maximum_fusion.5), channel_id=1, source_target_pairs={{0,8},{4,12},{8,0},{12,4},{16,24},{20,28},{24,16},{28,20},{1,9},{5... | collective-permute-start | bytes 1179656 | tf_op jit(solution)/shard_map/ppermute | solution.py:29
  72.2 14.2 %collective-permute-start.20 = (bf16[384,640]{1,0:T(8,128)(2,1)S(1)}, bf16[384,640]{1,0:T(8,128)(2,1)S(1)}, u32[]{:S(2)}, u32[]{:S(2)}) collective-permute-start(bf16[384,640]{1,0:T(8,128)(2,1)S(1)} %shard_map.63), channel_id=1, source_target_pairs={{0,4},{4,0},{8,12},{12,8},{16,20},{20,16},{24,28},{28,24},{1,5},{5... | collective-permute-start | bytes 1474568 | tf_op jit(solution)/shard_map/ppermute | solution.py:29
  74.5 18.2 %collective-permute-start.15 = (f32[32,3072]{1,0:T(8,128)S(1)}, f32[32,3072]{1,0:T(8,128)S(1)}, u32[]{:S(2)}, u32[]{:S(2)}) collective-permute-start(f32[32,3072]{1,0:T(8,128)S(1)} %select_bitcast_fusion.1), channel_id=1, source_target_pairs={{0,2},{1,3},{2,0},{3,1},{4,6},{5,7},{6,4},{7,5},{8,10},{9,11},{10,... | collective-permute-start | bytes 1179656 | tf_op jit(solution)/shard_map/ppermute | solution.py:29
  80.0 11.3 %collective-permute-start.21 = (bf16[384,384]{1,0:T(8,128)(2,1)S(1)}, bf16[384,384]{1,0:T(8,128)(2,1)S(1)}, u32[]{:S(2)}, u32[]{:S(2)}) collective-permute-start(bf16[384,384]{1,0:T(8,128)(2,1)S(1)} %shard_map.61), channel_id=1, source_target_pairs={{0,4},{4,0},{8,12},{12,8},{16,20},{20,16},{24,28},{28,24},{1,5},{5... | collective-permute-start | bytes 884744 | tf_op jit(solution)/shard_map/ppermute | solution.py:29
  (2 other events, 2.6 us)

commit v5 on v4

--- a/solution.py
+++ b/solution.py
@@ -204,7 +204,7 @@
     far0 = xor_permute(own0, "dp", 4)
     near0 = xor_permute(own0, "dp", 2)
 
-    other = xor_permute(out_grad, "tensor", 2)
+    other = xor_permute(after(out_grad, sent0), "tensor", 2)
     rows_y = jnp.stack([either(y, out_grad, other), either(y, other, out_grad)])
     other = xor_permute(rows_y, "tensor", 1)
     group = jnp.stack([either(core, rows_y, other), either(core, other, rows_y)], axis=1).reshape(tokens, width)
@@ -253,8 +253,9 @@
 
     result = write_columns(place, None, after(mine, their2), products, backs[:1], units, scale)
     result = write_columns(place, result, mine, [], backs[1:2], units, scale)
-    result = write_columns(place, result, mine, [], backs[2:], units, scale)
-    return (in_grad.astype(BF16), result)
+    in_grad = in_grad.astype(BF16)
+    result = write_columns(place, after(result, in_grad), mine, [], backs[2:], units, scale)
+    return (in_grad, result)
 
 
 def solution(mesh):

time: 93.7 us -> 91.5 us (0.977)
  waiting for transfers between devices: 29.3 us -> 26.2 us
    ppermute x22, waiting for transfers between devices: 29.3 us -> 26.2 us  [xor_permute(): return lax.ppermute(value, axis, [(i, i ^ mask) for i in range(count)])]
  transfers between devices with their start and end apart: 22 -> 22, of which waited for: 10 -> 10; matrix products, arithmetic and copies ran while one was open for 26% -> 26% of each run, Pallas kernels for 11% -> 10%
where the time goes in v5:
time: 91.5 us; the launch traced here: 91.3 us
  starting transfers between devices  28 us (31%)
  waiting for transfers between devices  26.2 us (29%)
  matrix products  19.4 us (21%)
  Pallas kernels  10.2 us (11%)
  other arithmetic  5.7 us (6%)
    ppermute x22, starting transfers between devices, xor_permute(): return lax.ppermute(value, axis, [(i, i ^ mask) for i in range(count)])  28 us
    ppermute x22, waiting for transfers between devices, xor_permute(): return lax.ppermute(value, axis, [(i, i ^ mask) for i in range(count)])  26.2 us
    dot_general x1, matrix products, plane_plan(): lax.dot_general(pre_grad, w_up, (((1,), (1,)), ((), ())), preferred_eleme...  19.4 us
    pallas_call x3, Pallas kernels, write_columns(): pl.pallas_call(body, in_specs=[pl.BlockSpec(memory_space=pltpu.SMEM), who...  6.59 us
    convert_element_type x2, other arithmetic, gelu_value_of(): return (pre_float * normal_cdf).astype(BF16)  2.44 us
    pallas_call x3, Pallas kernels, their_product(): pl.pallas_call(body, in_specs=[whole()] * (1 + len(pieces)), out_specs=wh...  1.93 us
  transfers between devices with their start and end apart: 22, of which 10 were waited for; matrix products, arithmetic and copies ran while one was open for 26% of the time, Pallas kernels for 10%

profile of v5, /device:TPU:0, one launch (start us, length us, event | category | flops | bytes accessed | tf_op | source)
XLA Modules:
  0.0 91.3 jit_solution(5627499995397570884)
XLA Ops:
  1.8 3.0 %collective-permute-start.3 = (bf16[128,512]{1,0:T(8,128)(2,1)S(1)}, bf16[128,512]{1,0:T(8,128)(2,1)S(1)}, u32[]{:S(2)}, u32[]{:S(2)}) collective-permute-start(bf16[128,512]{1,0:T(8,128)(2,1)S(1)} %get-tuple-element.35), channel_id=1, source_target_pairs={{0,4},{4,0},{8,12},{12,8},{16,20},{20,16},{24,28},{28,24},{1,5},{5... | collective-permute-start | bytes 393224 | tf_op jit(solution)/shard_map/ppermute | solution.py:29
  4.8 1.5 %collective-permute-start = (bf16[32,3072]{1,0:T(8,128)(2,1)}, bf16[32,3072]{1,0:T(8,128)(2,1)S(1)}, u32[]{:S(2)}, u32[]{:S(2)}) collective-permute-start(bf16[32,3072]{1,0:T(8,128)(2,1)} %param.5), channel_id=1, source_target_pairs={{0,2},{1,3},{2,0},{3,1},{4,6},{5,7},{6,4},{7,5},{8,10},{9,11},{10,... | collective-permute-start | bytes 589832 | tf_op jit(solution)/shard_map/ppermute | solution.py:29
  8.4 3.9 %collective-permute-start.6 = (bf16[32,768]{1,0:T(8,128)(2,1)S(1)}, bf16[32,768]{1,0:T(8,128)(2,1)S(1)}, u32[]{:S(2)}, u32[]{:S(2)}) collective-permute-start(bf16[32,768]{1,0:T(8,128)(2,1)S(1)} %get-tuple-element.45), channel_id=1, source_target_pairs={{0,24},{4,28},{8,16},{12,20},{16,8},{20,12},{24,0},{28,4},{1,25},{... | collective-permute-start | bytes 147464 | tf_op jit(solution)/shard_map/ppermute | solution.py:29
  13.0 1.6 %collective-permute-done.6 = bf16[32,768]{1,0:T(8,128)(2,1)S(1)} collective-permute-done((bf16[32,768]{1,0:T(8,128)(2,1)S(1)}, bf16[32,768]{1,0:T(8,128)(2,1)S(1)}, u32[]{:S(2)}, u32[]{:S(2)}) %collective-permute-start.6) | collective-permute-done | bytes 49184 | tf_op jit(solution)/shard_map/ppermute | solution.py:29
  15.7 1.7 %collective-permute-done.5 = bf16[32,768]{1,0:T(8,128)(2,1)S(1)} collective-permute-done((bf16[32,768]{1,0:T(8,128)(2,1)S(1)}, bf16[32,768]{1,0:T(8,128)(2,1)S(1)}, u32[]{:S(2)}, u32[]{:S(2)}) %collective-permute-start.5) | collective-permute-done | bytes 49184 | tf_op jit(solution)/shard_map/ppermute | solution.py:29
  17.4 1.9 %collective-permute-start.8 = (bf16[256,512]{1,0:T(8,128)(2,1)S(1)}, bf16[256,512]{1,0:T(8,128)(2,1)S(1)}, u32[]{:S(2)}, u32[]{:S(2)}) collective-permute-start(bf16[256,512]{1,0:T(8,128)(2,1)S(1)} %pad_maximum_fusion.6.refs_0_), channel_id=1, source_target_pairs={{0,16},{4,20},{8,24},{12,28},{16,0},{20,4},{24,8},{28,12},{1,17},{... | collective-permute-start | bytes 786440 | tf_op jit(solution)/shard_map/ppermute | solution.py:29
  19.4 1.6 %collective-permute-start.7 = (bf16[4,32,768]{2,1,0:T(8,128)(2,1)S(1)}, bf16[4,32,768]{2,1,0:T(8,128)(2,1)S(1)}, u32[]{:S(2)}, u32[]{:S(2)}) collective-permute-start(bf16[4,32,768]{2,1,0:T(8,128)(2,1)S(1)} %get-tuple-element.43), channel_id=1, source_target_pairs={{0,4},{4,0},{8,12},{12,8},{16,20},{20,16},{24,28},{28,24},{1,5},{5... | collective-permute-start | bytes 589832 | tf_op jit(solution)/shard_map/ppermute | solution.py:29
  21.2 3.9 %collective-permute-done.7 = bf16[4,32,768]{2,1,0:T(8,128)(2,1)S(1)} collective-permute-done((bf16[4,32,768]{2,1,0:T(8,128)(2,1)S(1)}, bf16[4,32,768]{2,1,0:T(8,128)(2,1)S(1)}, u32[]{:S(2)}, u32[]{:S(2)}) %collective-permute-start.7) | collective-permute-done | bytes 196640 | tf_op jit(solution)/shard_map/ppermute | solution.py:29
  25.3 2.1 %collective-permute-start.12 = (bf16[2,4,32,768]{3,2,1,0:T(8,128)(2,1)S(1)}, bf16[2,4,32,768]{3,2,1,0:T(8,128)(2,1)}, u32[]{:S(2)}, u32[]{:S(2)}) collective-permute-start(bf16[2,4,32,768]{3,2,1,0:T(8,128)(2,1)S(1)} %pad_maximum_fusion.4.refs_0_), channel_id=1, source_target_pairs={{0,2},{1,3},{2,0},{3,1},{4,6},{5,7},{6,4},{7,5},{8,10},{9,11},{10,... | collective-permute-start | bytes 1179656 | tf_op jit(solution)/shard_map/ppermute | solution.py:29
  27.4 2.6 %collective-permute-done.8.refs_1_ = bf16[256,512]{1,0:T(8,128)(2,1)S(1)} collective-permute-done((bf16[256,512]{1,0:T(8,128)(2,1)S(1)}, bf16[256,512]{1,0:T(8,128)(2,1)S(1)}, u32[]{:S(2)}, u32[]{:S(2)}) %collective-permute-start.8) | collective-permute-done | bytes 262176 | tf_op jit(solution)/shard_map/ppermute | solution.py:29
  30.9 1.7 %collective-permute-start.10 = (bf16[256,1152]{1,0:T(8,128)(2,1)}, bf16[256,1152]{1,0:T(8,128)(2,1)S(1)}, u32[]{:S(2)}, u32[]{:S(2)}) collective-permute-start(bf16[256,1152]{1,0:T(8,128)(2,1)} %pad_maximum_fusion.2), channel_id=1, source_target_pairs={{0,8},{4,12},{8,0},{12,4},{16,24},{20,28},{24,16},{28,20},{1,9},{5... | collective-permute-start | bytes 1769480 | tf_op jit(solution)/shard_map/ppermute | solution.py:29
  33.6 19.4 %fusion.7 = f32[128,3072]{1,0:T(8,128)} fusion(bf16[3072,3072]{1,0:T(8,128)(2,1)} %param.6, bf16[128,3072]{1,0:T(8,128)(2,1)} %bitcast.49, bf16[3072,3072]{1,0:T(8,128)(2,1)} %param.7, bf16[128,3072]{1,0:T(8,128)(2,1)} %param.4), kind=kOutput, calls=%fused_computation.26 | convolution fusion | flops 4836163584 | bytes 40894464 | tf_op jit(solution)/shard_map/dot_general | solution.py:229
  53.0 3.1 %collective-permute-done.10.refs_3_.refs_6_.refs_2_ = bf16[256,1152]{1,0:T(8,128)(2,1)S(1)} collective-permute-done((bf16[256,1152]{1,0:T(8,128)(2,1)}, bf16[256,1152]{1,0:T(8,128)(2,1)S(1)}, u32[]{:S(2)}, u32[]{:S(2)}) %collective-permute-start.10) | collective-permute-done | bytes 589856 | tf_op jit(solution)/shard_map/ppermute | solution.py:29
  56.1 1.7 %shard_map.59 = (bf16[384,1024]{1,0:T(8,128)(2,1)S(1)}, bf16[384,1024]{1,0:T(8,128)(2,1)S(1)}) custom-call(s32[2]{0:T(128)S(1)} %pad_add_fusion.place_ref, bf16[2,4,32,768]{3,2,1,0:T(8,128)(2,1)S(1)} %pad_maximum_fusion.4.refs_0_, bf16[2,4,32,768]{3,2,1,0:T(8,128)(2,1)} %collective-permute-done.11.refs_1_, ...), custom_call_target="tpu_custom_call" | custom-call | bytes 6291456 | tf_op jit(solution)/shard_map/pallas_call | solution.py:91
  59.7 2.1 %collective-permute-start.19 = (bf16[384,512]{1,0:T(8,128)(2,1)S(1)}, bf16[384,512]{1,0:T(8,128)(2,1)S(1)}, u32[]{:S(2)}, u32[]{:S(2)}) collective-permute-start(bf16[384,512]{1,0:T(8,128)(2,1)S(1)} %shard_map.60), channel_id=1, source_target_pairs={{0,4},{4,0},{8,12},{12,8},{16,20},{20,16},{24,28},{28,24},{1,5},{5... | collective-permute-start | bytes 1179656 | tf_op jit(solution)/shard_map/ppermute | solution.py:29
  61.8 2.0 %collective-permute-start.17 = (bf16[512,384]{1,0:T(8,128)(2,1)S(1)}, bf16[512,384]{1,0:T(8,128)(2,1)S(1)}, u32[]{:S(2)}, u32[]{:S(2)}) collective-permute-start(bf16[512,384]{1,0:T(8,128)(2,1)S(1)} %pad_maximum_fusion.5), channel_id=1, source_target_pairs={{0,8},{4,12},{8,0},{12,4},{16,24},{20,28},{24,16},{28,20},{1,9},{5... | collective-permute-start | bytes 1179656 | tf_op jit(solution)/shard_map/ppermute | solution.py:29
  63.8 6.2 %collective-permute-done.18.refs_7_.refs_3_ = bf16[256,640]{1,0:T(8,128)(2,1)S(1)} collective-permute-done((bf16[256,640]{1,0:T(8,128)(2,1)S(1)}, bf16[256,640]{1,0:T(8,128)(2,1)S(1)}, u32[]{:S(2)}, u32[]{:S(2)}) %collective-permute-start.18) | collective-permute-done | bytes 327712 | tf_op jit(solution)/shard_map/ppermute | solution.py:29
  70.8 2.1 %collective-permute-start.20 = (bf16[384,640]{1,0:T(8,128)(2,1)S(1)}, bf16[384,640]{1,0:T(8,128)(2,1)S(1)}, u32[]{:S(2)}, u32[]{:S(2)}) collective-permute-start(bf16[384,640]{1,0:T(8,128)(2,1)S(1)} %shard_map.63), channel_id=1, source_target_pairs={{0,4},{4,0},{8,12},{12,8},{16,20},{20,16},{24,28},{28,24},{1,5},{5... | collective-permute-start | bytes 1474568 | tf_op jit(solution)/shard_map/ppermute | solution.py:29
  74.4 3.6 %collective-permute-done.17.refs_2_.refs_10_ = bf16[512,384]{1,0:T(8,128)(2,1)S(1)} collective-permute-done((bf16[512,384]{1,0:T(8,128)(2,1)S(1)}, bf16[512,384]{1,0:T(8,128)(2,1)S(1)}, u32[]{:S(2)}, u32[]{:S(2)}) %collective-permute-start.17) | collective-permute-done | bytes 393248 | tf_op jit(solution)/shard_map/ppermute | solution.py:29
  78.6 2.1 %collective-permute-start.21 = (bf16[384,384]{1,0:T(8,128)(2,1)S(1)}, bf16[384,384]{1,0:T(8,128)(2,1)S(1)}, u32[]{:S(2)}, u32[]{:S(2)}) collective-permute-start(bf16[384,384]{1,0:T(8,128)(2,1)S(1)} %shard_map.61), channel_id=1, source_target_pairs={{0,4},{4,0},{8,12},{12,8},{16,20},{20,16},{24,28},{28,24},{1,5},{5... | collective-permute-start | bytes 884744 | tf_op jit(solution)/shard_map/ppermute | solution.py:29
  80.7 3.6 %shard_map.62.refs_0_ = f32[384,3072]{1,0:T(8,128)} custom-call(s32[2]{0:T(128)S(1)} %pad_add_fusion.place_ref, bf16[384,1024]{1,0:T(8,128)(2,1)S(1)} %get-tuple-element.32.grad_ref, bf16[256,512]{1,0:T(8,128)(2,1)S(1)} %pad_maximum_fusion.6.refs_0_, bf16[256,512]{1,0:T(8,128)(2,1)S(1)} %collective-permute-done.8.refs_1_, ...), custom_call_target="tpu_custom_call" | custom-call | flops 1610612736 | bytes 3145728 | tf_op jit(solution)/shard_map/pallas_call | solution.py:161
  85.0 1.6 %shard_map.64.refs_0_ = f32[384,3072]{1,0:T(8,128)} custom-call(s32[2]{0:T(128)S(1)} %pad_add_fusion.place_ref, bf16[384,1024]{1,0:T(8,128)(2,1)S(1)} %get-tuple-element.32.grad_ref, f32[384,3072]{1,0:T(8,128)} %shard_map.62.refs_0_, bf16[384,640]{1,0:T(8,128)(2,1)S(1)} %collective-permute-done.20.refs_1_), custom_call_target="tpu_custom_call", output_to_operand_aliasing={{}: (2, {})} | custom-call | bytes 983040 | tf_op jit(solution)/shard_map/pallas_call | solution.py:161
  87.3 2.6 %collective-permute-done.21.refs_1_ = bf16[384,384]{1,0:T(8,128)(2,1)S(1)} collective-permute-done((bf16[384,384]{1,0:T(8,128)(2,1)S(1)}, bf16[384,384]{1,0:T(8,128)(2,1)S(1)}, u32[]{:S(2)}, u32[]{:S(2)}) %collective-permute-start.21) | collective-permute-done | bytes 294944 | tf_op jit(solution)/shard_map/ppermute | solution.py:29
  89.9 1.4 %shard_map.65 = f32[384,3072]{1,0:T(8,128)} custom-call(s32[2]{0:T(128)S(1)} %pad_add_fusion.place_ref, bf16[384,1024]{1,0:T(8,128)(2,1)S(1)} %get-tuple-element.32.grad_ref, f32[384,3072]{1,0:T(8,128)} %shard_map.64.refs_0_, bf16[384,384]{1,0:T(8,128)(2,1)S(1)} %collective-permute-done.21.refs_1_), custom_call_target="tpu_custom_call", output_to_operand_aliasing={{}: (2, {})} | custom-call | bytes 589824 | tf_op jit(solution)/shard_map/pallas_call | solution.py:161
  (58 shorter events, 13.4 us)
Async XLA Ops:
  0.6 7.7 %copy-start.3 = (bf16[32,3072]{1,0:T(8,128)(2,1)S(1)}, bf16[32,3072]{1,0:T(8,128)(2,1)}, u32[]{:S(2)}) copy-start(bf16[32,3072]{1,0:T(8,128)(2,1)} %param.5) | copy-start | bytes 589828
  1.8 6.5 %collective-permute-start.3 = (bf16[128,512]{1,0:T(8,128)(2,1)S(1)}, bf16[128,512]{1,0:T(8,128)(2,1)S(1)}, u32[]{:S(2)}, u32[]{:S(2)}) collective-permute-start(bf16[128,512]{1,0:T(8,128)(2,1)S(1)} %get-tuple-element.35), channel_id=1, source_target_pairs={{0,4},{4,0},{8,12},{12,8},{16,20},{20,16},{24,28},{28,24},{1,5},{5... | collective-permute-start | bytes 393224 | tf_op jit(solution)/shard_map/ppermute | solution.py:29
  4.8 16.1 %collective-permute-start = (bf16[32,3072]{1,0:T(8,128)(2,1)}, bf16[32,3072]{1,0:T(8,128)(2,1)S(1)}, u32[]{:S(2)}, u32[]{:S(2)}) collective-permute-start(bf16[32,3072]{1,0:T(8,128)(2,1)} %param.5), channel_id=1, source_target_pairs={{0,2},{1,3},{2,0},{3,1},{4,6},{5,7},{6,4},{7,5},{8,10},{9,11},{10,... | collective-permute-start | bytes 589832 | tf_op jit(solution)/shard_map/ppermute | solution.py:29
  7.6 13.5 %collective-permute-start.2 = (bf16[128,1024]{1,0:T(8,128)(2,1)S(1)}, bf16[128,1024]{1,0:T(8,128)(2,1)S(1)}, u32[]{:S(2)}, u32[]{:S(2)}) collective-permute-start(bf16[128,1024]{1,0:T(8,128)(2,1)S(1)} %get-tuple-element.37), channel_id=1, source_target_pairs={{0,4},{4,0},{8,12},{12,8},{16,20},{20,16},{24,28},{28,24},{1,5},{5... | collective-permute-start | bytes 786440 | tf_op jit(solution)/shard_map/ppermute | solution.py:29
  8.4 6.2 %collective-permute-start.6 = (bf16[32,768]{1,0:T(8,128)(2,1)S(1)}, bf16[32,768]{1,0:T(8,128)(2,1)S(1)}, u32[]{:S(2)}, u32[]{:S(2)}) collective-permute-start(bf16[32,768]{1,0:T(8,128)(2,1)S(1)} %get-tuple-element.45), channel_id=1, source_target_pairs={{0,24},{4,28},{8,16},{12,20},{16,8},{20,12},{24,0},{28,4},{1,25},{... | collective-permute-start | bytes 147464 | tf_op jit(solution)/shard_map/ppermute | solution.py:29
  12.3 5.1 %collective-permute-start.5 = (bf16[32,768]{1,0:T(8,128)(2,1)S(1)}, bf16[32,768]{1,0:T(8,128)(2,1)S(1)}, u32[]{:S(2)}, u32[]{:S(2)}) collective-permute-start(bf16[32,768]{1,0:T(8,128)(2,1)S(1)} %get-tuple-element.46), channel_id=1, source_target_pairs={{0,16},{4,20},{8,24},{12,28},{16,0},{20,4},{24,8},{28,12},{1,17},{... | collective-permute-start | bytes 147464 | tf_op jit(solution)/shard_map/ppermute | solution.py:29
  12.3 7.0 %collective-permute-start.4 = (bf16[32,768]{1,0:T(8,128)(2,1)S(1)}, bf16[32,768]{1,0:T(8,128)(2,1)S(1)}, u32[]{:S(2)}, u32[]{:S(2)}) collective-permute-start(bf16[32,768]{1,0:T(8,128)(2,1)S(1)} %get-tuple-element.47), channel_id=1, source_target_pairs={{0,8},{4,12},{8,0},{12,4},{16,24},{20,28},{24,16},{28,20},{1,9},{5... | collective-permute-start | bytes 147464 | tf_op jit(solution)/shard_map/ppermute | solution.py:29
  14.6 12.7 %collective-permute-start.9 = (bf16[256,512]{1,0:T(8,128)(2,1)S(1)}, bf16[256,512]{1,0:T(8,128)(2,1)S(1)}, u32[]{:S(2)}, u32[]{:S(2)}) collective-permute-start(bf16[256,512]{1,0:T(8,128)(2,1)S(1)} %pad_maximum_fusion.6.refs_0_), channel_id=1, source_target_pairs={{0,8},{4,12},{8,0},{12,4},{16,24},{20,28},{24,16},{28,20},{1,9},{5... | collective-permute-start | bytes 786440 | tf_op jit(solution)/shard_map/ppermute | solution.py:29
  17.4 12.6 %collective-permute-start.8 = (bf16[256,512]{1,0:T(8,128)(2,1)S(1)}, bf16[256,512]{1,0:T(8,128)(2,1)S(1)}, u32[]{:S(2)}, u32[]{:S(2)}) collective-permute-start(bf16[256,512]{1,0:T(8,128)(2,1)S(1)} %pad_maximum_fusion.6.refs_0_), channel_id=1, source_target_pairs={{0,16},{4,20},{8,24},{12,28},{16,0},{20,4},{24,8},{28,12},{1,17},{... | collective-permute-start | bytes 786440 | tf_op jit(solution)/shard_map/ppermute | solution.py:29
  19.4 5.7 %collective-permute-start.7 = (bf16[4,32,768]{2,1,0:T(8,128)(2,1)S(1)}, bf16[4,32,768]{2,1,0:T(8,128)(2,1)S(1)}, u32[]{:S(2)}, u32[]{:S(2)}) collective-permute-start(bf16[4,32,768]{2,1,0:T(8,128)(2,1)S(1)} %get-tuple-element.43), channel_id=1, source_target_pairs={{0,4},{4,0},{8,12},{12,8},{16,20},{20,16},{24,28},{28,24},{1,5},{5... | collective-permute-start | bytes 589832 | tf_op jit(solution)/shard_map/ppermute | solution.py:29
  21.0 9.9 %collective-permute-start.1 = (bf16[2,32,3072]{2,1,0:T(8,128)(2,1)S(1)}, bf16[2,32,3072]{2,1,0:T(8,128)(2,1)S(1)}, u32[]{:S(2)}, u32[]{:S(2)}) collective-permute-start(bf16[2,32,3072]{2,1,0:T(8,128)(2,1)S(1)} %pad_maximum_fusion.3), channel_id=1, source_target_pairs={{0,1},{1,0},{2,3},{3,2},{4,5},{5,4},{6,7},{7,6},{8,9},{9,8},{10,11... | collective-permute-start | bytes 1179656 | tf_op jit(solution)/shard_map/ppermute | solution.py:29
  21.1 8.9 %copy-start.1 = (bf16[128,1024]{1,0:T(8,128)(2,1)}, bf16[128,1024]{1,0:T(8,128)(2,1)S(1)}, u32[]{:S(2)}) copy-start(bf16[128,1024]{1,0:T(8,128)(2,1)S(1)} %collective-permute-done.2) | copy-start | bytes 786436
  25.2 27.8 %collective-permute-start.13 = (bf16[2,4,32,768]{3,2,1,0:T(8,128)(2,1)S(1)}, bf16[2,4,32,768]{3,2,1,0:T(8,128)(2,1)S(1)}, u32[]{:S(2)}, u32[]{:S(2)}) collective-permute-start(bf16[2,4,32,768]{3,2,1,0:T(8,128)(2,1)S(1)} %pad_maximum_fusion.4.refs_0_), channel_id=1, source_target_pairs={{0,3},{1,2},{2,1},{3,0},{4,7},{5,6},{6,5},{7,4},{8,11},{9,10},{10,... | collective-permute-start | bytes 1179656 | tf_op jit(solution)/shard_map/ppermute | solution.py:29
  25.3 27.7 %collective-permute-start.12 = (bf16[2,4,32,768]{3,2,1,0:T(8,128)(2,1)S(1)}, bf16[2,4,32,768]{3,2,1,0:T(8,128)(2,1)}, u32[]{:S(2)}, u32[]{:S(2)}) collective-permute-start(bf16[2,4,32,768]{3,2,1,0:T(8,128)(2,1)S(1)} %pad_maximum_fusion.4.refs_0_), channel_id=1, source_target_pairs={{0,2},{1,3},{2,0},{3,1},{4,6},{5,7},{6,4},{7,5},{8,10},{9,11},{10,... | collective-permute-start | bytes 1179656 | tf_op jit(solution)/shard_map/ppermute | solution.py:29
  27.3 25.7 %collective-permute-start.11 = (bf16[2,4,32,768]{3,2,1,0:T(8,128)(2,1)S(1)}, bf16[2,4,32,768]{3,2,1,0:T(8,128)(2,1)}, u32[]{:S(2)}, u32[]{:S(2)}) collective-permute-start(bf16[2,4,32,768]{3,2,1,0:T(8,128)(2,1)S(1)} %pad_maximum_fusion.4.refs_0_), channel_id=1, source_target_pairs={{0,1},{1,0},{2,3},{3,2},{4,5},{5,4},{6,7},{7,6},{8,9},{9,8},{10,11... | collective-permute-start | bytes 1179656 | tf_op jit(solution)/shard_map/ppermute | solution.py:29
  30.9 28.5 %collective-permute-start.16 = (bf16[256,1024]{1,0:T(8,128)(2,1)S(1)}, bf16[256,1024]{1,0:T(8,128)(2,1)S(1)}, u32[]{:S(2)}, u32[]{:S(2)}) collective-permute-start(bf16[256,1024]{1,0:T(8,128)(2,1)S(1)} %pad_maximum_fusion.1.refs_0_.refs_4_.refs_8_), channel_id=1, source_target_pairs={{0,16},{4,20},{8,24},{12,28},{16,0},{20,4},{24,8},{28,12},{1,17},{... | collective-permute-start | bytes 1572872 | tf_op jit(solution)/shard_map/ppermute | solution.py:29
  30.9 25.2 %collective-permute-start.10 = (bf16[256,1152]{1,0:T(8,128)(2,1)}, bf16[256,1152]{1,0:T(8,128)(2,1)S(1)}, u32[]{:S(2)}, u32[]{:S(2)}) collective-permute-start(bf16[256,1152]{1,0:T(8,128)(2,1)} %pad_maximum_fusion.2), channel_id=1, source_target_pairs={{0,8},{4,12},{8,0},{12,4},{16,24},{20,28},{24,16},{28,20},{1,9},{5... | collective-permute-start | bytes 1769480 | tf_op jit(solution)/shard_map/ppermute | solution.py:29
  59.3 13.6 %collective-permute-start.14 = (f32[2,32,3072]{2,1,0:T(8,128)S(1)}, f32[2,32,3072]{2,1,0:T(8,128)S(1)}, u32[]{:S(2)}, u32[]{:S(2)}) collective-permute-start(f32[2,32,3072]{2,1,0:T(8,128)S(1)} %select_bitcast_fusion), channel_id=1, source_target_pairs={{0,1},{1,0},{2,3},{3,2},{4,5},{5,4},{6,7},{7,6},{8,9},{9,8},{10,11... | collective-permute-start | bytes 2359304 | tf_op jit(solution)/shard_map/ppermute | solution.py:29
  59.4 10.6 %collective-permute-start.18 = (bf16[256,640]{1,0:T(8,128)(2,1)S(1)}, bf16[256,640]{1,0:T(8,128)(2,1)S(1)}, u32[]{:S(2)}, u32[]{:S(2)}) collective-permute-start(bf16[256,640]{1,0:T(8,128)(2,1)S(1)} %slice.55), channel_id=1, source_target_pairs={{0,8},{4,12},{8,0},{12,4},{16,24},{20,28},{24,16},{28,20},{1,9},{5... | collective-permute-start | bytes 983048 | tf_op jit(solution)/shard_map/ppermute | solution.py:29
  59.7 21.0 %collective-permute-start.19 = (bf16[384,512]{1,0:T(8,128)(2,1)S(1)}, bf16[384,512]{1,0:T(8,128)(2,1)S(1)}, u32[]{:S(2)}, u32[]{:S(2)}) collective-permute-start(bf16[384,512]{1,0:T(8,128)(2,1)S(1)} %shard_map.60), channel_id=1, source_target_pairs={{0,4},{4,0},{8,12},{12,8},{16,20},{20,16},{24,28},{28,24},{1,5},{5... | collective-permute-start | bytes 1179656 | tf_op jit(solution)/shard_map/ppermute | solution.py:29
  61.8 16.2 %collective-permute-start.17 = (bf16[512,384]{1,0:T(8,128)(2,1)S(1)}, bf16[512,384]{1,0:T(8,128)(2,1)S(1)}, u32[]{:S(2)}, u32[]{:S(2)}) collective-permute-start(bf16[512,384]{1,0:T(8,128)(2,1)S(1)} %pad_maximum_fusion.5), channel_id=1, source_target_pairs={{0,8},{4,12},{8,0},{12,4},{16,24},{20,28},{24,16},{28,20},{1,9},{5... | collective-permute-start | bytes 1179656 | tf_op jit(solution)/shard_map/ppermute | solution.py:29
  70.8 14.2 %collective-permute-start.20 = (bf16[384,640]{1,0:T(8,128)(2,1)S(1)}, bf16[384,640]{1,0:T(8,128)(2,1)S(1)}, u32[]{:S(2)}, u32[]{:S(2)}) collective-permute-start(bf16[384,640]{1,0:T(8,128)(2,1)S(1)} %shard_map.63), channel_id=1, source_target_pairs={{0,4},{4,0},{8,12},{12,8},{16,20},{20,16},{24,28},{28,24},{1,5},{5... | collective-permute-start | bytes 1474568 | tf_op jit(solution)/shard_map/ppermute | solution.py:29
  73.1 13.5 %collective-permute-start.15 = (f32[32,3072]{1,0:T(8,128)S(1)}, f32[32,3072]{1,0:T(8,128)S(1)}, u32[]{:S(2)}, u32[]{:S(2)}) collective-permute-start(f32[32,3072]{1,0:T(8,128)S(1)} %select_bitcast_fusion.1), channel_id=1, source_target_pairs={{0,2},{1,3},{2,0},{3,1},{4,6},{5,7},{6,4},{7,5},{8,10},{9,11},{10,... | collective-permute-start | bytes 1179656 | tf_op jit(solution)/shard_map/ppermute | solution.py:29
  78.6 11.3 %collective-permute-start.21 = (bf16[384,384]{1,0:T(8,128)(2,1)S(1)}, bf16[384,384]{1,0:T(8,128)(2,1)S(1)}, u32[]{:S(2)}, u32[]{:S(2)}) collective-permute-start(bf16[384,384]{1,0:T(8,128)(2,1)S(1)} %shard_map.61), channel_id=1, source_target_pairs={{0,4},{4,0},{8,12},{12,8},{16,20},{20,16},{24,28},{28,24},{1,5},{5... | collective-permute-start | bytes 884744 | tf_op jit(solution)/shard_map/ppermute | solution.py:29
  (2 other events, 2.6 us)

commit v6 on v5

--- a/solution.py
+++ b/solution.py
@@ -186,8 +186,8 @@
     half = units // 2
     pair = width // 4
     scale = 1.0 / math.sqrt(tokens * 8)
-    head = half // 3
-    tail = half // 4
+    head = half // 4
+    tail = half // 3
     middle = half - head - tail
 
     def columns(pre, bit, offset, size):

time: 91.5 us -> 89 us (0.973)
  starting transfers between devices: 28 us -> 26.3 us
    ppermute x22, starting transfers between devices: 28 us -> 26.3 us  [xor_permute(): return lax.ppermute(value, axis, [(i, i ^ mask) for i in range(count)])]
  transfers between devices with their start and end apart: 22 -> 22, of which waited for: 10 -> 7; matrix products, arithmetic and copies ran while one was open for 26% -> 27% of each run, Pallas kernels for 10% -> 10%
where the time goes in v6:
time: 89 us; the launch traced here: 88.8 us
  starting transfers between devices  26.3 us (30%)
  waiting for transfers between devices  25.5 us (29%)
  matrix products  19.4 us (22%)
  Pallas kernels  10.3 us (12%)
  other arithmetic  5.72 us (6%)
  between operations  0.95 us (1%)
    ppermute x22, starting transfers between devices, xor_permute(): return lax.ppermute(value, axis, [(i, i ^ mask) for i in range(count)])  26.3 us
    ppermute x22, waiting for transfers between devices, xor_permute(): return lax.ppermute(value, axis, [(i, i ^ mask) for i in range(count)])  25.5 us
    dot_general x1, matrix products, plane_plan(): lax.dot_general(pre_grad, w_up, (((1,), (1,)), ((), ())), preferred_eleme...  19.4 us
    pallas_call x3, Pallas kernels, write_columns(): pl.pallas_call(body, in_specs=[pl.BlockSpec(memory_space=pltpu.SMEM), who...  6.66 us
    convert_element_type x2, other arithmetic, gelu_value_of(): return (pre_float * normal_cdf).astype(BF16)  2.45 us
    pallas_call x3, Pallas kernels, their_product(): pl.pallas_call(body, in_specs=[whole()] * (1 + len(pieces)), out_specs=wh...  1.92 us
  transfers between devices with their start and end apart: 22, of which 7 were waited for; matrix products, arithmetic and copies ran while one was open for 27% of the time, Pallas kernels for 10%

profile of v6, /device:TPU:0, one launch (start us, length us, event | category | flops | bytes accessed | tf_op | source)
XLA Modules:
  0.0 88.8 jit_solution(13592861746949259837)
XLA Ops:
  1.8 3.0 %collective-permute-start.3 = (bf16[128,384]{1,0:T(8,128)(2,1)S(1)}, bf16[128,384]{1,0:T(8,128)(2,1)S(1)}, u32[]{:S(2)}, u32[]{:S(2)}) collective-permute-start(bf16[128,384]{1,0:T(8,128)(2,1)S(1)} %get-tuple-element.35), channel_id=1, source_target_pairs={{0,4},{4,0},{8,12},{12,8},{16,20},{20,16},{24,28},{28,24},{1,5},{5... | collective-permute-start | bytes 294920 | tf_op jit(solution)/shard_map/ppermute | solution.py:29
  4.8 1.5 %collective-permute-start = (bf16[32,3072]{1,0:T(8,128)(2,1)}, bf16[32,3072]{1,0:T(8,128)(2,1)S(1)}, u32[]{:S(2)}, u32[]{:S(2)}) collective-permute-start(bf16[32,3072]{1,0:T(8,128)(2,1)} %param.5), channel_id=1, source_target_pairs={{0,2},{1,3},{2,0},{3,1},{4,6},{5,7},{6,4},{7,5},{8,10},{9,11},{10,... | collective-permute-start | bytes 589832 | tf_op jit(solution)/shard_map/ppermute | solution.py:29
  6.3 1.3 %fusion.11 = (bf16[128,1152]{1,0:T(8,128)(2,1)S(1)}, bf16[128,1152]{1,0:T(8,128)(2,1)S(1)}) fusion(pred[]{:T(512)S(6)} %eq.26, bf16[128,3072]{1,0:T(8,128)(2,1)} %param.4, pred[]{:T(512)S(6)} %eq.13), kind=kLoop, calls=%fused_computation.30 | loop fusion | flops 2064384 | bytes 1179650 | tf_op jit(solution)/shard_map/convert_element_type | solution.py:17
  8.3 3.7 %collective-permute-start.6 = (bf16[32,768]{1,0:T(8,128)(2,1)S(1)}, bf16[32,768]{1,0:T(8,128)(2,1)S(1)}, u32[]{:S(2)}, u32[]{:S(2)}) collective-permute-start(bf16[32,768]{1,0:T(8,128)(2,1)S(1)} %get-tuple-element.45), channel_id=1, source_target_pairs={{0,24},{4,28},{8,16},{12,20},{16,8},{20,12},{24,0},{28,4},{1,25},{... | collective-permute-start | bytes 147464 | tf_op jit(solution)/shard_map/ppermute | solution.py:29
  12.9 1.5 %collective-permute-done.6 = bf16[32,768]{1,0:T(8,128)(2,1)S(1)} collective-permute-done((bf16[32,768]{1,0:T(8,128)(2,1)S(1)}, bf16[32,768]{1,0:T(8,128)(2,1)S(1)}, u32[]{:S(2)}, u32[]{:S(2)}) %collective-permute-start.6) | collective-permute-done | bytes 49184 | tf_op jit(solution)/shard_map/ppermute | solution.py:29
  15.3 1.8 %collective-permute-done.5 = bf16[32,768]{1,0:T(8,128)(2,1)S(1)} collective-permute-done((bf16[32,768]{1,0:T(8,128)(2,1)S(1)}, bf16[32,768]{1,0:T(8,128)(2,1)S(1)}, u32[]{:S(2)}, u32[]{:S(2)}) %collective-permute-start.5) | collective-permute-done | bytes 49184 | tf_op jit(solution)/shard_map/ppermute | solution.py:29
  17.1 2.0 %collective-permute-start.8 = (bf16[256,384]{1,0:T(8,128)(2,1)S(1)}, bf16[256,384]{1,0:T(8,128)(2,1)S(1)}, u32[]{:S(2)}, u32[]{:S(2)}) collective-permute-start(bf16[256,384]{1,0:T(8,128)(2,1)S(1)} %pad_maximum_fusion.6.refs_0_), channel_id=1, source_target_pairs={{0,16},{4,20},{8,24},{12,28},{16,0},{20,4},{24,8},{28,12},{1,17},{... | collective-permute-start | bytes 589832 | tf_op jit(solution)/shard_map/ppermute | solution.py:29
  19.1 1.6 %collective-permute-start.7 = (bf16[4,32,768]{2,1,0:T(8,128)(2,1)S(1)}, bf16[4,32,768]{2,1,0:T(8,128)(2,1)S(1)}, u32[]{:S(2)}, u32[]{:S(2)}) collective-permute-start(bf16[4,32,768]{2,1,0:T(8,128)(2,1)S(1)} %get-tuple-element.43), channel_id=1, source_target_pairs={{0,4},{4,0},{8,12},{12,8},{16,20},{20,16},{24,28},{28,24},{1,5},{5... | collective-permute-start | bytes 589832 | tf_op jit(solution)/shard_map/ppermute | solution.py:29
  20.9 1.6 %collective-permute-done.9.refs_2_ = bf16[256,384]{1,0:T(8,128)(2,1)S(1)} collective-permute-done((bf16[256,384]{1,0:T(8,128)(2,1)S(1)}, bf16[256,384]{1,0:T(8,128)(2,1)S(1)}, u32[]{:S(2)}, u32[]{:S(2)}) %collective-permute-start.9) | collective-permute-done | bytes 196640 | tf_op jit(solution)/shard_map/ppermute | solution.py:29
  22.4 4.4 %collective-permute-done.8.refs_1_ = bf16[256,384]{1,0:T(8,128)(2,1)S(1)} collective-permute-done((bf16[256,384]{1,0:T(8,128)(2,1)S(1)}, bf16[256,384]{1,0:T(8,128)(2,1)S(1)}, u32[]{:S(2)}, u32[]{:S(2)}) %collective-permute-start.8) | collective-permute-done | bytes 196640 | tf_op jit(solution)/shard_map/ppermute | solution.py:29
  27.8 1.8 %collective-permute-start.16 = (bf16[256,1152]{1,0:T(8,128)(2,1)S(1)}, bf16[256,1152]{1,0:T(8,128)(2,1)S(1)}, u32[]{:S(2)}, u32[]{:S(2)}) collective-permute-start(bf16[256,1152]{1,0:T(8,128)(2,1)S(1)} %pad_maximum_fusion.1.refs_0_.refs_4_.refs_8_), channel_id=1, source_target_pairs={{0,16},{4,20},{8,24},{12,28},{16,0},{20,4},{24,8},{28,12},{1,17},{... | collective-permute-start | bytes 1769480 | tf_op jit(solution)/shard_map/ppermute | solution.py:29
  32.6 19.4 %fusion.7 = f32[128,3072]{1,0:T(8,128)} fusion(bf16[3072,3072]{1,0:T(8,128)(2,1)} %param.6, bf16[128,3072]{1,0:T(8,128)(2,1)} %bitcast.49, bf16[3072,3072]{1,0:T(8,128)(2,1)} %param.7, bf16[128,3072]{1,0:T(8,128)(2,1)} %param.4), kind=kOutput, calls=%fused_computation.26 | convolution fusion | flops 4836163584 | bytes 40894464 | tf_op jit(solution)/shard_map/dot_general | solution.py:229
  52.0 1.7 %shard_map.59 = (bf16[384,1024]{1,0:T(8,128)(2,1)S(1)}, bf16[384,1024]{1,0:T(8,128)(2,1)S(1)}) custom-call(s32[2]{0:T(128)S(1)} %pad_add_fusion.place_ref, bf16[2,4,32,768]{3,2,1,0:T(8,128)(2,1)S(1)} %pad_maximum_fusion.5.refs_0_, bf16[2,4,32,768]{3,2,1,0:T(8,128)(2,1)} %collective-permute-done.11.refs_1_, ...), custom_call_target="tpu_custom_call" | custom-call | bytes 6291456 | tf_op jit(solution)/shard_map/pallas_call | solution.py:91
  55.4 1.6 %collective-permute-start.19 = (bf16[384,384]{1,0:T(8,128)(2,1)S(1)}, bf16[384,384]{1,0:T(8,128)(2,1)S(1)}, u32[]{:S(2)}, u32[]{:S(2)}) collective-permute-start(bf16[384,384]{1,0:T(8,128)(2,1)S(1)} %shard_map.60), channel_id=1, source_target_pairs={{0,4},{4,0},{8,12},{12,8},{16,20},{20,16},{24,28},{28,24},{1,5},{5... | collective-permute-start | bytes 884744 | tf_op jit(solution)/shard_map/ppermute | solution.py:29
  57.0 1.4 %collective-permute-start.17 = (bf16[512,512]{1,0:T(8,128)(2,1)S(1)}, bf16[512,512]{1,0:T(8,128)(2,1)S(1)}, u32[]{:S(2)}, u32[]{:S(2)}) collective-permute-start(bf16[512,512]{1,0:T(8,128)(2,1)S(1)} %pad_maximum_fusion.3), channel_id=1, source_target_pairs={{0,8},{4,12},{8,0},{12,4},{16,24},{20,28},{24,16},{28,20},{1,9},{5... | collective-permute-start | bytes 1572872 | tf_op jit(solution)/shard_map/ppermute | solution.py:29
  58.3 6.8 %collective-permute-done.18.refs_7_.refs_3_ = bf16[256,640]{1,0:T(8,128)(2,1)S(1)} collective-permute-done((bf16[256,640]{1,0:T(8,128)(2,1)S(1)}, bf16[256,640]{1,0:T(8,128)(2,1)S(1)}, u32[]{:S(2)}, u32[]{:S(2)}) %collective-permute-start.18) | collective-permute-done | bytes 327712 | tf_op jit(solution)/shard_map/ppermute | solution.py:29
  65.9 1.6 %collective-permute-start.20 = (bf16[384,640]{1,0:T(8,128)(2,1)S(1)}, bf16[384,640]{1,0:T(8,128)(2,1)S(1)}, u32[]{:S(2)}, u32[]{:S(2)}) collective-permute-start(bf16[384,640]{1,0:T(8,128)(2,1)S(1)} %shard_map.63), channel_id=1, source_target_pairs={{0,4},{4,0},{8,12},{12,8},{16,20},{20,16},{24,28},{28,24},{1,5},{5... | collective-permute-start | bytes 1474568 | tf_op jit(solution)/shard_map/ppermute | solution.py:29
  67.6 2.1 %collective-permute-start.15 = (f32[32,3072]{1,0:T(8,128)S(1)}, f32[32,3072]{1,0:T(8,128)S(1)}, u32[]{:S(2)}, u32[]{:S(2)}) collective-permute-start(f32[32,3072]{1,0:T(8,128)S(1)} %select_bitcast_fusion.1), channel_id=1, source_target_pairs={{0,2},{1,3},{2,0},{3,1},{4,6},{5,7},{6,4},{7,5},{8,10},{9,11},{10,... | collective-permute-start | bytes 1179656 | tf_op jit(solution)/shard_map/ppermute | solution.py:29
  69.7 6.2 %collective-permute-done.17.refs_2_.refs_10_ = bf16[512,512]{1,0:T(8,128)(2,1)S(1)} collective-permute-done((bf16[512,512]{1,0:T(8,128)(2,1)S(1)}, bf16[512,512]{1,0:T(8,128)(2,1)S(1)}, u32[]{:S(2)}, u32[]{:S(2)}) %collective-permute-start.17) | collective-permute-done | bytes 524320 | tf_op jit(solution)/shard_map/ppermute | solution.py:29
  76.5 1.6 %collective-permute-start.21 = (bf16[384,512]{1,0:T(8,128)(2,1)S(1)}, bf16[384,512]{1,0:T(8,128)(2,1)S(1)}, u32[]{:S(2)}, u32[]{:S(2)}) collective-permute-start(bf16[384,512]{1,0:T(8,128)(2,1)S(1)} %shard_map.61), channel_id=1, source_target_pairs={{0,4},{4,0},{8,12},{12,8},{16,20},{20,16},{24,28},{28,24},{1,5},{5... | collective-permute-start | bytes 1179656 | tf_op jit(solution)/shard_map/ppermute | solution.py:29
  78.1 3.6 %shard_map.62.refs_0_ = f32[384,3072]{1,0:T(8,128)} custom-call(s32[2]{0:T(128)S(1)} %pad_add_fusion.place_ref, bf16[384,1024]{1,0:T(8,128)(2,1)S(1)} %get-tuple-element.32.grad_ref, bf16[256,384]{1,0:T(8,128)(2,1)S(1)} %pad_maximum_fusion.6.refs_0_, bf16[256,384]{1,0:T(8,128)(2,1)S(1)} %collective-permute-done.8.refs_1_, ...), custom_call_target="tpu_custom_call" | custom-call | flops 1509949440 | bytes 2949120 | tf_op jit(solution)/shard_map/pallas_call | solution.py:161
  81.7 1.6 %shard_map.64.refs_0_ = f32[384,3072]{1,0:T(8,128)} custom-call(s32[2]{0:T(128)S(1)} %pad_add_fusion.place_ref, bf16[384,1024]{1,0:T(8,128)(2,1)S(1)} %get-tuple-element.32.grad_ref, f32[384,3072]{1,0:T(8,128)} %shard_map.62.refs_0_, bf16[384,640]{1,0:T(8,128)(2,1)S(1)} %collective-permute-done.20.refs_1_), custom_call_target="tpu_custom_call", output_to_operand_aliasing={{}: (2, {})} | custom-call | bytes 983040 | tf_op jit(solution)/shard_map/pallas_call | solution.py:161
  84.0 3.3 %collective-permute-done.21.refs_1_ = bf16[384,512]{1,0:T(8,128)(2,1)S(1)} collective-permute-done((bf16[384,512]{1,0:T(8,128)(2,1)S(1)}, bf16[384,512]{1,0:T(8,128)(2,1)S(1)}, u32[]{:S(2)}, u32[]{:S(2)}) %collective-permute-start.21) | collective-permute-done | bytes 393248 | tf_op jit(solution)/shard_map/ppermute | solution.py:29
  87.3 1.5 %shard_map.65 = f32[384,3072]{1,0:T(8,128)} custom-call(s32[2]{0:T(128)S(1)} %pad_add_fusion.place_ref, bf16[384,1024]{1,0:T(8,128)(2,1)S(1)} %get-tuple-element.32.grad_ref, f32[384,3072]{1,0:T(8,128)} %shard_map.64.refs_0_, bf16[384,512]{1,0:T(8,128)(2,1)S(1)} %collective-permute-done.21.refs_1_), custom_call_target="tpu_custom_call", output_to_operand_aliasing={{}: (2, {})} | custom-call | bytes 786432 | tf_op jit(solution)/shard_map/pallas_call | solution.py:161
  (62 shorter events, 11.6 us)
Async XLA Ops:
  0.6 7.7 %copy-start.5 = (bf16[32,3072]{1,0:T(8,128)(2,1)S(1)}, bf16[32,3072]{1,0:T(8,128)(2,1)}, u32[]{:S(2)}) copy-start(bf16[32,3072]{1,0:T(8,128)(2,1)} %param.5) | copy-start | bytes 589828
  1.8 6.5 %collective-permute-start.3 = (bf16[128,384]{1,0:T(8,128)(2,1)S(1)}, bf16[128,384]{1,0:T(8,128)(2,1)S(1)}, u32[]{:S(2)}, u32[]{:S(2)}) collective-permute-start(bf16[128,384]{1,0:T(8,128)(2,1)S(1)} %get-tuple-element.35), channel_id=1, source_target_pairs={{0,4},{4,0},{8,12},{12,8},{16,20},{20,16},{24,28},{28,24},{1,5},{5... | collective-permute-start | bytes 294920 | tf_op jit(solution)/shard_map/ppermute | solution.py:29
  4.8 15.9 %collective-permute-start = (bf16[32,3072]{1,0:T(8,128)(2,1)}, bf16[32,3072]{1,0:T(8,128)(2,1)S(1)}, u32[]{:S(2)}, u32[]{:S(2)}) collective-permute-start(bf16[32,3072]{1,0:T(8,128)(2,1)} %param.5), channel_id=1, source_target_pairs={{0,2},{1,3},{2,0},{3,1},{4,6},{5,7},{6,4},{7,5},{8,10},{9,11},{10,... | collective-permute-start | bytes 589832 | tf_op jit(solution)/shard_map/ppermute | solution.py:29
  7.6 19.2 %copy-start.1 = (bf16[128,1152]{1,0:T(8,128)(2,1)}, bf16[128,1152]{1,0:T(8,128)(2,1)S(1)}, u32[]{:S(2)}) copy-start(bf16[128,1152]{1,0:T(8,128)(2,1)S(1)} %get-tuple-element.36) | copy-start | bytes 884740
  7.6 13.2 %collective-permute-start.2 = (bf16[128,1152]{1,0:T(8,128)(2,1)S(1)}, bf16[128,1152]{1,0:T(8,128)(2,1)S(1)}, u32[]{:S(2)}, u32[]{:S(2)}) collective-permute-start(bf16[128,1152]{1,0:T(8,128)(2,1)S(1)} %get-tuple-element.37), channel_id=1, source_target_pairs={{0,4},{4,0},{8,12},{12,8},{16,20},{20,16},{24,28},{28,24},{1,5},{5... | collective-permute-start | bytes 884744 | tf_op jit(solution)/shard_map/ppermute | solution.py:29
  8.3 6.0 %collective-permute-start.6 = (bf16[32,768]{1,0:T(8,128)(2,1)S(1)}, bf16[32,768]{1,0:T(8,128)(2,1)S(1)}, u32[]{:S(2)}, u32[]{:S(2)}) collective-permute-start(bf16[32,768]{1,0:T(8,128)(2,1)S(1)} %get-tuple-element.45), channel_id=1, source_target_pairs={{0,24},{4,28},{8,16},{12,20},{16,8},{20,12},{24,0},{28,4},{1,25},{... | collective-permute-start | bytes 147464 | tf_op jit(solution)/shard_map/ppermute | solution.py:29
  12.0 5.1 %collective-permute-start.5 = (bf16[32,768]{1,0:T(8,128)(2,1)S(1)}, bf16[32,768]{1,0:T(8,128)(2,1)S(1)}, u32[]{:S(2)}, u32[]{:S(2)}) collective-permute-start(bf16[32,768]{1,0:T(8,128)(2,1)S(1)} %get-tuple-element.46), channel_id=1, source_target_pairs={{0,16},{4,20},{8,24},{12,28},{16,0},{20,4},{24,8},{28,12},{1,17},{... | collective-permute-start | bytes 147464 | tf_op jit(solution)/shard_map/ppermute | solution.py:29
  12.0 7.0 %collective-permute-start.4 = (bf16[32,768]{1,0:T(8,128)(2,1)S(1)}, bf16[32,768]{1,0:T(8,128)(2,1)S(1)}, u32[]{:S(2)}, u32[]{:S(2)}) collective-permute-start(bf16[32,768]{1,0:T(8,128)(2,1)S(1)} %get-tuple-element.47), channel_id=1, source_target_pairs={{0,8},{4,12},{8,0},{12,4},{16,24},{20,28},{24,16},{28,20},{1,9},{5... | collective-permute-start | bytes 147464 | tf_op jit(solution)/shard_map/ppermute | solution.py:29
  14.4 8.1 %collective-permute-start.9 = (bf16[256,384]{1,0:T(8,128)(2,1)S(1)}, bf16[256,384]{1,0:T(8,128)(2,1)S(1)}, u32[]{:S(2)}, u32[]{:S(2)}) collective-permute-start(bf16[256,384]{1,0:T(8,128)(2,1)S(1)} %pad_maximum_fusion.6.refs_0_), channel_id=1, source_target_pairs={{0,8},{4,12},{8,0},{12,4},{16,24},{20,28},{24,16},{28,20},{1,9},{5... | collective-permute-start | bytes 589832 | tf_op jit(solution)/shard_map/ppermute | solution.py:29
  17.1 9.8 %collective-permute-start.8 = (bf16[256,384]{1,0:T(8,128)(2,1)S(1)}, bf16[256,384]{1,0:T(8,128)(2,1)S(1)}, u32[]{:S(2)}, u32[]{:S(2)}) collective-permute-start(bf16[256,384]{1,0:T(8,128)(2,1)S(1)} %pad_maximum_fusion.6.refs_0_), channel_id=1, source_target_pairs={{0,16},{4,20},{8,24},{12,28},{16,0},{20,4},{24,8},{28,12},{1,17},{... | collective-permute-start | bytes 589832 | tf_op jit(solution)/shard_map/ppermute | solution.py:29
  19.1 10.5 %collective-permute-start.7 = (bf16[4,32,768]{2,1,0:T(8,128)(2,1)S(1)}, bf16[4,32,768]{2,1,0:T(8,128)(2,1)S(1)}, u32[]{:S(2)}, u32[]{:S(2)}) collective-permute-start(bf16[4,32,768]{2,1,0:T(8,128)(2,1)S(1)} %get-tuple-element.43), channel_id=1, source_target_pairs={{0,4},{4,0},{8,12},{12,8},{16,20},{20,16},{24,28},{28,24},{1,5},{5... | collective-permute-start | bytes 589832 | tf_op jit(solution)/shard_map/ppermute | solution.py:29
  20.7 10.0 %collective-permute-start.1 = (bf16[2,32,3072]{2,1,0:T(8,128)(2,1)S(1)}, bf16[2,32,3072]{2,1,0:T(8,128)(2,1)S(1)}, u32[]{:S(2)}, u32[]{:S(2)}) collective-permute-start(bf16[2,32,3072]{2,1,0:T(8,128)(2,1)S(1)} %pad_maximum_fusion.4), channel_id=1, source_target_pairs={{0,1},{1,0},{2,3},{3,2},{4,5},{5,4},{6,7},{7,6},{8,9},{9,8},{10,11... | collective-permute-start | bytes 1179656 | tf_op jit(solution)/shard_map/ppermute | solution.py:29
  27.8 24.2 %collective-permute-start.10 = (bf16[256,1024]{1,0:T(8,128)(2,1)}, bf16[256,1024]{1,0:T(8,128)(2,1)S(1)}, u32[]{:S(2)}, u32[]{:S(2)}) collective-permute-start(bf16[256,1024]{1,0:T(8,128)(2,1)} %pad_maximum_fusion.2), channel_id=1, source_target_pairs={{0,8},{4,12},{8,0},{12,4},{16,24},{20,28},{24,16},{28,20},{1,9},{5... | collective-permute-start | bytes 1572872 | tf_op jit(solution)/shard_map/ppermute | solution.py:29
  27.8 26.7 %collective-permute-start.16 = (bf16[256,1152]{1,0:T(8,128)(2,1)S(1)}, bf16[256,1152]{1,0:T(8,128)(2,1)S(1)}, u32[]{:S(2)}, u32[]{:S(2)}) collective-permute-start(bf16[256,1152]{1,0:T(8,128)(2,1)S(1)} %pad_maximum_fusion.1.refs_0_.refs_4_.refs_8_), channel_id=1, source_target_pairs={{0,16},{4,20},{8,24},{12,28},{16,0},{20,4},{24,8},{28,12},{1,17},{... | collective-permute-start | bytes 1769480 | tf_op jit(solution)/shard_map/ppermute | solution.py:29
  29.6 22.3 %collective-permute-start.13 = (bf16[2,4,32,768]{3,2,1,0:T(8,128)(2,1)S(1)}, bf16[2,4,32,768]{3,2,1,0:T(8,128)(2,1)S(1)}, u32[]{:S(2)}, u32[]{:S(2)}) collective-permute-start(bf16[2,4,32,768]{3,2,1,0:T(8,128)(2,1)S(1)} %pad_maximum_fusion.5.refs_0_), channel_id=1, source_target_pairs={{0,3},{1,2},{2,1},{3,0},{4,7},{5,6},{6,5},{7,4},{8,11},{9,10},{10,... | collective-permute-start | bytes 1179656 | tf_op jit(solution)/shard_map/ppermute | solution.py:29
  29.7 22.3 %collective-permute-start.12 = (bf16[2,4,32,768]{3,2,1,0:T(8,128)(2,1)S(1)}, bf16[2,4,32,768]{3,2,1,0:T(8,128)(2,1)S(1)}, u32[]{:S(2)}, u32[]{:S(2)}) collective-permute-start(bf16[2,4,32,768]{3,2,1,0:T(8,128)(2,1)S(1)} %pad_maximum_fusion.5.refs_0_), channel_id=1, source_target_pairs={{0,2},{1,3},{2,0},{3,1},{4,6},{5,7},{6,4},{7,5},{8,10},{9,11},{10,... | collective-permute-start | bytes 1179656 | tf_op jit(solution)/shard_map/ppermute | solution.py:29
  30.7 21.3 %collective-permute-start.11 = (bf16[2,4,32,768]{3,2,1,0:T(8,128)(2,1)S(1)}, bf16[2,4,32,768]{3,2,1,0:T(8,128)(2,1)}, u32[]{:S(2)}, u32[]{:S(2)}) collective-permute-start(bf16[2,4,32,768]{3,2,1,0:T(8,128)(2,1)S(1)} %pad_maximum_fusion.5.refs_0_), channel_id=1, source_target_pairs={{0,1},{1,0},{2,3},{3,2},{4,5},{5,4},{6,7},{7,6},{8,9},{9,8},{10,11... | collective-permute-start | bytes 1179656 | tf_op jit(solution)/shard_map/ppermute | solution.py:29
  54.4 13.0 %collective-permute-start.14 = (f32[2,32,3072]{2,1,0:T(8,128)S(1)}, f32[2,32,3072]{2,1,0:T(8,128)S(1)}, u32[]{:S(2)}, u32[]{:S(2)}) collective-permute-start(f32[2,32,3072]{2,1,0:T(8,128)S(1)} %select_bitcast_fusion), channel_id=1, source_target_pairs={{0,1},{1,0},{2,3},{3,2},{4,5},{5,4},{6,7},{7,6},{8,9},{9,8},{10,11... | collective-permute-start | bytes 2359304 | tf_op jit(solution)/shard_map/ppermute | solution.py:29
  54.5 10.6 %collective-permute-start.18 = (bf16[256,640]{1,0:T(8,128)(2,1)S(1)}, bf16[256,640]{1,0:T(8,128)(2,1)S(1)}, u32[]{:S(2)}, u32[]{:S(2)}) collective-permute-start(bf16[256,640]{1,0:T(8,128)(2,1)S(1)} %slice.55), channel_id=1, source_target_pairs={{0,8},{4,12},{8,0},{12,4},{16,24},{20,28},{24,16},{28,20},{1,9},{5... | collective-permute-start | bytes 983048 | tf_op jit(solution)/shard_map/ppermute | solution.py:29
  55.4 22.7 %collective-permute-start.19 = (bf16[384,384]{1,0:T(8,128)(2,1)S(1)}, bf16[384,384]{1,0:T(8,128)(2,1)S(1)}, u32[]{:S(2)}, u32[]{:S(2)}) collective-permute-start(bf16[384,384]{1,0:T(8,128)(2,1)S(1)} %shard_map.60), channel_id=1, source_target_pairs={{0,4},{4,0},{8,12},{12,8},{16,20},{20,16},{24,28},{28,24},{1,5},{5... | collective-permute-start | bytes 884744 | tf_op jit(solution)/shard_map/ppermute | solution.py:29
  57.0 19.0 %collective-permute-start.17 = (bf16[512,512]{1,0:T(8,128)(2,1)S(1)}, bf16[512,512]{1,0:T(8,128)(2,1)S(1)}, u32[]{:S(2)}, u32[]{:S(2)}) collective-permute-start(bf16[512,512]{1,0:T(8,128)(2,1)S(1)} %pad_maximum_fusion.3), channel_id=1, source_target_pairs={{0,8},{4,12},{8,0},{12,4},{16,24},{20,28},{24,16},{28,20},{1,9},{5... | collective-permute-start | bytes 1572872 | tf_op jit(solution)/shard_map/ppermute | solution.py:29
  65.9 15.8 %collective-permute-start.20 = (bf16[384,640]{1,0:T(8,128)(2,1)S(1)}, bf16[384,640]{1,0:T(8,128)(2,1)S(1)}, u32[]{:S(2)}, u32[]{:S(2)}) collective-permute-start(bf16[384,640]{1,0:T(8,128)(2,1)S(1)} %shard_map.63), channel_id=1, source_target_pairs={{0,4},{4,0},{8,12},{12,8},{16,20},{20,16},{24,28},{28,24},{1,5},{5... | collective-permute-start | bytes 1474568 | tf_op jit(solution)/shard_map/ppermute | solution.py:29
  67.6 15.7 %collective-permute-start.15 = (f32[32,3072]{1,0:T(8,128)S(1)}, f32[32,3072]{1,0:T(8,128)S(1)}, u32[]{:S(2)}, u32[]{:S(2)}) collective-permute-start(f32[32,3072]{1,0:T(8,128)S(1)} %select_bitcast_fusion.1), channel_id=1, source_target_pairs={{0,2},{1,3},{2,0},{3,1},{4,6},{5,7},{6,4},{7,5},{8,10},{9,11},{10,... | collective-permute-start | bytes 1179656 | tf_op jit(solution)/shard_map/ppermute | solution.py:29
  76.5 10.8 %collective-permute-start.21 = (bf16[384,512]{1,0:T(8,128)(2,1)S(1)}, bf16[384,512]{1,0:T(8,128)(2,1)S(1)}, u32[]{:S(2)}, u32[]{:S(2)}) collective-permute-start(bf16[384,512]{1,0:T(8,128)(2,1)S(1)} %shard_map.61), channel_id=1, source_target_pairs={{0,4},{4,0},{8,12},{12,8},{16,20},{20,16},{24,28},{28,24},{1,5},{5... | collective-permute-start | bytes 1179656 | tf_op jit(solution)/shard_map/ppermute | solution.py:29
  (4 other events, 10.4 us)
